TPU v7x, 32 devices: a whole 2x2x4 slice. The times are simulated.
32 devices in a mesh: dp: 2 (over y), fsdp: 16 (over z, x, core).
Axes of the slice: x: 2, y: 2, z: 4, core: 2. Of those that a mesh axis runs over, the one named last changes fastest.
Arguments:
- inputs: bfloat16 [2, 2048, 2048], P('dp', 'fsdp'), may hold values from -6 to 6
- weight: bfloat16 [2048, 6144], P('fsdp', 'dp'), may hold values from -0.125 to 0.125
- gain: float32 [2048], replicated, may hold values from 0.5 to 1.5
- shift: float32 [2048], replicated, may hold values from -1.5 to 1.5
- forget_vec: float32 [2048], replicated, may hold values from -0.8 to 0.8
- reset_vec: float32 [2048], replicated, may hold values from -0.8 to 0.8
- forget_bias: float32 [2048], replicated, may hold values from 3 to 10
- reset_bias: float32 [2048], replicated, may hold values from 0 to 3
- initial: float32 [2, 2048], P('dp'), may hold values from -5 to 5
- resets: int32 [2, 2048], P('dp', 'fsdp'), may hold values from 0 to 1, as said below
- grad_out: bfloat16 [2, 2048, 2048], P('dp', 'fsdp'), may hold values from -6 to 6
Outputs:
- hidden: bfloat16 [2, 2048, 2048], P('dp', 'fsdp')
- grad_inputs: bfloat16 [2, 2048, 2048], P('dp', 'fsdp')
- final_state: float32 [2, 2048], P('dp', 'fsdp')
- grad_weight: float32 [2048, 6144], P('fsdp', 'dp')
- grad_forget_vec: float32 [2048], replicated
- grad_reset_vec: float32 [2048], replicated
- grad_forget_bias: float32 [2048], replicated
- grad_reset_bias: float32 [2048], replicated
- grad_gain: float32 [2048], replicated
- grad_shift: float32 [2048], replicated
Inputs may be any that keep to these rules, and one draw needn't show every extreme that they name: `resets`: A 1 marks the first token of a sentence; position 0 of every row is 0. The first 1 of a row lies at position 641 to 768, and exactly at 768 in some row. The last 1 of a row lies at position 1857 or later. After a row's first 1, two consecutive sentence starts lie 128 // 2 to 191 tokens apart.
All inputs are finite; a program needn't handle non-finite values.
Results may differ from a plain program's by a relative error of at most 0.011.
Values may be sent and summed in bfloat16 or wider, within the bound.
No kernel may reach another device: no remote copies, remote signals or barrier semaphores. Data moves between devices by JAX's collectives and lax.ppermute only.
A program may use at most 192 MiB of HBM per device.

v0:
```python
import functools
import math

import jax
import jax.numpy as jnp
from jax import lax
from jax.experimental import pallas as pl
from jax.experimental.pallas import tpu as pltpu
from jax.sharding import PartitionSpec as P

SENT = 128
LEAD = 768
REACH = 192
EPSILON = 1e-05
LANES = 128
BLOCK = 128
SPACED = 136
EARLY = REACH - BLOCK
COVERED = EARLY + 2 * BLOCK
STATS = 16
UNROLL = 8
f32 = jnp.float32
bf16 = jnp.bfloat16


def spaced(token):
    return token + (SPACED - BLOCK) * (token // BLOCK)


def tiles_of(ref, count):
    return [ref[:, LANES * i : LANES * (i + 1)] for i in range(count)]


def call(kernel, out_shape, operands, scalars=(), waits=(), scratch=(), mebibytes=14, name=None):
    in_vmem, in_smem = pl.BlockSpec(memory_space=pltpu.VMEM), pl.BlockSpec(memory_space=pltpu.SMEM)
    before = len(scalars) + len(operands)

    def body(*refs):
        kernel(*refs[:before], *refs[before + len(waits) :])

    return pl.pallas_call(
        body,
        in_specs=[in_smem] * len(scalars) + [in_vmem] * len(operands) + [pl.BlockSpec(memory_space=pl.ANY)] * len(waits),
        out_specs=[in_vmem] * len(out_shape),
        out_shape=[jax.ShapeDtypeStruct(*shape) for shape in out_shape],
        scratch_shapes=[pltpu.VMEM(*shape) for shape in scratch],
        compiler_params=pltpu.CompilerParams(vmem_limit_bytes=mebibytes << 20),
        name=name,
    )(*scalars, *operands, *waits)


def fence(value, waits):
    return pl.pallas_call(
        lambda *refs: None,
        in_specs=[pl.BlockSpec(memory_space=pl.ANY)] * (1 + len(waits)),
        out_specs=pl.BlockSpec(memory_space=pl.ANY),
        out_shape=jax.ShapeDtypeStruct(value.shape, value.dtype),
        input_output_aliases={0: 0},
        name="fence",
    )(value, *waits)


def deal_kernel(in_ref, out_ref, *, chunks):
    group = out_ref.shape[0]
    for q in range(group):
        for c in range(chunks):
            lane = (c * group + q) * LANES
            out_ref[q, :, LANES * c : LANES * (c + 1)] = in_ref[:, lane : lane + LANES]


def deal(value, group, waits=()):
    n, features = value.shape
    kernel = functools.partial(deal_kernel, chunks=features // group // LANES)
    return call(kernel, [((group, n, features // group), value.dtype)], (value,), waits=waits, name="deal")[0]


def collect_kernel(*refs):
    *in_refs, out_ref = refs
    row = 0
    for ref in in_refs:
        group, n, width = ref.shape
        for q in range(group):
            for c in range(width // LANES):
                lane = (c * group + q) * LANES
                value = ref[q, :, LANES * c : LANES * (c + 1)]
                out_ref[row : row + n, lane : lane + LANES] = value.astype(out_ref.dtype)
        row += n


def collect(pieces, dtype, waits=()):
    group, _, width = pieces[0].shape
    shape = (sum(value.shape[1] for value in pieces), group * width)
    return call(collect_kernel, [(shape, dtype)], pieces, waits=waits, name="collect")[0]


def add_kernel(a_ref, b_ref, out_ref):
    out_ref[...] = (a_ref[...].astype(f32) + b_ref[...].astype(f32)).astype(out_ref.dtype)


def added(a, b, waits=()):
    return call(add_kernel, [(a.shape, a.dtype)], (a, b), waits=waits, name="added")[0]


def blocks_of(refs):
    return [ref.at[i] for ref in refs for i in range(ref.shape[0])]


def halve_kernel(*refs):
    *in_refs, first_stays, first_goes, second_stays, second_goes = refs
    n = len(in_refs) // 4
    parts = [blocks_of(in_refs[n * i : n * (i + 1)]) for i in range(4)]
    outs = (blocks_of((first_stays, first_goes)), blocks_of((second_stays, second_goes)))
    for kept, got, out in zip(parts[:2], parts[2:], outs):
        for kept_ref, got_ref, out_ref in zip(kept, got, out):
            out_ref[...] = (kept_ref[...].astype(f32) + got_ref[...].astype(f32)).astype(bf16)


def halve(kept, got, waits=()):
    n = sum(value.shape[0] for value in kept) // 4
    out = call(halve_kernel, [((n, *kept[0].shape[1:]), bf16)] * 4, (*kept, *got), waits=waits, name="halve")
    return out[0::2], out[1::2]


def merge_kernel(own_ref, got_ref, away_ref, out_ref):
    value = own_ref[...].astype(f32) + got_ref[...].astype(f32) + away_ref[...].astype(f32)
    out_ref[...] = value.astype(bf16)


def merge(own, got, away, waits=()):
    return call(merge_kernel, [(own.shape, bf16)], (own, got, away), waits=waits, name="merge")[0]


def finish_kernel(where_ref, *refs):
    *in_refs, out_ref = refs
    width = in_refs[0].shape[-1]
    for part in range(2):
        kept_ref, got_ref = in_refs[part], in_refs[2 + part]
        lane = pl.ds(pl.multiple_of((where_ref[0] ^ part) * width, LANES), width)
        out_ref[:, :, lane] = (kept_ref[0].astype(f32) + got_ref[0].astype(f32)).astype(bf16)


def finish(where, kept, got, waits=()):
    _, rows, block, width = kept[0].shape
    return call(finish_kernel, [((rows, block, 2 * width), bf16)], (*kept, *got), (where,), waits, name="finish")[0]


def stats_kernel(where_ref, x_ref, keep_ref, first_ref, second_ref):
    total, block, features = x_ref.shape
    half_width = features // 2

    def row(column):
        return jnp.transpose(jnp.broadcast_to(column, (block, LANES)))[0:1, :]

    for r in range(total):
        for part, ref in enumerate((first_ref, second_ref)):
            lane = pl.multiple_of((where_ref[0] ^ part) * half_width, LANES)
            ref[0, r, :block, :] = x_ref[r, :, pl.ds(lane, half_width)]
        x = x_ref[r].astype(f32)
        mean = jnp.sum(x, axis=-1, keepdims=True) * (1.0 / features)
        centred = x - mean
        inv = lax.rsqrt(jnp.sum(centred * centred, axis=-1, keepdims=True) * (1.0 / features) + EPSILON)
        rows = [keep_ref[r]]
        for value in (row(mean), row(inv)):
            for _ in range(3):
                upper = value.astype(bf16).astype(f32)
                rows.append(upper)
                value = value - upper
        rows = jnp.concatenate(rows + [jnp.zeros_like(rows[0])] * (STATS - len(rows)), axis=0)
        if block < LANES:
            rows = jnp.concatenate([rows, jnp.zeros((STATS, LANES - block), f32)], axis=1)
        first_ref[0, r, block:, :LANES] = rows.astype(bf16)
        first_ref[0, r, block:, LANES:] = jnp.zeros((STATS, half_width - LANES), bf16)


def stats(where, inputs, keep, waits):
    rows, block, features = inputs.shape
    out_shape = [((1, rows, block + STATS, features // 2), bf16), ((1, rows, block, features // 2), bf16)]
    return call(stats_kernel, out_shape, (inputs, keep), (where,), waits, name="stats")


def norm_kernel(where_ref, gain_ref, shift_ref, *refs, orders):
    block_refs, (normed_ref, stats_ref, keep_ref, *own_refs) = refs[:4], refs[4:]
    half_width = block_refs[0].shape[-1]
    total, block = block_refs[1].shape[1:3]
    per_block = BLOCK // block

    def device(r, first_ref, d, second_ref, e, bits):
        q = where_ref[3] ^ bits
        at = pl.ds(pl.multiple_of(q * block, block), block)
        spaced_at = pl.ds(pl.multiple_of(q // per_block * SPACED + q % per_block * block, 8), block)
        rows = first_ref[d, r, block:, :block].astype(f32)

        def column(*of):
            row = functools.reduce(jnp.add, [rows[k : k + 1, :] for k in of])
            return jnp.transpose(jnp.broadcast_to(row, (LANES, block)))

        keep_ref[r, spaced_at, :] = column(0)
        mean, inv = column(1, 2, 3), column(4, 5, 6)
        stats_ref[r, 0, at, :] = mean
        stats_ref[r, 1, at, :] = inv
        for part, x_ref, at_d in ((0, first_ref, d), (1, second_ref, e)):
            for j in range(half_width // LANES):
                x = x_ref[at_d, r, :block, LANES * j : LANES * (j + 1)].astype(f32)
                out = slice(part * half_width + j * LANES, part * half_width + (j + 1) * LANES)
                normed_ref[r, at, out] = ((x - mean) * inv * gain_ref[:, out] + shift_ref[:, out]).astype(bf16)
            for ref in own_refs:
                lane = pl.ds(pl.multiple_of(where_ref[3] * LANES, LANES), LANES)
                ref[r, where_ref[0] ^ part, at, :] = x_ref[at_d, r, :block, lane]

    for r in range(total):
        for odd in range(2):
            for d, bits in enumerate(orders[0]):
                e = orders[1].index(bits)
                device(r, block_refs[2 * odd], d, block_refs[2 * odd + 1], e, bits | odd)


def norm(where, blocks, gain, shift, orders, aligned):
    count, rows, block, half_width = blocks[1].shape
    tokens = 2 * count * block
    out_shape = [
        ((rows, tokens, 2 * half_width), bf16),
        ((rows, 2, tokens, LANES), f32),
        ((rows, tokens // BLOCK * SPACED, LANES), f32),
    ]
    if aligned:
        out_shape.append(((rows, 2, tokens, LANES), bf16))
    return call(functools.partial(norm_kernel, orders=orders), out_shape, (gain, shift, *blocks), (where,), name="norm")


def weight_into(w_ref, parts):
    if len(parts) == 1:
        w_ref[...] = parts[0][...]
        return
    row = 0
    for own, other in zip(parts[0::2], parts[1::2]):
        rows, columns = own.shape
        w_ref[row : row + rows, :columns] = own[...]
        w_ref[row : row + rows, columns:] = other[...]
        row += rows


def slot_of(where_ref, s, slots):
    return lax.rem(where_ref[4] + s, slots)


def project_kernel(where_ref, normed_ref, rows_ref, *refs):
    *parts, sum_ref, vectors_ref, w_ref = refs
    weight_into(w_ref, parts)
    depth = w_ref.shape[0]
    total, slots = sum_ref.shape[:2]
    step = 2 * BLOCK
    vectors_ref[...] = jnp.dot(rows_ref[:, :depth], w_ref[...], preferred_element_type=f32)
    for r in range(total):

        @pl.loop(0, normed_ref.shape[1] // step)
        def _(j):
            at = pl.ds(pl.multiple_of(j * step, step), step)
            p = jnp.dot(normed_ref[r, at, :depth], w_ref[...], preferred_element_type=f32)
            for s in range(slots):
                sum_ref[r, s, at, :] = p[:, LANES * s : LANES * (s + 1)]


def project(where, normed, vector_rows, parts, depth, slots):
    rows, tokens, _ = normed.shape
    out_shape = [
        ((rows, slots, tokens, LANES), f32), ((vector_rows.shape[0], slots * LANES), f32), ((depth, slots * LANES), bf16),
    ]
    return call(project_kernel, out_shape, (normed, vector_rows, *parts), (where,), name="project")


def blocks_kernel(where_ref, normed_ref, rows_ref, sum_ref, some_ref, bias_ref, keep_ref, hfv_ref, init_ref, *refs):
    *parts, p_ref, seg_ref, lead_ref, end_ref, lead_end_ref, vectors_ref, w_ref = refs
    weight_into(w_ref, parts)
    depth = w_ref.shape[0]
    total, slots = p_ref.shape[:2]
    tiles = slots // 3
    step = 2 * BLOCK
    features = normed_ref.shape[2]
    by_column = some_ref[...] + jnp.dot(rows_ref[:, features - depth :], w_ref[...], preferred_element_type=f32)
    for s in range(slots):
        slot = slot_of(where_ref, s, slots)
        lanes = slice(LANES * s, LANES * (s + 1))
        vectors_ref[slot, 0:1, :] = jnp.sum(by_column[0:3, lanes], axis=0, keepdims=True)
        vectors_ref[slot, 1:2, :] = jnp.sum(by_column[3:6, lanes], axis=0, keepdims=True) + bias_ref[slot]
    for r in range(total):

        @pl.loop(0, normed_ref.shape[1] // step)
        def _(j):
            at = pl.ds(pl.multiple_of(j * step, step), step)
            p = jnp.dot(normed_ref[r, at, features - depth :], w_ref[...], preferred_element_type=f32)
            for s in range(slots):
                slot = slot_of(where_ref, s, slots)
                scale = jnp.where(slot < tiles, 1.0, 0.5)
                value = scale * (p[:, LANES * s : LANES * (s + 1)] + sum_ref[r, s, at, :] + bias_ref[slot])
                for k in range(2):
                    to = pl.ds(pl.multiple_of((2 * j + k) * SPACED, 8), BLOCK)
                    p_ref[r, slot, to, :] = value[BLOCK * k : BLOCK * (k + 1)]

        row_blocks(
            p_ref.at[r], keep_ref.at[r], hfv_ref, init_ref.at[r], seg_ref.at[r], lead_ref.at[r], end_ref.at[r],
            lead_end_ref.at[r],
        )


def blocks_forward(where, normed, vector_rows, some, some_vectors, bias, keep, hfv, init, parts, depth):
    rows, tokens, _ = normed.shape
    slots = bias.shape[0]
    tiles = slots // 3
    state = ((rows, 1, tiles * LANES), f32)
    length = tokens // BLOCK * SPACED
    out_shape = [
        ((rows, slots, length, LANES), f32), ((rows, tiles, length, LANES), f32),
        ((rows, tiles, spaced(COVERED), LANES), f32), state, state, ((slots, 2, LANES), f32), ((depth, slots * LANES), bf16),
    ]
    return call(
        blocks_kernel, out_shape, (normed, vector_rows, some, some_vectors, bias, keep, hfv, init, *parts), (where,),
        name="blocks_forward",
    )


def chain_step(p_ref, kb_ref, prev_ref, hfv, carried, row, next_row):
    tiles = len(hfv)
    keep = kb_ref[next_row, :]
    out = []
    for i, (y, prev) in enumerate(carried):
        tau = jnp.tanh(y)
        half = 0.5 * p_ref[i, row, :]
        mid, gap = 0.5 * prev + half, 0.5 * prev - half
        prev_ref[i, row, :] = prev
        reach = hfv[i] * keep
        out.append(
            ((p_ref[tiles + i, next_row, :] + reach * mid) + (reach * gap) * tau, (keep * mid) + (keep * gap) * tau)
        )
    return out


def begin(p_ref, hfv, previous, row):
    return [(p_ref[len(hfv) + i, row, :] + hfv[i] * prev, prev) for i, prev in enumerate(previous)]


def rows_of(token):
    return pl.ds(spaced(token), 1)


def run_chain(p_ref, kb_ref, prev_ref, hfv, carried, first, count):
    def body(j, now):
        for u in range(UNROLL):
            token = first + j * UNROLL + u
            now = chain_step(p_ref, kb_ref, prev_ref, hfv, now, rows_of(token), rows_of(token + 1))
        return now

    return lax.fori_loop(0, count // UNROLL, body, carried)


def row_blocks(p_ref, kb_ref, hfv_ref, init_ref, seg_ref, lead_ref, end_ref, lead_end_ref):
    tiles = seg_ref.shape[0]
    blocks = p_ref.shape[1] // SPACED
    hfv = tiles_of(hfv_ref, tiles)

    def seg_step(cells, step, store):
        row = pl.ds(step, blocks, stride=SPACED)
        keep = kb_ref[row, :]
        out = []
        for i, cell in enumerate(cells):
            prev = keep * cell
            tau = jnp.tanh(p_ref[tiles + i, row, :] + (hfv[i] * keep) * cell)
            half = 0.5 * p_ref[i, row, :]
            if store:
                seg_ref[i, row, :] = prev
            out.append((0.5 * prev + half) + (0.5 * prev - half) * tau)
        return out

    def run(cells, lead, first, token, count, store):
        def body(j, carried):
            cells, lead = carried
            for u in range(UNROLL):
                at = j * UNROLL + u
                cells = seg_step(cells, first + at, store)
                lead = chain_step(p_ref, kb_ref, lead_ref, hfv, lead, rows_of(token + at), rows_of(token + at + 1))
            return cells, lead

        return lax.fori_loop(0, count // UNROLL, body, (cells, lead))

    def moved(cells):
        return [jnp.concatenate([jnp.zeros((1, LANES), f32), cell[:-1]], axis=0) for cell in cells]

    cells = [jnp.zeros((blocks, LANES), f32) for _ in range(tiles)]
    lead = begin(p_ref, hfv, [kb_ref[0:1, :] * v for v in tiles_of(init_ref, tiles)], pl.ds(0, 1))
    cells, lead = run(cells, lead, BLOCK - EARLY, 0, EARLY, False)
    cells, lead = run(moved(cells), lead, 0, EARLY, BLOCK, False)
    cells, lead = run(moved(cells), lead, 0, EARLY + BLOCK, BLOCK, True)
    for i in range(tiles):
        end_ref[:, LANES * i : LANES * (i + 1)] = cells[i][-1:]
        lead_end_ref[:, LANES * i : LANES * (i + 1)] = lead[i][1]


def lead_kernel(p_ref, keep_ref, hfv_ref, start_ref, early_ref, lead_ref):
    rows, tiles = lead_ref.shape[:2]
    hfv = tiles_of(hfv_ref, tiles)
    lead_ref[:, :, : spaced(COVERED), :] = early_ref[...]
    for r in range(rows):
        carried = begin(p_ref.at[r], hfv, tiles_of(start_ref.at[r], tiles), rows_of(COVERED))
        run_chain(p_ref.at[r], keep_ref.at[r], lead_ref.at[r], hfv, carried, COVERED, LEAD - COVERED)


def lead_forward(p, keep, hfv, start, early):
    rows, tiles = early.shape[:2]
    out_shape = [((rows, tiles, spaced(LEAD), LANES), f32)]
    return call(lead_kernel, out_shape, (p, keep, hfv, start, early), name="lead_forward")[0]


def token_terms(prev, c, yf, yr, x, g, keep, hfv, hrv):
    tau_f = jnp.tanh(yf + hfv * prev)
    tau_r = jnp.tanh(yr + hrv * prev)
    f, omf, gate, omg = 0.5 + 0.5 * tau_f, 0.5 - 0.5 * tau_f, 0.5 + 0.5 * tau_r, 0.5 - 0.5 * tau_r
    cell = f * prev + omf * c
    gg = g * gate
    dr = gg * omg * (cell - x)
    e = (prev - c) * f * omf
    slope = f + e * (2.0 * hfv)
    return dict(
        cell=cell, hidden=gate * cell + omg * x, high=g * omg, gg=gg, dr=dr, e=e, omf=omf,
        a=keep * slope, b=keep * (slope * gg + dr * (2.0 * hrv)),
    )


def block_terms(p_ref, keep_ref, prev_ref, x_ref, g_ref, hfv, hrv, r, k, i):
    tiles = len(hfv)
    at = pl.ds(pl.multiple_of(k * SPACED, 8), BLOCK)
    devices = BLOCK // g_ref.shape[2]
    lanes = slice(LANES * i, LANES * (i + 1))
    g = jnp.concatenate([g_ref[k * devices + n, r, :, lanes].astype(f32) for n in range(devices)], axis=0)
    x = x_ref[r, i, pl.ds(pl.multiple_of(k * BLOCK, BLOCK), BLOCK), :].astype(f32)
    c, yf, yr = (p_ref[r, m * tiles + i, at, :] for m in range(3))
    return token_terms(prev_ref[i, at, :], c, yf, yr, x, g, keep_ref[r, at, :], hfv[i], hrv[i])


def run_back(a_ref, b_ref, d_ref, carried, count):
    def body(j, carried):
        base = pl.multiple_of(count - UNROLL * (j + 1), UNROLL)
        for u in reversed(range(UNROLL)):
            row = pl.ds(base + u, 1)
            now = []
            for i, d in enumerate(carried):
                if d_ref is not None:
                    d_ref[i, row, :] = d
                now.append(a_ref[i, row, :] * d + b_ref[i, row, :])
            carried = now
        return carried

    return lax.fori_loop(0, count // UNROLL, body, carried)


def entry_kernel(
    p_ref, keep_ref, seg_ref, x_ref, g_ref, hfv_ref, hrv_ref, start_ref, first_ref, back_ref, prev_ref, a_ref, b_ref
):
    rows, slots = p_ref.shape[:2]
    tiles = slots // 3
    hfv, hrv = tiles_of(hfv_ref, tiles), tiles_of(hrv_ref, tiles)
    blocks = -(-REACH // BLOCK)
    for r in range(rows):
        prev_ref[...] = seg_ref[r, :, : blocks * SPACED, :]
        start = [keep_ref[r, 0:1, :] * v for v in tiles_of(start_ref.at[r], tiles)]
        run_chain(p_ref.at[r], keep_ref.at[r], prev_ref, hfv, begin(p_ref.at[r], hfv, start, pl.ds(0, 1)), 0, REACH)
        first_ref[r] = prev_ref[:, : spaced(REACH), :]
        for k in range(blocks):
            for i in range(tiles):
                t = block_terms(p_ref, keep_ref, prev_ref, x_ref, g_ref, hfv, hrv, r, k, i)
                a_ref[i, BLOCK * k : BLOCK * (k + 1), :] = t["a"]
                b_ref[i, BLOCK * k : BLOCK * (k + 1), :] = t["b"]
        carried = run_back(a_ref, b_ref, None, [jnp.zeros((1, LANES), f32)] * tiles, blocks * BLOCK)
        for i in range(tiles):
            back_ref[r, :, LANES * i : LANES * (i + 1)] = carried[i]


def entry(p, keep, seg, x_own, g_own, hfv, hrv, start, waits):
    rows, slots, _, _ = p.shape
    tiles = slots // 3
    blocks = -(-REACH // BLOCK)
    length, count = blocks * SPACED, blocks * BLOCK
    return call(
        entry_kernel,
        [((rows, tiles, spaced(REACH), LANES), f32), ((rows, 1, tiles * LANES), f32)],
        (p, keep, seg, x_own, g_own, hfv, hrv, start),
        waits=waits,
        scratch=[((tiles, length, LANES), f32)] + [((tiles, count, LANES), f32)] * 2,
        name="entry",
    )


def backward_kernel(
    where_ref, p_ref, keep_ref, seg_ref, lead_ref, first_ref, x_ref, g_ref, hfv_ref, hrv_ref, carry_ref, vectors_ref,
    gp_ref, hidden_ref, high_ref, sums_ref, final_ref, means_ref,
    prev_ref, a_ref, b_ref, gg_ref, e_ref, omf_ref, dr_ref, d_ref,
):
    rows, slots = p_ref.shape[:2]
    tiles = slots // 3
    blocks = p_ref.shape[2] // SPACED
    hfv, hrv = tiles_of(hfv_ref, tiles), tiles_of(hrv_ref, tiles)
    devices, block = BLOCK // g_ref.shape[2], g_ref.shape[2]
    sums_ref[...] = jnp.zeros_like(sums_ref)
    for r in range(rows):
        prev_ref[...] = seg_ref[r]

        @pl.when(where_ref[0] == 0)
        def _():
            prev_ref[:, : spaced(LEAD), :] = lead_ref[r]

        @pl.when(where_ref[0] != 0)
        def _():
            prev_ref[:, : spaced(REACH), :] = first_ref[r]

        @pl.loop(0, blocks)
        def _(k):
            out = pl.ds(pl.multiple_of(k * BLOCK, BLOCK), BLOCK)
            for i in range(tiles):
                t = block_terms(p_ref, keep_ref, prev_ref, x_ref, g_ref, hfv, hrv, r, k, i)
                lanes = slice(LANES * i, LANES * (i + 1))
                for n in range(devices):
                    hidden_ref[k * devices + n, r, :, lanes] = t["hidden"][n * block : (n + 1) * block].astype(bf16)
                high_ref[r, i, out, :] = t["high"].astype(bf16)
                for ref, name in zip((a_ref, b_ref, gg_ref, e_ref, omf_ref, dr_ref), "a b gg e omf dr".split()):
                    ref[i, out, :] = t[name]
                final_ref[r, :, lanes] = t["cell"][-1:]

        run_back(a_ref, b_ref, d_ref, tiles_of(carry_ref.at[r], tiles), blocks * BLOCK)

        @pl.loop(0, blocks)
        def _(k):
            at = pl.ds(pl.multiple_of(k * SPACED, 8), BLOCK)
            out = pl.ds(pl.multiple_of(k * BLOCK, BLOCK), BLOCK)
            first, second = jnp.zeros((BLOCK, LANES), f32), jnp.zeros((BLOCK, LANES), f32)
            for i in range(tiles):
                prev = prev_ref[i, at, :]
                u = d_ref[i, out, :] + gg_ref[i, out, :]
                df, dr = u * e_ref[i, out, :], dr_ref[i, out, :]
                dc = u * omf_ref[i, out, :]
                for m, value in enumerate((dc, df, dr)):
                    slot = m * tiles + i
                    lane = lax.rem(slot + slots - where_ref[4], slots) * LANES
                    gp_ref[r, out, pl.ds(pl.multiple_of(lane, LANES), LANES)] = value.astype(bf16)
                    first += value * vectors_ref[slot, 0:1, :]
                    second += value * ((1.0 if m == 0 else 2.0) * p_ref[r, slot, at, :] - vectors_ref[slot, 1:2, :])
                lanes = slice(LANES * i, LANES * (i + 1))
                for m, value in enumerate((df * prev, dr * prev, df, dr)):
                    sums_ref[m : m + 1, lanes] += jnp.sum(value, axis=0, keepdims=True)
                for m, value in enumerate((dc, df, dr)):
                    lane = lax.rem(m * tiles + i + slots - where_ref[4], slots) * LANES
                    at_lane = pl.ds(pl.multiple_of(lane, LANES), LANES)
                    sums_ref[7:8, at_lane] += jnp.sum(value, axis=0, keepdims=True)
            means_ref[r, 0, out, :] = first
            means_ref[r, 1, out, :] = second


def backward(where, p, keep, seg, lead, first, x_own, g_own, hfv, hrv, carry, vectors):
    rows, slots, length, _ = p.shape
    tiles = slots // 3
    tokens = length // SPACED * BLOCK
    width = tiles * LANES
    return call(
        backward_kernel,
        [
            ((rows, tokens, 3 * width), bf16),
            (g_own.shape, bf16),
            ((rows, tiles, tokens, LANES), bf16),
            ((8, 3 * width), f32),
            ((rows, 1, width), f32),
            ((rows, 2, tokens, LANES), f32),
        ],
        (p, keep, seg, lead, first, x_own, g_own, hfv, hrv, carry, vectors),
        (where,),
        scratch=[((tiles, length, LANES), f32)] + [((tiles, tokens, LANES), f32)] * 7,
        name="backward",
    )


def weight_back_kernel(normed_ref, gp_ref, sums_ref, *refs, part, group, cuts):
    count = sum(len(rows) for rows in cuts)
    w_refs, (by_feature_ref, *out_refs) = refs[: len(refs) - count - 1], refs[len(refs) - count - 1 :]
    total, _, features = normed_ref.shape
    row_block = features // 2 // group
    columns = out_refs[0].shape[2]
    span = 2 * LANES
    devices = span // row_block
    lane_tiles = gp_ref.shape[2] // LANES
    for k in range(group // devices):
        lane = slice(part * (features // 2) + k * span, part * (features // 2) + (k + 1) * span)
        p = sum(
            lax.dot_general(normed_ref[r, :, lane], gp_ref[r], (((0,), (0,)), ((), ())), preferred_element_type=f32)
            for r in range(total)
        )
        first = w_refs[0].shape[0]
        w = [w_refs[0][lane.start : min(lane.stop, first), :]] if lane.start < first else []
        if lane.stop > first:
            w.append(w_refs[1][max(lane.start - first, 0) : lane.stop - first, :])
        w = jnp.concatenate(w).astype(f32)
        for m, value in enumerate((p * w, w * sums_ref[7:8, :])):
            value = functools.reduce(jnp.add, [value[:, LANES * j : LANES * (j + 1)] for j in range(lane_tiles)])
            by_feature_ref[m : m + 1, k * span : (k + 1) * span] = jnp.sum(jnp.transpose(value), axis=0, keepdims=True)
        p = p.astype(bf16)
        outs = iter(out_refs)
        for split, rows in enumerate(cuts):
            start = 0
            for step in rows:
                out_ref = next(outs)
                for n in range(devices):
                    row = n * row_block + start
                    out_ref[k * devices + n] = p[row : row + step, split * columns : (split + 1) * columns]
                start += step


def weight_back(normed, gp, sums, weights, part, group, cuts, waits):
    features = normed.shape[2]
    columns = gp.shape[2] // len(cuts)
    kernel = functools.partial(weight_back_kernel, part=part, group=group, cuts=cuts)
    out_shape = [((2, features // 2), f32)] + [((group, step, columns), bf16) for rows in cuts for step in rows]
    return call(kernel, out_shape, (normed, gp, sums, *weights), waits=waits, name="weight_back")


def norm_back_kernel(where_ref, first_ref, second_ref, stats_ref, means_ref, gp_ref, gain_ref, *refs, orders, odd, with_high):
    *w_refs, high_ref, a_low, a_high, b_low, b_high, some_ref, gn_ref = refs
    half_count, total, block, half_width = a_low.shape
    out_refs = ((a_low, a_high), (b_low, b_high))
    features = 2 * half_width
    together = gn_ref.shape[0] // block
    for r in range(total):
        for d in range(0, len(orders[0]), together):
            tokens = []
            for n in range(together):
                place = where_ref[3] ^ (orders[0][d + n] | odd)
                tokens.append(pl.ds(pl.multiple_of(place * block, 16), block))
                some_ref[n * block : (n + 1) * block, :] = gp_ref[r, tokens[n], :]
            lane = 0
            for w_ref in w_refs:
                rows = w_ref.shape[0]
                gn_ref[:, lane : lane + rows] = lax.dot_general(
                    some_ref[...], w_ref[...], (((1,), (1,)), ((), ())), preferred_element_type=f32
                )
                lane += rows
            for n in range(together):
                mean, inv = stats_ref[r, 0, tokens[n], :], stats_ref[r, 1, tokens[n], :]
                first, second = (
                    jnp.sum(means_ref[r, m, tokens[n], :], axis=-1, keepdims=True) * (1.0 / features) for m in range(2)
                )
                slope = inv * inv * second
                rest = inv * first - slope * mean
                for part, x_ref in enumerate((first_ref, second_ref)):
                    at_d = orders[part].index(orders[0][d + n])
                    for j in range(half_width // LANES):
                        at = slice(part * half_width + LANES * j, part * half_width + LANES * (j + 1))
                        lanes = slice(LANES * j, LANES * (j + 1))
                        value = inv * (gn_ref[n * block : (n + 1) * block, at] * gain_ref[:, at])
                        value -= slope * x_ref[at_d, r, :block, lanes].astype(f32) + rest
                        if with_high:
                            add = high_ref[r, where_ref[0] ^ part, tokens[n], :].astype(f32)
                            value += jnp.where(where_ref[3] == j, add, 0.0)
                        out_refs[part][at_d // half_count][at_d % half_count, r, :, lanes] = value.astype(bf16)


def norm_back(where, first, second, orders, odd, stats, means, gp, weights, gain, high, with_high, waits):
    count, rows, block, half_width = second.shape
    together = 2 * LANES // block
    return call(
        functools.partial(norm_back_kernel, orders=orders, odd=odd, with_high=with_high),
        [((count // 2, *second.shape[1:]), bf16)] * 4,
        (first, second, stats, means, gp, gain, *weights, high), (where,), waits,
        scratch=[((together * block, gp.shape[2]), bf16), ((together * block, 2 * half_width), f32)],
        name="norm_back",
    )


def totals_kernel(where_ref, sums_ref, own_ref, other_ref, gain_ref, shift_ref, out_ref, *, chunk):
    half_width = own_ref.shape[1]
    out_ref[...] = jnp.zeros_like(out_ref)
    for i in range(2):
        lane = pl.ds(pl.multiple_of(i * chunk + where_ref[3] * LANES, LANES), LANES)
        out_ref[0:4, lane] = sums_ref[0:4, LANES * i : LANES * (i + 1)]
    for part, ref in enumerate((own_ref, other_ref)):
        lane = pl.ds(pl.multiple_of((where_ref[0] ^ part) * half_width, LANES), half_width)
        at = slice(part * half_width, (part + 1) * half_width)
        out_ref[4:5, lane] = (ref[0:1, :] - shift_ref[:, at] * ref[1:2, :]) / gain_ref[:, at]
        out_ref[5:6, lane] = ref[1:2, :]


def bf16_parts(row):
    rows = []
    for _ in range(3):
        upper = lax.reduce_precision(row, 8, 7)
        rows.append(upper.astype(bf16))
        row = row - upper
    return rows


def local(inputs, weight, gain, shift, forget_vec, reset_vec, forget_bias, reset_bias, initial, resets, grad_out):
    rows, block_len, features = inputs.shape
    row_block, columns_here = weight.shape
    sections = lax.axis_size("fsdp")
    ranks = lax.axis_size("dp")
    group = sections // 2
    tokens = group * block_len
    index = lax.axis_index("fsdp")
    half, place = index // group, index % group
    rank = lax.axis_index("dp")
    first_half = half == 0
    groups = [list(range(group)), list(range(group, sections))]
    chunk = math.gcd(features, columns_here)
    chunks, piece = features // chunk, chunk // group
    width = chunks * piece
    tiles = width // LANES
    slots = 3 * tiles
    parts = columns_here // chunk
    columns = parts * piece
    aligned = piece == LANES and chunks == 2
    paired = ranks == 2 and aligned
    turn = rank * (columns // LANES) if paired else jnp.zeros_like(rank)
    where = jnp.stack([half, rank, index % 2, place, turn]).astype(jnp.int32)
    bits = [1 << b for b in range(1, group.bit_length() - 1)]
    ways = (bits[::-1], bits)
    orders = []
    for way in ways:
        order = [0]
        for bit in way:
            order += [d | bit for d in order]
        orders.append(order)

    def across(value):
        return lax.ppermute(value, "fsdp", [(j, (j + group) % sections) for j in range(sections)])

    def flipped(value, bit):
        return lax.ppermute(value, "fsdp", [(j, j ^ bit) for j in range(sections)])

    def swapped(value):
        return lax.ppermute(value, "dp", [(0, 1), (1, 0)])

    def shared(value):
        return lax.all_to_all(value, "fsdp", 0, 0, tiled=True, axis_index_groups=groups)

    def own(vector):
        return lax.dynamic_index_in_dim(vector.reshape(-1, chunks, group, piece), place, 2, False).reshape(-1, width)

    def halves_turned(vector):
        low, high = vector[..., : features // 2], vector[..., features // 2 :]
        return jnp.concatenate([jnp.where(first_half, low, high), jnp.where(first_half, high, low)], axis=-1)

    def dealt(value, waits=()):
        if aligned:
            return deal(value, group, waits)
        n, wide = value.shape
        return value.reshape(n, wide // chunk, group, piece).transpose(2, 0, 1, 3).reshape(group, n, wide // group)

    def collected(pieces, dtype, waits=()):
        if aligned:
            return collect(pieces, dtype, waits)
        wide = pieces[0].shape[2]
        back = lambda v: v.reshape(group, -1, wide // piece, piece).transpose(1, 2, 0, 3).reshape(-1, wide * group)
        return jnp.concatenate([back(v) for v in pieces]).astype(dtype)

    mine = shared(dealt(weight)).reshape(-1, columns)
    early_rows = (group - 1) * row_block
    theirs = [across(mine[:early_rows]), across(mine[early_rows:])]
    early_rows += features // 2
    near = list(stats(where, inputs, (1 - resets).astype(f32)[:, None, :], (mine,)))
    for way in zip(*ways):
        near = [jnp.concatenate([value, flipped(value, bit)]) for value, bit in zip(near, way)]
    blocks = [*near, *(flipped(value, 1) for value in near)]
    if paired:
        beside = swapped(mine)
        theirs_beside = []
        for i in range(2):
            theirs[i] = fence(theirs[i], (beside, *theirs_beside[-1:]))
            theirs_beside.append(swapped(theirs[i]))
        early, late = [mine, beside, theirs[0], theirs_beside[0]], [theirs[1], theirs_beside[1]]
    else:
        whole = [lax.all_gather(v, "dp", axis=1, tiled=True) for v in (mine, jnp.concatenate(theirs))]
        whole = jnp.concatenate(whole, axis=0)
        early, late = [whole[:early_rows]], [whole[early_rows:]]
    g_own = shared(dealt(grad_out.reshape(-1, features), (theirs[0],)).reshape(group, rows, block_len, width))

    hfv, hrv = 0.5 * own(forget_vec), 0.5 * own(reset_vec)
    bias = jnp.concatenate([jnp.zeros((1, width), f32), own(forget_bias), own(reset_bias)]).reshape(-1, 1, LANES)
    gain_row, shift_row = halves_turned(gain)[None], halves_turned(shift)[None]
    vector_rows = [*bf16_parts(gain_row), *bf16_parts(shift_row)]
    vector_rows = jnp.pad(jnp.concatenate(vector_rows), ((0, 10), (0, 0)))
    normed, token_stats, keep, *x_own = norm(where, blocks, gain_row, shift_row, orders, aligned)
    if aligned:
        x_own = x_own[0]
    else:
        at = lambda part, d: blocks[2 * (d % 2) + part][orders[part].index(d & ~1)][:, :block_len]
        by_place = jnp.stack([jnp.concatenate([at(0, d), at(1, d)], axis=-1) for d in range(group)])
        in_order = halves_turned(by_place[place ^ jnp.arange(group)]).swapaxes(0, 1).reshape(rows * tokens, features)
        x_own = own(in_order).reshape(rows, tokens, tiles, LANES).swapaxes(1, 2)
    some, some_vectors, early_weight = project(where, normed, vector_rows, early, early_rows, slots)
    p, seg, lead, end, lead_end, vectors, late_weight = blocks_forward(
        where, normed, vector_rows, some, some_vectors, bias, keep, hfv, own(initial)[:, None, :], late,
        features - early_rows,
    )
    weights = (early_weight, late_weight)
    start = across(end)
    lead = lead_forward(p, keep, hfv, lead_end, lead)
    first, back = entry(p, keep, seg, x_own, g_own, hfv, hrv, start, ())
    carry = jnp.where(first_half, across(back), 0.0)
    gp, hidden_own, high_own, sums, final, means = backward(
        where, p, keep, seg, lead, first, x_own, g_own, hfv, hrv, carry, vectors
    )

    mask = (jnp.arange(group) == place)[:, None]

    def norm_part(odd, waits):
        out = norm_back(
            where, *blocks[2 * odd : 2 * odd + 2], orders, odd, token_stats, means, gp, weights, gain_row, high_own, aligned,
            waits,
        )
        if aligned:
            return out
        spread = high_own.swapaxes(1, 2).reshape(rows, group, block_len, chunks, 1, piece).swapaxes(0, 1)
        spread = jnp.where(mask, spread.astype(f32), 0.0).reshape(group, rows, block_len, features)
        spread = halves_turned(spread)[place ^ jnp.arange(group)]
        halves = (spread[..., : features // 2], spread[..., features // 2 :])
        add = [add[d | odd] for add, order in zip(halves, orders) for d in order]
        n = group // 4
        return [(v.astype(f32) + jnp.stack(add[i * n : (i + 1) * n])).astype(bf16) for i, v in enumerate(out)]

    pieces = 1
    cuts = [(row_block // pieces,) * pieces] * (2 if paired else 1)
    by_feature_other, *away = weight_back(normed, gp, sums, weights, 1, group, cuts, ())
    away_got = [swapped(value) for value in away[pieces:]]
    sent = norm_part(1, (by_feature_other,))
    got = [flipped(value, 1) for value in sent]
    by_feature_own, *here = weight_back(normed, gp, sums, weights, 0, group, cuts, sent[:1])
    kept = norm_part(0, (by_feature_own,))
    kept, sent = halve(kept, got, kept[:1])
    bit_pairs = list(zip(*(w[::-1] for w in ways)))
    got = [flipped(value, bit) for value, bit in zip(sent, bit_pairs.pop(0))]
    hidden_got = shared(fence(hidden_own, kept[:1]))
    if paired:
        away = [added(a, b, kept[:1]) for a, b in zip(away, away_got)]
        here_got = [swapped(fence(value, away)) for value in here[pieces:]]
    else:
        away, here = ([lax.psum_scatter(x, "dp", scatter_dimension=2, tiled=True) for x in v] for v in (away, here))
    z_got = [across(value) for value in away]

    hidden = collected([hidden_got.reshape(group, -1, width)], bf16).reshape(rows, block_len, features)
    for way in bit_pairs:
        kept, sent = halve(kept, got, (hidden,))
        got = [flipped(value, bit) for value, bit in zip(sent, way)]
    grad_inputs = finish(where, kept, got)

    if aligned:
        totals = call(
            functools.partial(totals_kernel, chunk=chunk), [((8, features), f32)],
            (sums, by_feature_own, by_feature_other, gain_row, shift_row), (where,), kept[:1], name="totals",
        )[0]
    else:
        spread = jnp.where(mask, sums[:4, :width].reshape(4, chunks, 1, piece), 0.0).reshape(4, features)
        product, shift_sum = jnp.concatenate([by_feature_own, by_feature_other], axis=1)
        gain_sum = (product - shift_row[0] * shift_sum) / gain_row[0]
        totals = jnp.concatenate([spread, halves_turned(jnp.stack([gain_sum, shift_sum]))], axis=0)
    for bit in [1 << b for b in range(group.bit_length() - 1)]:
        totals = added(totals, flipped(totals, bit))
    waits = (grad_inputs, totals)
    grad_weight = []
    for i in range(pieces):
        value = merge(here[i], here_got[i], z_got[i], waits) if paired else added(here[i], z_got[i], waits)
        grad_weight.append(shared(value))
    grad_weight = collected(grad_weight, f32)
    totals = added(totals, swapped(totals)) if ranks == 2 else lax.psum(totals, "dp")
    totals = added(totals, across(totals))

    own_width = features // sections
    if piece == own_width and chunks == 2:
        final = final[:, 0]
        low_part = lax.ppermute(final[:, :piece], "fsdp", [(j + group, j) for j in range(group)])
        final_state = jnp.where(first_half, low_part, final[:, piece:])
    else:
        spread = jnp.where(mask, final.reshape(rows, chunks, 1, piece), 0.0).reshape(rows, features)
        spread = lax.psum(jnp.where(first_half, 0.0, spread), "fsdp")
        final_state = lax.dynamic_slice_in_dim(spread, index * own_width, own_width, 1)

    return (hidden, grad_inputs, final_state, grad_weight, *[totals[i] for i in range(6)])


def solution(mesh):
    in_specs = (
        P("dp", "fsdp", None), P("fsdp", "dp"), P(), P(), P(), P(), P(), P(),
        P("dp", None), P("dp", "fsdp"), P("dp", "fsdp", None),
    )
    out_specs = (
        P("dp", "fsdp", None), P("dp", "fsdp", None), P("dp", "fsdp"), P("fsdp", "dp"), P(), P(), P(), P(), P(), P(),
    )
    return jax.shard_map(local, mesh=mesh, in_specs=in_specs, out_specs=out_specs, check_vma=False)
```

profile of v0, /device:TPU:8, one launch (start us, length us, event | category | flops | bytes accessed | tf_op | source)
XLA Modules:
  0.0 228.9 jit_solution(18079429980527214455)
XLA Ops:
  2.8 4.4 %all-to-all-start = ((bf16[8,128,384]{2,1,0:T(8,128)(2,1)}), bf16[8,128,384]{2,1,0:T(8,128)(2,1)S(1)}, u32[]{:S(2)}, u32[]{:S(2)}) async-start(bf16[8,128,384]{2,1,0:T(8,128)(2,1)} %deal.2), calls=%async_computation | async-start | bytes 1572864 | tf_op jit(solution)/shard_map/all_to_all | solution.py:736
  8.0 10.3 %all-to-all-done = bf16[8,128,384]{2,1,0:T(8,128)(2,1)S(1)} async-done(((bf16[8,128,384]{2,1,0:T(8,128)(2,1)}), bf16[8,128,384]{2,1,0:T(8,128)(2,1)S(1)}, u32[]{:S(2)}, u32[]{:S(2)}) %all-to-all-start) | async-done | bytes 786464 | tf_op jit(solution)/shard_map/all_to_all | solution.py:736
  23.0 4.0 %collective-permute-done = bf16[1,1,144,1024]{3,2,1,0:T(8,128)(2,1)S(1)} collective-permute-done((bf16[1,1,144,1024]{3,2,1,0:T(8,128)(2,1)S(1)}, bf16[1,1,144,1024]{3,2,1,0:T(8,128)(2,1)S(1)}, u32[]{:S(2)}, u32[]{:S(2)}) %collective-permute-start) | collective-permute-done | bytes 294944 | tf_op jit(solution)/shard_map/ppermute | solution.py:730
  30.2 2.7 %collective-permute-start.7 = (bf16[896,384]{1,0:T(8,128)(2,1)S(1)}, bf16[896,384]{1,0:T(8,128)(2,1)S(1)}, u32[]{:S(2)}, u32[]{:S(2)}) collective-permute-start(bf16[896,384]{1,0:T(8,128)(2,1)S(1)} %bitcast.62), channel_id=1, source_target_pairs={{0,8},{1,9},{2,10},{3,11},{4,12},{5,13},{6,14},{7,15},{8,0},{9,1},... | collective-permute-start | bytes 2064392 | tf_op jit(solution)/shard_map/ppermute | solution.py:727
  35.3 5.5 %collective-permute-done.1 = bf16[2,1,144,1024]{3,2,1,0:T(8,128)(2,1)S(1)} collective-permute-done((bf16[2,1,144,1024]{3,2,1,0:T(8,128)(2,1)S(1)}, bf16[2,1,144,1024]{3,2,1,0:T(8,128)(2,1)S(1)}, u32[]{:S(2)}, u32[]{:S(2)}) %collective-permute-start.1) | collective-permute-done | bytes 589856 | tf_op jit(solution)/shard_map/ppermute | solution.py:730
  41.9 10.0 %collective-permute-done.3 = bf16[2,1,128,1024]{3,2,1,0:T(8,128)(2,1)S(1)} collective-permute-done((bf16[2,1,128,1024]{3,2,1,0:T(8,128)(2,1)S(1)}, bf16[2,1,128,1024]{3,2,1,0:T(8,128)(2,1)S(1)}, u32[]{:S(2)}, u32[]{:S(2)}) %collective-permute-start.3) | collective-permute-done | bytes 524320 | tf_op jit(solution)/shard_map/ppermute | solution.py:730
  52.7 8.0 %collective-permute-done.7.refs_0_ = bf16[896,384]{1,0:T(8,128)(2,1)S(1)} collective-permute-done((bf16[896,384]{1,0:T(8,128)(2,1)S(1)}, bf16[896,384]{1,0:T(8,128)(2,1)S(1)}, u32[]{:S(2)}, u32[]{:S(2)}) %collective-permute-start.7) | collective-permute-done | bytes 688160 | tf_op jit(solution)/shard_map/ppermute | solution.py:727
  67.0 5.4 %all-to-all-start.1 = ((bf16[8,1,128,256]{3,2,1,0:T(8,128)(2,1)}), bf16[8,1,128,256]{3,2,1,0:T(8,128)(2,1)}, u32[]{:S(2)}, u32[]{:S(2)}) async-start(bf16[8,1,128,256]{3,2,1,0:T(8,128)(2,1)} %bitcast.24), calls=%async_computation.1 | async-start | bytes 1048576 | tf_op jit(solution)/shard_map/all_to_all | solution.py:736
  73.2 2.2 collective-permute-start.9
  76.1 6.8 %collective-permute-done.9.refs_0_ = bf16[128,384]{1,0:T(8,128)(2,1)S(1)} collective-permute-done((bf16[128,384]{1,0:T(8,128)(2,1)S(1)}, bf16[128,384]{1,0:T(8,128)(2,1)S(1)}, u32[]{:S(2)}, u32[]{:S(2)}) %collective-permute-start.9) | collective-permute-done | bytes 98336 | tf_op jit(solution)/shard_map/ppermute | solution.py:727
  84.1 4.0 %norm.1 = (bf16[1,1024,2048]{2,1,0:T(8,128)(2,1)S(1)}, f32[1,2,1024,128]{3,2,1,0:T(8,128)S(1)}, f32[1,1088,128]{2,1,0:T(8,128)S(1)}, bf16[1,2,1024,128]{3,2,1,0:T(8,128)(2,1)S(1)}) custom-call(s32[5]{0:T(128)S(1)} %stack.23.refs_0_, f32[1,2048]{1,0:T(1,128)S(1)} %bitcast.54, f32[1,2048]{1,0:T(1,128)S(1)} %bitcast.58, ...), custom_call_target="tpu_custom_call" | custom-call | tf_op jit(solution)/shard_map/norm/pallas_call | solution.py:41
  89.2 6.3 %project.1 = (f32[1,6,1024,128]{3,2,1,0:T(8,128)S(1)}, f32[16,768]{1,0:T(8,128)S(1)}, bf16[1920,768]{1,0:T(8,128)(2,1)S(1)}) custom-call(s32[5]{0:T(128)S(1)} %stack.23.refs_0_, bf16[1,1024,2048]{2,1,0:T(8,128)(2,1)S(1)} %get-tuple-element.58.refs_1_.refs_0_, bf16[16,2048]{1,0:T(8,128)(2,1)S(1)} %copy-done.40, bf16[1024,384]{1,0:T(8,128)(2,1)S(1)} %bitcast.49, ...), custom_call_target="tpu_custom_call" | custom-call | tf_op jit(solution)/shard_map/project/pallas_call | solution.py:41
  95.6 6.2 %blocks_forward.1 = (f32[1,6,1088,128]{3,2,1,0:T(8,128)S(1)}, f32[1,2,1088,128]{3,2,1,0:T(8,128)S(1)}, f32[1,2,336,128]{3,2,1,0:T(8,128)S(1)}, f32[1,1,256]{2,1,...) custom-call(s32[5]{0:T(128)S(1)} %stack.23.refs_0_, ...), custom_call_target="tpu_custom_call" | custom-call | tf_op jit(solution)/shard_map/blocks_forward/pallas_call | solution.py:41
  106.7 4.0 %collective-permute-done.11.refs_7_ = f32[1,1,256]{2,1,0:T(1,128)S(1)} collective-permute-done((f32[1,1,256]{2,1,0:T(1,128)}, f32[1,1,256]{2,1,0:T(1,128)S(1)}, u32[]{:S(2)}, u32[]{:S(2)}) %collective-permute-start.11) | collective-permute-done | bytes 1056 | tf_op jit(solution)/shard_map/ppermute | solution.py:727
  110.7 1.9 copy-done.4
  114.9 3.9 %entry.1 = (f32[1,2,200,128]{3,2,1,0:T(8,128)S(1)}, f32[1,1,256]{2,1,0:T(1,128)S(1)}) custom-call(f32[1,6,1088,128]{3,2,1,0:T(8,128)S(1)} %copy-done.4, f32[1,1088,128]{2,1,0:T(8,128)S(1)} %get-tuple-element.61.refs_6_.refs_1_.refs_2_, f32[1,2,1088,128]{3,2,1,0:T(8,128)S(1)} %copy-done.19, bf16[1,2,1024,128]{3,2,1,0:T(8,128)(2,1)S(1)} %copy-done.31, ...), custom_call_target="tpu_custom_call" | custom-call | tf_op jit(solution)/shard_map/entry/pallas_call | solution.py:41
  119.0 4.1 %lead_forward.1.refs_4_ = f32[1,2,816,128]{3,2,1,0:T(8,128)S(1)} custom-call(f32[1,6,1088,128]{3,2,1,0:T(8,128)S(1)} %copy-done.5, f32[1,1088,128]{2,1,0:T(8,128)S(1)} %get-tuple-element.61.refs_6_.refs_1_.refs_2_, f32[1,256]{1,0:T(1,128)S(1)} %fusion.7.refs_7_.refs_2_.refs_5_.refs_8_, f32[1,1,256]{2,1,0:T(1,128)S(1)} %get-tuple-element.64.refs_3_, ...), custom_call_target="tpu_custom_call" | custom-call | tf_op jit(solution)/shard_map/lead_forward/pallas_call | solution.py:41
  124.4 7.1 %backward.1 = (bf16[1,1024,768]{2,1,0:T(8,128)(2,1)S(1)}, bf16[8,1,128,256]{3,2,1,0:T(8,128)(2,1)S(1)}, bf16[1,2,1024,128]{3,2,1,0:T(8,128)(2,1)S(1)}, f32[8,768...) custom-call(s32[5]{0:T(128)S(1)} %copy-done.50, f32[1,6,1088,128]{3,2,1,0:T(8,128)S(1)} %copy-done.5, ...), custom_call_target="tpu_custom_call" | custom-call | tf_op jit(solution)/shard_map/backward/pallas_call | solution.py:41
  131.5 3.1 %weight_back.2 = (f32[2,1024]{1,0:T(2,128)S(1)}, bf16[8,128,384]{2,1,0:T(8,128)(2,1)S(1)}, bf16[8,128,384]{2,1,0:T(8,128)(2,1)}) custom-call(bf16[1,1024,2048]{2,1,0:T(8,128)(2,1)S(1)} %copy-done.2, bf16[1,1024,768]{2,1,0:T(8,128)(2,1)S(1)} %get-tuple-element.74.refs_1_.refs_5_, f32[8,768]{1,0:T(8,128)S(1)} %get-tuple-element.78.refs_2_.refs_1_, ...), custom_call_target="tpu_custom_call" | custom-call | tf_op jit(solution)/shard_map/weight_back/pallas_call | solution.py:41
  135.5 4.2 %norm_back.2 = (bf16[2,1,128,1024]{3,2,1,0:T(8,128)(2,1)S(1)}, bf16[2,1,128,1024]{3,2,1,0:T(8,128)(2,1)S(1)}, bf16[2,1,128,1024]{3,2,1,0:T(8,128)(2,1)S(1)}, bf16[2,1,128,1024]{3,2,1,0:T(8,128)(2,1)S(1)}) custom-call(s32[5]{0:T(128)S(1)} %copy-done.50, bf16[4,1,144,1024]{3,2,1,0:T(8,128)(2,1)} %collective-permute-done.4.refs_5_.refs_1_, ...), custom_call_target="tpu_custom_call" | custom-call | tf_op jit(solution)/shard_map/norm_back/pallas_call | solution.py:41
  142.3 2.3 weight_back.3
  146.3 3.8 %norm_back.3 = (bf16[2,1,128,1024]{3,2,1,0:T(8,128)(2,1)S(1)}, bf16[2,1,128,1024]{3,2,1,0:T(8,128)(2,1)S(1)}, bf16[2,1,128,1024]{3,2,1,0:T(8,128)(2,1)S(1)}, bf16[2,1,128,1024]{3,2,1,0:T(8,128)(2,1)S(1)}) custom-call(s32[5]{0:T(128)S(1)} %copy-done.50, bf16[4,1,144,1024]{3,2,1,0:T(8,128)(2,1)S(1)} %copy-done.15, ...), custom_call_target="tpu_custom_call" | custom-call | tf_op jit(solution)/shard_map/norm_back/pallas_call | solution.py:41
  153.2 5.3 %all-to-all-start.2 = ((bf16[8,1,128,256]{3,2,1,0:T(8,128)(2,1)}), bf16[8,1,128,256]{3,2,1,0:T(8,128)(2,1)S(1)}, u32[]{:S(2)}, u32[]{:S(2)}) async-start(bf16[8,1,128,256]{3,2,1,0:T(8,128)(2,1)} %fence.6), calls=%async_computation.2 | async-start | bytes 1048576 | tf_op jit(solution)/shard_map/all_to_all | solution.py:736
  164.4 2.8 %collective-permute-start.24 = (bf16[8,128,384]{2,1,0:T(8,128)(2,1)S(1)}, bf16[8,128,384]{2,1,0:T(8,128)(2,1)S(1)}, u32[]{:S(2)}, u32[]{:S(2)}) collective-permute-start(bf16[8,128,384]{2,1,0:T(8,128)(2,1)S(1)} %copy-done.24), channel_id=1, source_target_pairs={{0,8},{1,9},{2,10},{3,11},{4,12},{5,13},{6,14},{7,15},{8,0},{9,1},... | collective-permute-start | bytes 2359304 | tf_op jit(solution)/shard_map/ppermute | solution.py:727
  168.3 9.9 %collective-permute-done.17.refs_2_ = bf16[2,1,128,1024]{3,2,1,0:T(8,128)(2,1)} collective-permute-done((bf16[2,1,128,1024]{3,2,1,0:T(8,128)(2,1)}, bf16[2,1,128,1024]{3,2,1,0:T(8,128)(2,1)}, u32[]{:S(2)}, u32[]{:S(2)}) %collective-permute-start.17) | collective-permute-done | bytes 524320 | tf_op jit(solution)/shard_map/ppermute | solution.py:730
  178.2 9.4 %collective-permute-done.18.refs_3_ = bf16[2,1,128,1024]{3,2,1,0:T(8,128)(2,1)} collective-permute-done((bf16[2,1,128,1024]{3,2,1,0:T(8,128)(2,1)}, bf16[2,1,128,1024]{3,2,1,0:T(8,128)(2,1)}, u32[]{:S(2)}, u32[]{:S(2)}) %collective-permute-start.18) | collective-permute-done | bytes 524320 | tf_op jit(solution)/shard_map/ppermute | solution.py:730
  190.2 2.5 %collective-permute-start.19 = (bf16[1,1,128,1024]{3,2,1,0:T(8,128)(2,1)S(1)}, bf16[1,1,128,1024]{3,2,1,0:T(8,128)(2,1)S(1)}, u32[]{:S(2)}, u32[]{:S(2)}) collective-permute-start(bf16[1,1,128,1024]{3,2,1,0:T(8,128)(2,1)S(1)} %get-tuple-element.95), channel_id=1, source_target_pairs={{0,4},{1,5},{2,6},{3,7},{4,0},{5,1},{6,2},{7,3},{8,12},{9,13},{10,... | collective-permute-start | bytes 786440 | tf_op jit(solution)/shard_map/ppermute | solution.py:730
  196.7 5.0 %collective-permute-done.26.refs_1_ = f32[8,2048]{1,0:T(8,128)S(1)} collective-permute-done((f32[8,2048]{1,0:T(8,128)S(1)}, f32[8,2048]{1,0:T(8,128)S(1)}, u32[]{:S(2)}, u32[]{:S(2)}) %collective-permute-start.26) | collective-permute-done | bytes 65568 | tf_op jit(solution)/shard_map/ppermute | solution.py:730
  202.2 3.9 %collective-permute-done.27.refs_1_ = f32[8,2048]{1,0:T(8,128)S(1)} collective-permute-done((f32[8,2048]{1,0:T(8,128)S(1)}, f32[8,2048]{1,0:T(8,128)S(1)}, u32[]{:S(2)}, u32[]{:S(2)}) %collective-permute-start.27) | collective-permute-done | bytes 65568 | tf_op jit(solution)/shard_map/ppermute | solution.py:730
  209.8 5.0 %all-to-all-start.3 = ((bf16[8,128,384]{2,1,0:T(8,128)(2,1)}), bf16[8,128,384]{2,1,0:T(8,128)(2,1)S(1)}, u32[]{:S(2)}, u32[]{:S(2)}) async-start(bf16[8,128,384]{2,1,0:T(8,128)(2,1)} %merge.1), calls=%async_computation.3 | async-start | bytes 1572864 | tf_op jit(solution)/shard_map/all_to_all | solution.py:736
  216.6 2.5 %collective-permute-done.28.refs_1_ = f32[8,2048]{1,0:T(8,128)S(1)} collective-permute-done((f32[8,2048]{1,0:T(8,128)S(1)}, f32[8,2048]{1,0:T(8,128)S(1)}, u32[]{:S(2)}, u32[]{:S(2)}) %collective-permute-start.28) | collective-permute-done | bytes 65568 | tf_op jit(solution)/shard_map/ppermute | solution.py:733
  220.3 5.7 %collective-permute-done.21 = f32[1,128]{1,0:T(1,128)S(1)} collective-permute-done((f32[1,128]{1,0:T(1,128)S(1)}, f32[1,128]{1,0:T(1,128)S(1)}, u32[]{:S(2)}, u32[]{:S(2)}) %collective-permute-start.21) | collective-permute-done | bytes 544 | tf_op jit(solution)/shard_map/ppermute | solution.py:872
  (226 shorter events, 65.5 us)
Async XLA Ops:
  2.8 15.5 %all-to-all-start = ((bf16[8,128,384]{2,1,0:T(8,128)(2,1)}), bf16[8,128,384]{2,1,0:T(8,128)(2,1)S(1)}, u32[]{:S(2)}, u32[]{:S(2)}) async-start(bf16[8,128,384]{2,1,0:T(8,128)(2,1)} %deal.2), calls=%async_computation | async-start | bytes 1572864 | tf_op jit(solution)/shard_map/all_to_all | solution.py:736
  19.2 7.8 %collective-permute-start = (bf16[1,1,144,1024]{3,2,1,0:T(8,128)(2,1)S(1)}, bf16[1,1,144,1024]{3,2,1,0:T(8,128)(2,1)S(1)}, u32[]{:S(2)}, u32[]{:S(2)}) collective-permute-start(bf16[1,1,144,1024]{3,2,1,0:T(8,128)(2,1)S(1)} %get-tuple-element.56), channel_id=1, source_target_pairs={{0,4},{1,5},{2,6},{3,7},{4,0},{5,1},{6,2},{7,3},{8,12},{9,13},{10,... | collective-permute-start | bytes 884744 | tf_op jit(solution)/shard_map/ppermute | solution.py:730
  19.9 8.6 %collective-permute-start.2 = (bf16[1,1,128,1024]{3,2,1,0:T(8,128)(2,1)S(1)}, bf16[1,1,128,1024]{3,2,1,0:T(8,128)(2,1)S(1)}, u32[]{:S(2)}, u32[]{:S(2)}) collective-permute-start(bf16[1,1,128,1024]{3,2,1,0:T(8,128)(2,1)S(1)} %get-tuple-element.57), channel_id=1, source_target_pairs={{0,2},{1,3},{2,0},{3,1},{4,6},{5,7},{6,4},{7,5},{8,10},{9,11},{10,... | collective-permute-start | bytes 786440 | tf_op jit(solution)/shard_map/ppermute | solution.py:730
  21.4 39.3 %collective-permute-start.6 = (bf16[1024,384]{1,0:T(8,128)(2,1)S(1)}, bf16[1024,384]{1,0:T(8,128)(2,1)S(1)}, u32[]{:S(2)}, u32[]{:S(2)}) collective-permute-start(bf16[1024,384]{1,0:T(8,128)(2,1)S(1)} %bitcast.48), channel_id=1, source_target_pairs={{0,16},{16,0},{1,17},{17,1},{2,18},{18,2},{3,19},{19,3},{4,20},{20... | collective-permute-start | bytes 2359304 | tf_op jit(solution)/shard_map/ppermute | solution.py:733
  27.1 13.6 %collective-permute-start.1 = (bf16[2,1,144,1024]{3,2,1,0:T(8,128)(2,1)S(1)}, bf16[2,1,144,1024]{3,2,1,0:T(8,128)(2,1)S(1)}, u32[]{:S(2)}, u32[]{:S(2)}) collective-permute-start(bf16[2,1,144,1024]{3,2,1,0:T(8,128)(2,1)S(1)} %pad_maximum_fusion), channel_id=1, source_target_pairs={{0,2},{1,3},{2,0},{3,1},{4,6},{5,7},{6,4},{7,5},{8,10},{9,11},{10,... | collective-permute-start | bytes 1769480 | tf_op jit(solution)/shard_map/ppermute | solution.py:730
  28.6 23.3 %collective-permute-start.3 = (bf16[2,1,128,1024]{3,2,1,0:T(8,128)(2,1)S(1)}, bf16[2,1,128,1024]{3,2,1,0:T(8,128)(2,1)S(1)}, u32[]{:S(2)}, u32[]{:S(2)}) collective-permute-start(bf16[2,1,128,1024]{3,2,1,0:T(8,128)(2,1)S(1)} %pad_maximum_fusion.1), channel_id=1, source_target_pairs={{0,4},{1,5},{2,6},{3,7},{4,0},{5,1},{6,2},{7,3},{8,12},{9,13},{10,... | collective-permute-start | bytes 1572872 | tf_op jit(solution)/shard_map/ppermute | solution.py:730
  30.2 30.5 %collective-permute-start.7 = (bf16[896,384]{1,0:T(8,128)(2,1)S(1)}, bf16[896,384]{1,0:T(8,128)(2,1)S(1)}, u32[]{:S(2)}, u32[]{:S(2)}) collective-permute-start(bf16[896,384]{1,0:T(8,128)(2,1)S(1)} %bitcast.62), channel_id=1, source_target_pairs={{0,8},{1,9},{2,10},{3,11},{4,12},{5,13},{6,14},{7,15},{8,0},{9,1},... | collective-permute-start | bytes 2064392 | tf_op jit(solution)/shard_map/ppermute | solution.py:727
  40.8 43.2 %collective-permute-start.4 = (bf16[4,1,144,1024]{3,2,1,0:T(8,128)(2,1)S(1)}, bf16[4,1,144,1024]{3,2,1,0:T(8,128)(2,1)}, u32[]{:S(2)}, u32[]{:S(2)}) collective-permute-start(bf16[4,1,144,1024]{3,2,1,0:T(8,128)(2,1)S(1)} %constant_dynamic-update-slice_fusion.refs_3_.refs_1_), channel_id=1, source_target_pairs={{0,1},{1,0},{2,3},{3,2},{4,5},{5,4},{6,7},{7,6},{8,9},{9,8},{10,11... | collective-permute-start | bytes 3538952 | tf_op jit(solution)/shard_map/ppermute | solution.py:730
  52.7 31.3 %collective-permute-start.5 = (bf16[4,1,128,1024]{3,2,1,0:T(8,128)(2,1)}, bf16[4,1,128,1024]{3,2,1,0:T(8,128)(2,1)}, u32[]{:S(2)}, u32[]{:S(2)}) collective-permute-start(bf16[4,1,128,1024]{3,2,1,0:T(8,128)(2,1)} %constant_dynamic-update-slice_fusion.3.refs_4_.refs_2_), channel_id=1, source_target_pairs={{0,1},{1,0},{2,3},{3,2},{4,5},{5,4},{6,7},{7,6},{8,9},{9,8},{10,11... | collective-permute-start | bytes 3145736 | tf_op jit(solution)/shard_map/ppermute | solution.py:730
  62.5 20.4 %collective-permute-start.8 = (bf16[896,384]{1,0:T(8,128)(2,1)}, bf16[896,384]{1,0:T(8,128)(2,1)}, u32[]{:S(2)}, u32[]{:S(2)}) collective-permute-start(bf16[896,384]{1,0:T(8,128)(2,1)} %fence.4.refs_5_.refs_1_), channel_id=1, source_target_pairs={{0,16},{16,0},{1,17},{17,1},{2,18},{18,2},{3,19},{19,3},{4,20},{20... | collective-permute-start | bytes 2064392 | tf_op jit(solution)/shard_map/ppermute | solution.py:733
  67.0 39.7 %all-to-all-start.1 = ((bf16[8,1,128,256]{3,2,1,0:T(8,128)(2,1)}), bf16[8,1,128,256]{3,2,1,0:T(8,128)(2,1)}, u32[]{:S(2)}, u32[]{:S(2)}) async-start(bf16[8,1,128,256]{3,2,1,0:T(8,128)(2,1)} %bitcast.24), calls=%async_computation.1 | async-start | bytes 1048576 | tf_op jit(solution)/shard_map/all_to_all | solution.py:736
  73.2 9.7 %collective-permute-start.9 = (bf16[128,384]{1,0:T(8,128)(2,1)S(1)}, bf16[128,384]{1,0:T(8,128)(2,1)S(1)}, u32[]{:S(2)}, u32[]{:S(2)}) collective-permute-start(bf16[128,384]{1,0:T(8,128)(2,1)S(1)} %slice_bitcast_fusion), channel_id=1, source_target_pairs={{0,8},{1,9},{2,10},{3,11},{4,12},{5,13},{6,14},{7,15},{8,0},{9,1},... | collective-permute-start | bytes 294920 | tf_op jit(solution)/shard_map/ppermute | solution.py:727
  83.5 12.1 %collective-permute-start.10 = (bf16[128,384]{1,0:T(8,128)(2,1)}, bf16[128,384]{1,0:T(8,128)(2,1)S(1)}, u32[]{:S(2)}, u32[]{:S(2)}) collective-permute-start(bf16[128,384]{1,0:T(8,128)(2,1)} %fence.5.refs_9_), channel_id=1, source_target_pairs={{0,16},{16,0},{1,17},{17,1},{2,18},{18,2},{3,19},{19,3},{4,20},{20... | collective-permute-start | bytes 294920 | tf_op jit(solution)/shard_map/ppermute | solution.py:733
  106.0 4.7 %collective-permute-start.11 = (f32[1,1,256]{2,1,0:T(1,128)}, f32[1,1,256]{2,1,0:T(1,128)S(1)}, u32[]{:S(2)}, u32[]{:S(2)}) collective-permute-start(f32[1,1,256]{2,1,0:T(1,128)} %get-tuple-element.67), channel_id=1, source_target_pairs={{0,8},{1,9},{2,10},{3,11},{4,12},{5,13},{6,14},{7,15},{8,0},{9,1},... | collective-permute-start | bytes 3080 | tf_op jit(solution)/shard_map/ppermute | solution.py:727
  118.9 4.8 %collective-permute-start.12 = (f32[1,1,256]{2,1,0:T(1,128)S(1)}, f32[1,1,256]{2,1,0:T(1,128)S(1)}, u32[]{:S(2)}, u32[]{:S(2)}) collective-permute-start(f32[1,1,256]{2,1,0:T(1,128)S(1)} %get-tuple-element.69), channel_id=1, source_target_pairs={{0,8},{1,9},{2,10},{3,11},{4,12},{5,13},{6,14},{7,15},{8,0},{9,1},... | collective-permute-start | bytes 3080 | tf_op jit(solution)/shard_map/ppermute | solution.py:727
  139.7 10.5 %collective-permute-start.14 = (bf16[2,1,128,1024]{3,2,1,0:T(8,128)(2,1)S(1)}, bf16[2,1,128,1024]{3,2,1,0:T(8,128)(2,1)S(1)}, u32[]{:S(2)}, u32[]{:S(2)}) collective-permute-start(bf16[2,1,128,1024]{3,2,1,0:T(8,128)(2,1)S(1)} %get-tuple-element.86), channel_id=1, source_target_pairs={{0,1},{1,0},{2,3},{3,2},{4,5},{5,4},{6,7},{7,6},{8,9},{9,8},{10,11... | collective-permute-start | bytes 1572872 | tf_op jit(solution)/shard_map/ppermute | solution.py:730
  139.8 10.4 %collective-permute-start.15 = (bf16[2,1,128,1024]{3,2,1,0:T(8,128)(2,1)S(1)}, bf16[2,1,128,1024]{3,2,1,0:T(8,128)(2,1)S(1)}, u32[]{:S(2)}, u32[]{:S(2)}) collective-permute-start(bf16[2,1,128,1024]{3,2,1,0:T(8,128)(2,1)S(1)} %get-tuple-element.87), channel_id=1, source_target_pairs={{0,1},{1,0},{2,3},{3,2},{4,5},{5,4},{6,7},{7,6},{8,9},{9,8},{10,11... | collective-permute-start | bytes 1572872 | tf_op jit(solution)/shard_map/ppermute | solution.py:730
  140.2 9.9 %collective-permute-start.16 = (bf16[2,1,128,1024]{3,2,1,0:T(8,128)(2,1)S(1)}, bf16[2,1,128,1024]{3,2,1,0:T(8,128)(2,1)S(1)}, u32[]{:S(2)}, u32[]{:S(2)}) collective-permute-start(bf16[2,1,128,1024]{3,2,1,0:T(8,128)(2,1)S(1)} %get-tuple-element.88), channel_id=1, source_target_pairs={{0,1},{1,0},{2,3},{3,2},{4,5},{5,4},{6,7},{7,6},{8,9},{9,8},{10,11... | collective-permute-start | bytes 1572872 | tf_op jit(solution)/shard_map/ppermute | solution.py:730
  140.3 9.9 %collective-permute-start.13 = (bf16[2,1,128,1024]{3,2,1,0:T(8,128)(2,1)S(1)}, bf16[2,1,128,1024]{3,2,1,0:T(8,128)(2,1)S(1)}, u32[]{:S(2)}, u32[]{:S(2)}) collective-permute-start(bf16[2,1,128,1024]{3,2,1,0:T(8,128)(2,1)S(1)} %get-tuple-element.80.refs_5_), channel_id=1, source_target_pairs={{0,1},{1,0},{2,3},{3,2},{4,5},{5,4},{6,7},{7,6},{8,9},{9,8},{10,11... | collective-permute-start | bytes 1572872 | tf_op jit(solution)/shard_map/ppermute | solution.py:730
  140.8 19.8 %collective-permute-start.22 = (bf16[8,128,384]{2,1,0:T(8,128)(2,1)}, bf16[8,128,384]{2,1,0:T(8,128)(2,1)}, u32[]{:S(2)}, u32[]{:S(2)}) collective-permute-start(bf16[8,128,384]{2,1,0:T(8,128)(2,1)} %get-tuple-element.101), channel_id=1, source_target_pairs={{0,16},{16,0},{1,17},{17,1},{2,18},{18,2},{3,19},{19,3},{4,20},{20... | collective-permute-start | bytes 2359304 | tf_op jit(solution)/shard_map/ppermute | solution.py:733
  153.2 14.1 %all-to-all-start.2 = ((bf16[8,1,128,256]{3,2,1,0:T(8,128)(2,1)}), bf16[8,1,128,256]{3,2,1,0:T(8,128)(2,1)S(1)}, u32[]{:S(2)}, u32[]{:S(2)}) async-start(bf16[8,1,128,256]{3,2,1,0:T(8,128)(2,1)} %fence.6), calls=%async_computation.2 | async-start | bytes 1048576 | tf_op jit(solution)/shard_map/all_to_all | solution.py:736
  158.6 19.6 %collective-permute-start.17 = (bf16[2,1,128,1024]{3,2,1,0:T(8,128)(2,1)}, bf16[2,1,128,1024]{3,2,1,0:T(8,128)(2,1)}, u32[]{:S(2)}, u32[]{:S(2)}) collective-permute-start(bf16[2,1,128,1024]{3,2,1,0:T(8,128)(2,1)} %get-tuple-element.91), channel_id=1, source_target_pairs={{0,2},{1,3},{2,0},{3,1},{4,6},{5,7},{6,4},{7,5},{8,10},{9,11},{10,... | collective-permute-start | bytes 1572872 | tf_op jit(solution)/shard_map/ppermute | solution.py:730
  160.0 27.6 %collective-permute-start.18 = (bf16[2,1,128,1024]{3,2,1,0:T(8,128)(2,1)}, bf16[2,1,128,1024]{3,2,1,0:T(8,128)(2,1)}, u32[]{:S(2)}, u32[]{:S(2)}) collective-permute-start(bf16[2,1,128,1024]{3,2,1,0:T(8,128)(2,1)} %get-tuple-element.92), channel_id=1, source_target_pairs={{0,4},{1,5},{2,6},{3,7},{4,0},{5,1},{6,2},{7,3},{8,12},{9,13},{10,... | collective-permute-start | bytes 1572872 | tf_op jit(solution)/shard_map/ppermute | solution.py:730
  162.8 44.7 %collective-permute-start.23 = (bf16[8,128,384]{2,1,0:T(8,128)(2,1)}, bf16[8,128,384]{2,1,0:T(8,128)(2,1)S(1)}, u32[]{:S(2)}, u32[]{:S(2)}) collective-permute-start(bf16[8,128,384]{2,1,0:T(8,128)(2,1)} %fence.7), channel_id=1, source_target_pairs={{0,16},{16,0},{1,17},{17,1},{2,18},{18,2},{3,19},{19,3},{4,20},{20... | collective-permute-start | bytes 2359304 | tf_op jit(solution)/shard_map/ppermute | solution.py:733
  164.4 43.2 %collective-permute-start.24 = (bf16[8,128,384]{2,1,0:T(8,128)(2,1)S(1)}, bf16[8,128,384]{2,1,0:T(8,128)(2,1)S(1)}, u32[]{:S(2)}, u32[]{:S(2)}) collective-permute-start(bf16[8,128,384]{2,1,0:T(8,128)(2,1)S(1)} %copy-done.24), channel_id=1, source_target_pairs={{0,8},{1,9},{2,10},{3,11},{4,12},{5,13},{6,14},{7,15},{8,0},{9,1},... | collective-permute-start | bytes 2359304 | tf_op jit(solution)/shard_map/ppermute | solution.py:727
  190.2 15.9 %collective-permute-start.19 = (bf16[1,1,128,1024]{3,2,1,0:T(8,128)(2,1)S(1)}, bf16[1,1,128,1024]{3,2,1,0:T(8,128)(2,1)S(1)}, u32[]{:S(2)}, u32[]{:S(2)}) collective-permute-start(bf16[1,1,128,1024]{3,2,1,0:T(8,128)(2,1)S(1)} %get-tuple-element.95), channel_id=1, source_target_pairs={{0,4},{1,5},{2,6},{3,7},{4,0},{5,1},{6,2},{7,3},{8,12},{9,13},{10,... | collective-permute-start | bytes 786440 | tf_op jit(solution)/shard_map/ppermute | solution.py:730
  192.8 13.3 %collective-permute-start.20 = (bf16[1,1,128,1024]{3,2,1,0:T(8,128)(2,1)S(1)}, bf16[1,1,128,1024]{3,2,1,0:T(8,128)(2,1)S(1)}, u32[]{:S(2)}, u32[]{:S(2)}) collective-permute-start(bf16[1,1,128,1024]{3,2,1,0:T(8,128)(2,1)S(1)} %get-tuple-element.96), channel_id=1, source_target_pairs={{0,2},{1,3},{2,0},{3,1},{4,6},{5,7},{6,4},{7,5},{8,10},{9,11},{10,... | collective-permute-start | bytes 786440 | tf_op jit(solution)/shard_map/ppermute | solution.py:730
  196.0 5.8 %collective-permute-start.26 = (f32[8,2048]{1,0:T(8,128)S(1)}, f32[8,2048]{1,0:T(8,128)S(1)}, u32[]{:S(2)}, u32[]{:S(2)}) collective-permute-start(f32[8,2048]{1,0:T(8,128)S(1)} %added.7.refs_0_), channel_id=1, source_target_pairs={{0,2},{1,3},{2,0},{3,1},{4,6},{5,7},{6,4},{7,5},{8,10},{9,11},{10,... | collective-permute-start | bytes 196616 | tf_op jit(solution)/shard_map/ppermute | solution.py:730
  201.7 4.3 %collective-permute-start.27 = (f32[8,2048]{1,0:T(8,128)S(1)}, f32[8,2048]{1,0:T(8,128)S(1)}, u32[]{:S(2)}, u32[]{:S(2)}) collective-permute-start(f32[8,2048]{1,0:T(8,128)S(1)} %added.8.refs_0_), channel_id=1, source_target_pairs={{0,4},{1,5},{2,6},{3,7},{4,0},{5,1},{6,2},{7,3},{8,12},{9,13},{10,... | collective-permute-start | bytes 196616 | tf_op jit(solution)/shard_map/ppermute | solution.py:730
  209.8 17.8 %all-to-all-start.3 = ((bf16[8,128,384]{2,1,0:T(8,128)(2,1)}), bf16[8,128,384]{2,1,0:T(8,128)(2,1)S(1)}, u32[]{:S(2)}, u32[]{:S(2)}) async-start(bf16[8,128,384]{2,1,0:T(8,128)(2,1)} %merge.1), calls=%async_computation.3 | async-start | bytes 1572864 | tf_op jit(solution)/shard_map/all_to_all | solution.py:736
  215.3 10.6 %collective-permute-start.21 = (f32[1,128]{1,0:T(1,128)S(1)}, f32[1,128]{1,0:T(1,128)S(1)}, u32[]{:S(2)}, u32[]{:S(2)}) collective-permute-start(f32[1,128]{1,0:T(1,128)S(1)} %slice.66), channel_id=1, source_target_pairs={{8,0},{9,1},{10,2},{11,3},{12,4},{13,5},{14,6},{15,7},{24,16},{25,... | collective-permute-start | bytes 1544 | tf_op jit(solution)/shard_map/ppermute | solution.py:872
  219.1 7.8 %collective-permute-start.29 = (f32[8,2048]{1,0:T(8,128)S(1)}, f32[8,2048]{1,0:T(8,128)S(1)}, u32[]{:S(2)}, u32[]{:S(2)}) collective-permute-start(f32[8,2048]{1,0:T(8,128)S(1)} %added.10.refs_0_), channel_id=1, source_target_pairs={{0,8},{1,9},{2,10},{3,11},{4,12},{5,13},{6,14},{7,15},{8,0},{9,1},... | collective-permute-start | bytes 196616 | tf_op jit(solution)/shard_map/ppermute | solution.py:727
  (67 other events, 530.6 us)
where the time goes:
time: 231 us; the launch traced here: 229 us
  waiting for transfers between devices  86.8 us (38%)
  Pallas kernels  57.6 us (25%)
  starting transfers between devices  50.8 us (22%)
  local copies, waits for them, and re-layouts  30.3 us (13%)
    pallas_call x26, Pallas kernels, call(): pl.pallas_call(body, in_specs=[in_smem] * len(scalars) + [in_vmem] * len(...  57.6 us
    ppermute x17, waiting for transfers between devices, flipped(): return lax.ppermute(value, 'fsdp', [(j, j ^ bit) for j in range(sections)])  49 us
    unnamed x134, local copies, waits for them, and re-layouts  27.1 us
    all_to_all x4, starting transfers between devices, shared(): lax.all_to_all(value, 'fsdp', 0, 0, tiled=True, axis_index_groups=groups)  20.1 us
    ppermute x6, waiting for transfers between devices, across(): lax.ppermute(value, 'fsdp', [(j, (j + group) % sections) for j in range(s...  19.2 us
    ppermute x17, starting transfers between devices, flipped(): return lax.ppermute(value, 'fsdp', [(j, j ^ bit) for j in range(sections)])  13.3 us
    all_to_all x4, waiting for transfers between devices, shared(): lax.all_to_all(value, 'fsdp', 0, 0, tiled=True, axis_index_groups=groups)  10.4 us
    ppermute x6, starting transfers between devices, across(): lax.ppermute(value, 'fsdp', [(j, (j + group) % sections) for j in range(s...  8.89 us
  transfers between devices with their start and end apart: 34, of which 16 were waited for; matrix products, arithmetic and copies ran while one was open for 3% of the time, Pallas kernels for 15%

commit v1 on v0

--- a/solution.py
+++ b/solution.py
@@ -144,17 +144,14 @@
     return call(finish_kernel, [((rows, block, 2 * width), bf16)], (*kept, *got), (where,), waits, name="finish")[0]
 
 
-def stats_kernel(where_ref, x_ref, keep_ref, first_ref, second_ref):
+def stats_kernel(x_ref, keep_ref, out_ref):
     total, block, features = x_ref.shape
-    half_width = features // 2
 
     def row(column):
         return jnp.transpose(jnp.broadcast_to(column, (block, LANES)))[0:1, :]
 
     for r in range(total):
-        for part, ref in enumerate((first_ref, second_ref)):
-            lane = pl.multiple_of((where_ref[0] ^ part) * half_width, LANES)
-            ref[0, r, :block, :] = x_ref[r, :, pl.ds(lane, half_width)]
+        out_ref[r, :block, :] = x_ref[r]
         x = x_ref[r].astype(f32)
         mean = jnp.sum(x, axis=-1, keepdims=True) * (1.0 / features)
         centred = x - mean
@@ -168,27 +165,26 @@
         rows = jnp.concatenate(rows + [jnp.zeros_like(rows[0])] * (STATS - len(rows)), axis=0)
         if block < LANES:
             rows = jnp.concatenate([rows, jnp.zeros((STATS, LANES - block), f32)], axis=1)
-        first_ref[0, r, block:, :LANES] = rows.astype(bf16)
-        first_ref[0, r, block:, LANES:] = jnp.zeros((STATS, half_width - LANES), bf16)
-
-
-def stats(where, inputs, keep, waits):
+        out_ref[r, block:, :LANES] = rows.astype(bf16)
+        out_ref[r, block:, LANES:] = jnp.zeros((STATS, features - LANES), bf16)
+
+
+def stats(inputs, keep, waits):
     rows, block, features = inputs.shape
-    out_shape = [((1, rows, block + STATS, features // 2), bf16), ((1, rows, block, features // 2), bf16)]
-    return call(stats_kernel, out_shape, (inputs, keep), (where,), waits, name="stats")
-
-
-def norm_kernel(where_ref, gain_ref, shift_ref, *refs, orders):
-    block_refs, (normed_ref, stats_ref, keep_ref, *own_refs) = refs[:4], refs[4:]
-    half_width = block_refs[0].shape[-1]
-    total, block = block_refs[1].shape[1:3]
+    return call(stats_kernel, [((rows, block + STATS, features), bf16)], (inputs, keep), waits=waits, name="stats")[0]
+
+
+def norm_kernel(where_ref, gain_ref, shift_ref, *refs, count):
+    block_refs, (normed_ref, stats_ref, keep_ref, *own_refs) = refs[:count], refs[count:]
+    total, block, features = block_refs[0].shape
+    block -= STATS
+    half_width = features // 2
     per_block = BLOCK // block
 
-    def device(r, first_ref, d, second_ref, e, bits):
-        q = where_ref[3] ^ bits
+    def device(r, x_ref, q):
         at = pl.ds(pl.multiple_of(q * block, block), block)
         spaced_at = pl.ds(pl.multiple_of(q // per_block * SPACED + q % per_block * block, 8), block)
-        rows = first_ref[d, r, block:, :block].astype(f32)
+        rows = x_ref[r, block:, :block].astype(f32)
 
         def column(*of):
             row = functools.reduce(jnp.add, [rows[k : k + 1, :] for k in of])
@@ -198,45 +194,51 @@
         mean, inv = column(1, 2, 3), column(4, 5, 6)
         stats_ref[r, 0, at, :] = mean
         stats_ref[r, 1, at, :] = inv
-        for part, x_ref, at_d in ((0, first_ref, d), (1, second_ref, e)):
+        for part in range(2):
+            lane = pl.multiple_of((where_ref[0] ^ part) * half_width, LANES)
             for j in range(half_width // LANES):
-                x = x_ref[at_d, r, :block, LANES * j : LANES * (j + 1)].astype(f32)
+                x = x_ref[r, :block, pl.ds(lane + j * LANES, LANES)].astype(f32)
                 out = slice(part * half_width + j * LANES, part * half_width + (j + 1) * LANES)
                 normed_ref[r, at, out] = ((x - mean) * inv * gain_ref[:, out] + shift_ref[:, out]).astype(bf16)
-            for ref in own_refs:
-                lane = pl.ds(pl.multiple_of(where_ref[3] * LANES, LANES), LANES)
-                ref[r, where_ref[0] ^ part, at, :] = x_ref[at_d, r, :block, lane]
+        for ref in own_refs:
+            for i in range(2):
+                lane = pl.ds(pl.multiple_of(i * half_width + where_ref[3] * LANES, LANES), LANES)
+                ref[r, i, at, :] = x_ref[r, :block, lane]
 
     for r in range(total):
-        for odd in range(2):
-            for d, bits in enumerate(orders[0]):
-                e = orders[1].index(bits)
-                device(r, block_refs[2 * odd], d, block_refs[2 * odd + 1], e, bits | odd)
-
-
-def norm(where, blocks, gain, shift, orders, aligned):
-    count, rows, block, half_width = blocks[1].shape
-    tokens = 2 * count * block
+        for d, ref in enumerate(block_refs):
+            device(r, ref, where_ref[3] ^ d)
+
+
+def norm(where, blocks, gain, shift, aligned, waits):
+    rows, block, features = blocks[0].shape
+    tokens = len(blocks) * (block - STATS)
     out_shape = [
-        ((rows, tokens, 2 * half_width), bf16),
+        ((rows, tokens, features), bf16),
         ((rows, 2, tokens, LANES), f32),
         ((rows, tokens // BLOCK * SPACED, LANES), f32),
     ]
     if aligned:
         out_shape.append(((rows, 2, tokens, LANES), bf16))
-    return call(functools.partial(norm_kernel, orders=orders), out_shape, (gain, shift, *blocks), (where,), name="norm")
+    kernel = functools.partial(norm_kernel, count=len(blocks))
+    return call(kernel, out_shape, (gain, shift, *blocks), (where,), waits, name="norm")
 
 
 def weight_into(w_ref, parts):
     if len(parts) == 1:
         w_ref[...] = parts[0][...]
         return
-    row = 0
-    for own, other in zip(parts[0::2], parts[1::2]):
-        rows, columns = own.shape
-        w_ref[row : row + rows, :columns] = own[...]
-        w_ref[row : row + rows, columns:] = other[...]
-        row += rows
+    pieces = len(parts) // 2
+    group, _, columns = parts[0].shape
+    block = sum(part.shape[1] for part in parts[:pieces])
+    for rank in range(2):
+        start = 0
+        for part in parts[rank * pieces : (rank + 1) * pieces]:
+            rows = part.shape[1]
+            for q in range(group):
+                row = q * block + start
+                w_ref[row : row + rows, rank * columns : (rank + 1) * columns] = part[q]
+            start += rows
 
 
 def slot_of(where_ref, s, slots):
@@ -519,7 +521,7 @@
                 for n in range(devices):
                     hidden_ref[k * devices + n, r, :, lanes] = t["hidden"][n * block : (n + 1) * block].astype(bf16)
                 high_ref[r, i, out, :] = t["high"].astype(bf16)
-                for ref, name in zip((a_ref, b_ref, gg_ref, e_ref, omf_ref, dr_ref), "a b gg e omf dr".split()):
+                for ref, name in zip((a_ref, b_ref, gg_ref, e_ref, omf_ref, dr_ref), ("a", "b", "gg", "e", "omf", "dr")):
                     ref[i, out, :] = t[name]
                 final_ref[r, :, lanes] = t["cell"][-1:]
 
@@ -617,14 +619,16 @@
     return call(kernel, out_shape, (normed, gp, sums, *weights), waits=waits, name="weight_back")
 
 
-def norm_back_kernel(where_ref, first_ref, second_ref, stats_ref, means_ref, gp_ref, gain_ref, *refs, orders, odd, with_high):
+def norm_back_kernel(where_ref, stats_ref, means_ref, gp_ref, gain_ref, *refs, orders, odd, with_high):
+    count = len(orders[0])
+    x_refs, refs = refs[:count], refs[count:]
     *w_refs, high_ref, a_low, a_high, b_low, b_high, some_ref, gn_ref = refs
     half_count, total, block, half_width = a_low.shape
     out_refs = ((a_low, a_high), (b_low, b_high))
     features = 2 * half_width
     together = gn_ref.shape[0] // block
     for r in range(total):
-        for d in range(0, len(orders[0]), together):
+        for d in range(0, count, together):
             tokens = []
             for n in range(together):
                 place = where_ref[3] ^ (orders[0][d + n] | odd)
@@ -644,27 +648,32 @@
                 )
                 slope = inv * inv * second
                 rest = inv * first - slope * mean
-                for part, x_ref in enumerate((first_ref, second_ref)):
+                for part in range(2):
                     at_d = orders[part].index(orders[0][d + n])
+                    out_ref = out_refs[part][at_d // half_count]
+                    start = pl.multiple_of((where_ref[0] ^ part) * half_width, LANES)
+                    if with_high:
+                        high = high_ref[r, where_ref[0] ^ part, tokens[n], :].astype(f32)
                     for j in range(half_width // LANES):
                         at = slice(part * half_width + LANES * j, part * half_width + LANES * (j + 1))
-                        lanes = slice(LANES * j, LANES * (j + 1))
                         value = inv * (gn_ref[n * block : (n + 1) * block, at] * gain_ref[:, at])
-                        value -= slope * x_ref[at_d, r, :block, lanes].astype(f32) + rest
+                        x = x_refs[d + n][r, :block, pl.ds(start + LANES * j, LANES)].astype(f32)
+                        value -= slope * x + rest
                         if with_high:
-                            add = high_ref[r, where_ref[0] ^ part, tokens[n], :].astype(f32)
-                            value += jnp.where(where_ref[3] == j, add, 0.0)
-                        out_refs[part][at_d // half_count][at_d % half_count, r, :, lanes] = value.astype(bf16)
-
-
-def norm_back(where, first, second, orders, odd, stats, means, gp, weights, gain, high, with_high, waits):
-    count, rows, block, half_width = second.shape
+                            value += jnp.where(where_ref[3] == j, high, 0.0)
+                        out_ref[at_d % half_count, r, :, LANES * j : LANES * (j + 1)] = value.astype(bf16)
+
+
+def norm_back(where, blocks, orders, odd, stats, means, gp, weights, gain, high, with_high, waits):
+    count = len(blocks)
+    rows, block, features = blocks[0].shape
+    block -= STATS
     together = 2 * LANES // block
     return call(
         functools.partial(norm_back_kernel, orders=orders, odd=odd, with_high=with_high),
-        [((count // 2, *second.shape[1:]), bf16)] * 4,
-        (first, second, stats, means, gp, gain, *weights, high), (where,), waits,
-        scratch=[((together * block, gp.shape[2]), bf16), ((together * block, 2 * half_width), f32)],
+        [((count // 2, rows, block, features // 2), bf16)] * 4,
+        (stats, means, gp, gain, *blocks, *weights, high), (where,), waits,
+        scratch=[((together * block, gp.shape[2]), bf16), ((together * block, features), f32)],
         name="norm_back",
     )
 
@@ -755,40 +764,34 @@
         back = lambda v: v.reshape(group, -1, wide // piece, piece).transpose(1, 2, 0, 3).reshape(-1, wide * group)
         return jnp.concatenate([back(v) for v in pieces]).astype(dtype)
 
-    mine = shared(dealt(weight)).reshape(-1, columns)
-    early_rows = (group - 1) * row_block
-    theirs = [across(mine[:early_rows]), across(mine[early_rows:])]
-    early_rows += features // 2
-    near = list(stats(where, inputs, (1 - resets).astype(f32)[:, None, :], (mine,)))
-    for way in zip(*ways):
-        near = [jnp.concatenate([value, flipped(value, bit)]) for value, bit in zip(near, way)]
-    blocks = [*near, *(flipped(value, 1) for value in near)]
+    mine = shared(dealt(weight))
+    theirs = across(mine)
+    beside = swapped(mine) if paired else mine
+    blocks = {0: stats(inputs, (1 - resets).astype(f32)[:, None, :], (mine,))}
+    for bit in bits[::-1]:
+        blocks |= {d | bit: flipped(value, bit) for d, value in blocks.items()}
+    blocks = {d: fence(value, (theirs, beside)) for d, value in blocks.items()}
+    blocks |= {d | 1: flipped(value, 1) for d, value in blocks.items()}
+    blocks = [blocks[d] for d in range(group)]
+    early_rows = features // 2
     if paired:
-        beside = swapped(mine)
-        theirs_beside = []
-        for i in range(2):
-            theirs[i] = fence(theirs[i], (beside, *theirs_beside[-1:]))
-            theirs_beside.append(swapped(theirs[i]))
-        early, late = [mine, beside, theirs[0], theirs_beside[0]], [theirs[1], theirs_beside[1]]
+        early, late = [mine, beside], [theirs, swapped(theirs)]
     else:
-        whole = [lax.all_gather(v, "dp", axis=1, tiled=True) for v in (mine, jnp.concatenate(theirs))]
-        whole = jnp.concatenate(whole, axis=0)
-        early, late = [whole[:early_rows]], [whole[early_rows:]]
-    g_own = shared(dealt(grad_out.reshape(-1, features), (theirs[0],)).reshape(group, rows, block_len, width))
-
+        early, late = (
+            [lax.all_gather(v.reshape(-1, columns), "dp", axis=1, tiled=True)] for v in (mine, theirs)
+        )
     hfv, hrv = 0.5 * own(forget_vec), 0.5 * own(reset_vec)
     bias = jnp.concatenate([jnp.zeros((1, width), f32), own(forget_bias), own(reset_bias)]).reshape(-1, 1, LANES)
     gain_row, shift_row = halves_turned(gain)[None], halves_turned(shift)[None]
     vector_rows = [*bf16_parts(gain_row), *bf16_parts(shift_row)]
     vector_rows = jnp.pad(jnp.concatenate(vector_rows), ((0, 10), (0, 0)))
-    normed, token_stats, keep, *x_own = norm(where, blocks, gain_row, shift_row, orders, aligned)
+    g_own = shared(dealt(grad_out.reshape(-1, features)).reshape(group, rows, block_len, width))
+    normed, token_stats, keep, *x_own = norm(where, blocks, gain_row, shift_row, aligned, (g_own,))
     if aligned:
         x_own = x_own[0]
     else:
-        at = lambda part, d: blocks[2 * (d % 2) + part][orders[part].index(d & ~1)][:, :block_len]
-        by_place = jnp.stack([jnp.concatenate([at(0, d), at(1, d)], axis=-1) for d in range(group)])
-        in_order = halves_turned(by_place[place ^ jnp.arange(group)]).swapaxes(0, 1).reshape(rows * tokens, features)
-        x_own = own(in_order).reshape(rows, tokens, tiles, LANES).swapaxes(1, 2)
+        in_order = jnp.stack(blocks)[place ^ jnp.arange(group)][:, :, :block_len].swapaxes(0, 1)
+        x_own = own(in_order.reshape(rows * tokens, features)).reshape(rows, tokens, tiles, LANES).swapaxes(1, 2)
     some, some_vectors, early_weight = project(where, normed, vector_rows, early, early_rows, slots)
     p, seg, lead, end, lead_end, vectors, late_weight = blocks_forward(
         where, normed, vector_rows, some, some_vectors, bias, keep, hfv, own(initial)[:, None, :], late,
@@ -807,7 +810,7 @@
 
     def norm_part(odd, waits):
         out = norm_back(
-            where, *blocks[2 * odd : 2 * odd + 2], orders, odd, token_stats, means, gp, weights, gain_row, high_own, aligned,
+            where, [blocks[d | odd] for d in orders[0]], orders, odd, token_stats, means, gp, weights, gain_row, high_own, aligned,
             waits,
         )
         if aligned:
@@ -831,7 +834,7 @@
     kept, sent = halve(kept, got, kept[:1])
     bit_pairs = list(zip(*(w[::-1] for w in ways)))
     got = [flipped(value, bit) for value, bit in zip(sent, bit_pairs.pop(0))]
-    hidden_got = shared(fence(hidden_own, kept[:1]))
+    hidden_got = shared(hidden_own)
     if paired:
         away = [added(a, b, kept[:1]) for a, b in zip(away, away_got)]
         here_got = [swapped(fence(value, away)) for value in here[pieces:]]

time: 231 us -> 202 us (0.87)
  waiting for transfers between devices: 86.8 us -> 71.4 us
  local copies, waits for them, and re-layouts: 30.3 us -> 15.6 us
    unnamed x134 -> x98, local copies, waits for them, and re-layouts: 27.1 us -> 12.2 us
    ppermute x6 -> x5, waiting for transfers between devices: 19.2 us -> 9.48 us  [across(): lax.ppermute(value, 'fsdp', [(j, (j + group) % sections) for j in range(s...]
    ppermute x17 -> x18, waiting for transfers between devices: 49 us -> 42.6 us  [flipped(): return lax.ppermute(value, 'fsdp', [(j, j ^ bit) for j in range(sections)])]
    ppermute x6 -> x5, starting transfers between devices: 7.16 us -> 5.26 us  [swapped(): return lax.ppermute(value, 'dp', [(0, 1), (1, 0)])]
    ppermute x6 -> x5, starting transfers between devices: 8.89 us -> 10 us  [across(): lax.ppermute(value, 'fsdp', [(j, (j + group) % sections) for j in range(s...]
    ppermute x17 -> x18, starting transfers between devices: 13.3 us -> 12.8 us  [flipped(): return lax.ppermute(value, 'fsdp', [(j, j ^ bit) for j in range(sections)])]
  transfers between devices with their start and end apart: 34 -> 33, of which waited for: 16 -> 13; matrix products, arithmetic and copies ran while one was open for 3% -> 3% of each run, Pallas kernels for 15% -> 17%
where the time goes in v1:
time: 202 us; the launch traced here: 200 us
  waiting for transfers between devices  71.4 us (35%)
  Pallas kernels  58.8 us (29%)
  starting transfers between devices  50 us (25%)
  local copies, waits for them, and re-layouts  15.6 us (8%)
  other arithmetic  2.62 us (1%)
    pallas_call x26, Pallas kernels, call(): pl.pallas_call(body, in_specs=[in_smem] * len(scalars) + [in_vmem] * len(...  58.8 us
    ppermute x18, waiting for transfers between devices, flipped(): return lax.ppermute(value, 'fsdp', [(j, j ^ bit) for j in range(sections)])  42.6 us
    all_to_all x4, starting transfers between devices, shared(): lax.all_to_all(value, 'fsdp', 0, 0, tiled=True, axis_index_groups=groups)  20.6 us
    ppermute x18, starting transfers between devices, flipped(): return lax.ppermute(value, 'fsdp', [(j, j ^ bit) for j in range(sections)])  12.8 us
    unnamed x98, local copies, waits for them, and re-layouts  12.2 us
    all_to_all x4, waiting for transfers between devices, shared(): lax.all_to_all(value, 'fsdp', 0, 0, tiled=True, axis_index_groups=groups)  11.2 us
    ppermute x5, starting transfers between devices, across(): lax.ppermute(value, 'fsdp', [(j, (j + group) % sections) for j in range(s...  10 us
    ppermute x5, waiting for transfers between devices, across(): lax.ppermute(value, 'fsdp', [(j, (j + group) % sections) for j in range(s...  9.48 us
  transfers between devices with their start and end apart: 33, of which 13 were waited for; matrix products, arithmetic and copies ran while one was open for 3% of the time, Pallas kernels for 17%

profile of v1, /device:TPU:8, one launch (start us, length us, event | category | flops | bytes accessed | tf_op | source)
XLA Modules:
  0.0 199.6 jit_solution(7521476715154225776)
XLA Ops:
  2.8 4.4 %all-to-all-start = ((bf16[8,128,384]{2,1,0:T(8,128)(2,1)}), bf16[8,128,384]{2,1,0:T(8,128)(2,1)}, u32[]{:S(2)}, u32[]{:S(2)}) async-start(bf16[8,128,384]{2,1,0:T(8,128)(2,1)} %deal.2), calls=%async_computation | async-start | bytes 1572864 | tf_op jit(solution)/shard_map/all_to_all | solution.py:745
  7.2 11.2 %all-to-all-done.refs_2_.refs_3_ = bf16[8,128,384]{2,1,0:T(8,128)(2,1)} async-done(((bf16[8,128,384]{2,1,0:T(8,128)(2,1)}), bf16[8,128,384]{2,1,0:T(8,128)(2,1)}, u32[]{:S(2)}, u32[]{:S(2)}) %all-to-all-start) | async-done | bytes 786464 | tf_op jit(solution)/shard_map/all_to_all | solution.py:745
  19.4 2.9 %collective-permute-start = (bf16[8,128,384]{2,1,0:T(8,128)(2,1)}, bf16[8,128,384]{2,1,0:T(8,128)(2,1)S(1)}, u32[]{:S(2)}, u32[]{:S(2)}) collective-permute-start(bf16[8,128,384]{2,1,0:T(8,128)(2,1)} %all-to-all-done.refs_2_.refs_3_), channel_id=1, source_target_pairs={{0,8},{1,9},{2,10},{3,11},{4,12},{5,13},{6,14},{7,15},{8,0},{9,1},... | collective-permute-start | bytes 2359304 | tf_op jit(solution)/shard_map/ppermute | solution.py:736
  23.2 4.9 %all-to-all-start.1 = ((bf16[8,1,128,256]{3,2,1,0:T(8,128)(2,1)}), bf16[8,1,128,256]{3,2,1,0:T(8,128)(2,1)S(1)}, u32[]{:S(2)}, u32[]{:S(2)}) async-start(bf16[8,1,128,256]{3,2,1,0:T(8,128)(2,1)} %bitcast.9), calls=%async_computation.1 | async-start | bytes 1048576 | tf_op jit(solution)/shard_map/all_to_all | solution.py:745
  31.1 15.4 %collective-permute-done.5.refs_0_ = bf16[1,144,2048]{2,1,0:T(8,128)(2,1)} collective-permute-done((bf16[1,144,2048]{2,1,0:T(8,128)(2,1)S(1)}, bf16[1,144,2048]{2,1,0:T(8,128)(2,1)}, u32[]{:S(2)}, u32[]{:S(2)}) %collective-permute-start.5) | collective-permute-done | bytes 589856 | tf_op jit(solution)/shard_map/ppermute | solution.py:739
  48.8 7.0 %collective-permute-done.refs_1_.refs_9_ = bf16[8,128,384]{2,1,0:T(8,128)(2,1)S(1)} collective-permute-done((bf16[8,128,384]{2,1,0:T(8,128)(2,1)}, bf16[8,128,384]{2,1,0:T(8,128)(2,1)S(1)}, u32[]{:S(2)}, u32[]{:S(2)}) %collective-permute-start) | collective-permute-done | bytes 786464 | tf_op jit(solution)/shard_map/ppermute | solution.py:736
  59.5 2.7 %collective-permute-done.7.refs_0_ = bf16[1,144,2048]{2,1,0:T(8,128)(2,1)} collective-permute-done((bf16[1,144,2048]{2,1,0:T(8,128)(2,1)}, bf16[1,144,2048]{2,1,0:T(8,128)(2,1)}, u32[]{:S(2)}, u32[]{:S(2)}) %collective-permute-start.7) | collective-permute-done | bytes 589856 | tf_op jit(solution)/shard_map/ppermute | solution.py:739
  65.5 4.7 %norm.1 = (bf16[1,1024,2048]{2,1,0:T(8,128)(2,1)S(1)}, f32[1,2,1024,128]{3,2,1,0:T(8,128)S(1)}, f32[1,1088,128]{2,1,0:T(8,128)S(1)}, bf16[1,2,1024,128]{3,2,1,0:T(8,128)(2,1)S(1)}) custom-call(s32[5]{0:T(128)S(1)} %stack.23.refs_0_, f32[1,2048]{1,0:T(1,128)S(1)} %bitcast.46, f32[1,2048]{1,0:T(1,128)S(1)} %bitcast.50, bf16[1,144,2048]{2,1,0:T(8,128)(2,1)S(1)} %copy-done.10, ...), custom_call_target="tpu_custom_call" | custom-call | tf_op jit(solution)/shard_map/norm/pallas_call | solution.py:41
  71.0 4.5 %project.1 = (f32[1,6,1024,128]{3,2,1,0:T(8,128)S(1)}, f32[16,768]{1,0:T(8,128)S(1)}, bf16[1024,768]{1,0:T(8,128)(2,1)S(1)}) custom-call(s32[5]{0:T(128)S(1)} %copy-done.41, bf16[1,1024,2048]{2,1,0:T(8,128)(2,1)S(1)} %get-tuple-element.54.refs_1_.refs_0_, bf16[16,2048]{1,0:T(8,128)(2,1)S(1)} %copy-done.34, ...), custom_call_target="tpu_custom_call" | custom-call | tf_op jit(solution)/shard_map/project/pallas_call | solution.py:41
  75.5 7.9 %blocks_forward.1 = (f32[1,6,1088,128]{3,2,1,0:T(8,128)S(1)}, f32[1,2,1088,128]{3,2,1,0:T(8,128)S(1)}, f32[1,2,336,128]{3,2,1,0:T(8,128)S(1)}, f32[1,1,256]{2,1,...) custom-call(s32[5]{0:T(128)S(1)} %copy-done.41, ...), custom_call_target="tpu_custom_call" | custom-call | tf_op jit(solution)/shard_map/blocks_forward/pallas_call | solution.py:41
  85.9 2.1 %collective-permute-done.10.refs_7_ = f32[1,1,256]{2,1,0:T(1,128)S(1)} collective-permute-done((f32[1,1,256]{2,1,0:T(1,128)S(1)}, f32[1,1,256]{2,1,0:T(1,128)S(1)}, u32[]{:S(2)}, u32[]{:S(2)}) %collective-permute-start.10) | collective-permute-done | bytes 1056 | tf_op jit(solution)/shard_map/ppermute | solution.py:736
  88.0 2.7 %entry.1 = (f32[1,2,200,128]{3,2,1,0:T(8,128)S(1)}, f32[1,1,256]{2,1,0:T(1,128)S(1)}) custom-call(f32[1,6,1088,128]{3,2,1,0:T(8,128)S(1)} %get-tuple-element.58.refs_0_.refs_1_, f32[1,1088,128]{2,1,0:T(8,128)S(1)} %get-tuple-element.57.refs_6_.refs_1_.refs_2_, f32[1,2,1088,128]{3,2,1,0:T(8,128)S(1)} %get-tuple-element.59.refs_2_.refs_3_, ...), custom_call_target="tpu_custom_call" | custom-call | tf_op jit(solution)/shard_map/entry/pallas_call | solution.py:41
  92.4 4.1 %lead_forward.1.refs_4_ = f32[1,2,816,128]{3,2,1,0:T(8,128)S(1)} custom-call(f32[1,6,1088,128]{3,2,1,0:T(8,128)S(1)} %get-tuple-element.58.refs_0_.refs_1_, f32[1,1088,128]{2,1,0:T(8,128)S(1)} %get-tuple-element.57.refs_6_.refs_1_.refs_2_, f32[1,256]{1,0:T(1,128)S(1)} %copy-done.43, f32[1,1,256]{2,1,0:T(1,128)S(1)} %get-tuple-element.60.refs_3_, ...), custom_call_target="tpu_custom_call" | custom-call | tf_op jit(solution)/shard_map/lead_forward/pallas_call | solution.py:41
  96.5 6.4 %backward.1 = (bf16[1,1024,768]{2,1,0:T(8,128)(2,1)S(1)}, bf16[8,1,128,256]{3,2,1,0:T(8,128)(2,1)S(1)}, bf16[1,2,1024,128]{3,2,1,0:T(8,128)(2,1)S(1)}, f32[8,768...) custom-call(s32[5]{0:T(128)S(1)} %copy-done.41, ...), custom_call_target="tpu_custom_call" | custom-call | tf_op jit(solution)/shard_map/backward/pallas_call | solution.py:41
  102.9 3.1 %weight_back.2 = (f32[2,1024]{1,0:T(2,128)S(1)}, bf16[8,128,384]{2,1,0:T(8,128)(2,1)S(1)}, bf16[8,128,384]{2,1,0:T(8,128)(2,1)}) custom-call(bf16[1,1024,2048]{2,1,0:T(8,128)(2,1)S(1)} %get-tuple-element.54.refs_1_.refs_0_, bf16[1,1024,768]{2,1,0:T(8,128)(2,1)S(1)} %get-tuple-element.70.refs_1_.refs_3_, f32[8,768]{1,0:T(8,128)S(1)} %get-tuple-element.74.refs_2_.refs_1_, ...), custom_call_target="tpu_custom_call" | custom-call | tf_op jit(solution)/shard_map/weight_back/pallas_call | solution.py:41
  108.5 4.9 %norm_back.2 = (bf16[2,1,128,1024]{3,2,1,0:T(8,128)(2,1)}, bf16[2,1,128,1024]{3,2,1,0:T(8,128)(2,1)}, bf16[2,1,128,1024]{3,2,1,0:T(8,128)(2,1)}, bf16[2,1,128,1024]{3,2,1,0:T(8,128)(2,1)}) custom-call(s32[5]{0:T(128)S(1)} %copy-done.41, f32[1,2,1024,128]{3,2,1,0:T(8,128)S(1)} %get-tuple-element.68.refs_1_, ...), custom_call_target="tpu_custom_call" | custom-call | tf_op jit(solution)/shard_map/norm_back/pallas_call | solution.py:41
  114.5 5.4 %all-to-all-start.2 = ((bf16[8,1,128,256]{3,2,1,0:T(8,128)(2,1)}), bf16[8,1,128,256]{3,2,1,0:T(8,128)(2,1)}, u32[]{:S(2)}, u32[]{:S(2)}) async-start(bf16[8,1,128,256]{3,2,1,0:T(8,128)(2,1)} %copy-done.36), calls=%async_computation.2 | async-start | bytes 1048576 | tf_op jit(solution)/shard_map/all_to_all | solution.py:745
  119.8 2.2 %copy-done.2 = bf16[1,1024,2048]{2,1,0:T(8,128)(2,1)S(1)} copy-done((bf16[1,1024,2048]{2,1,0:T(8,128)(2,1)S(1)}, bf16[1,1024,2048]{2,1,0:T(8,128)(2,1)}, u32[]{:S(2)}) %copy-start.2) | copy-done | bytes 4194328
  123.5 2.2 %weight_back.3 = (f32[2,1024]{1,0:T(2,128)S(1)}, bf16[8,128,384]{2,1,0:T(8,128)(2,1)S(1)}, bf16[8,128,384]{2,1,0:T(8,128)(2,1)S(1)}) custom-call(bf16[1,1024,2048]{2,1,0:T(8,128)(2,1)S(1)} %copy-done.2, bf16[1,1024,768]{2,1,0:T(8,128)(2,1)S(1)} %copy-done.4, f32[8,768]{1,0:T(8,128)S(1)} %get-tuple-element.74.refs_2_.refs_1_, ...), custom_call_target="tpu_custom_call" | custom-call | tf_op jit(solution)/shard_map/weight_back/pallas_call | solution.py:41
  126.5 4.1 %norm_back.3 = (bf16[2,1,128,1024]{3,2,1,0:T(8,128)(2,1)S(1)}, bf16[2,1,128,1024]{3,2,1,0:T(8,128)(2,1)S(1)}, bf16[2,1,128,1024]{3,2,1,0:T(8,128)(2,1)S(1)}, bf16[2,1,128,1024]{3,2,1,0:T(8,128)(2,1)S(1)}) custom-call(s32[5]{0:T(128)S(1)} %copy-done.42, f32[1,2,1024,128]{3,2,1,0:T(8,128)S(1)} %copy-done.15, f32[1,2,1024,128]{3,2,1,0:T(8,128)S(1)} %copy-done.17, ...), custom_call_target="tpu_custom_call" | custom-call | tf_op jit(solution)/shard_map/norm_back/pallas_call | solution.py:41
  130.7 2.7 %halve.2 = (bf16[2,1,128,1024]{3,2,1,0:T(8,128)(2,1)S(1)}, bf16[2,1,128,1024]{3,2,1,0:T(8,128)(2,1)}, bf16[2,1,128,1024]{3,2,1,0:T(8,128)(2,1)S(1)}, bf16[2,1,128,1024]{3,2,1,0:T(8,128)(2,1)}) custom-call(bf16[2,1,128,1024]{3,2,1,0:T(8,128)(2,1)S(1)} %get-tuple-element.78.refs_0_.refs_8_, bf16[2,1,128,1024]{3,2,1,0:T(8,128)(2,1)S(1)} %get-tuple-element.79.refs_1_, ...), custom_call_target="tpu_custom_call" | custom-call | tf_op jit(solution)/shard_map/halve/pallas_call | solution.py:41
  138.7 2.5 %collective-permute-start.23 = (bf16[8,128,384]{2,1,0:T(8,128)(2,1)S(1)}, bf16[8,128,384]{2,1,0:T(8,128)(2,1)S(1)}, u32[]{:S(2)}, u32[]{:S(2)}) collective-permute-start(bf16[8,128,384]{2,1,0:T(8,128)(2,1)S(1)} %copy-done.19), channel_id=1, source_target_pairs={{0,8},{1,9},{2,10},{3,11},{4,12},{5,13},{6,14},{7,15},{8,0},{9,1},... | collective-permute-start | bytes 2359304 | tf_op jit(solution)/shard_map/ppermute | solution.py:736
  141.2 2.0 collect.2
  143.2 4.4 %collective-permute-done.16.refs_2_ = bf16[2,1,128,1024]{3,2,1,0:T(8,128)(2,1)} collective-permute-done((bf16[2,1,128,1024]{3,2,1,0:T(8,128)(2,1)}, bf16[2,1,128,1024]{3,2,1,0:T(8,128)(2,1)}, u32[]{:S(2)}, u32[]{:S(2)}) %collective-permute-start.16) | collective-permute-done | bytes 524320 | tf_op jit(solution)/shard_map/ppermute | solution.py:739
  147.7 7.2 %collective-permute-done.17.refs_3_ = bf16[2,1,128,1024]{3,2,1,0:T(8,128)(2,1)} collective-permute-done((bf16[2,1,128,1024]{3,2,1,0:T(8,128)(2,1)}, bf16[2,1,128,1024]{3,2,1,0:T(8,128)(2,1)}, u32[]{:S(2)}, u32[]{:S(2)}) %collective-permute-start.17) | collective-permute-done | bytes 524320 | tf_op jit(solution)/shard_map/ppermute | solution.py:739
  157.4 2.5 %collective-permute-start.18 = (bf16[1,1,128,1024]{3,2,1,0:T(8,128)(2,1)S(1)}, bf16[1,1,128,1024]{3,2,1,0:T(8,128)(2,1)S(1)}, u32[]{:S(2)}, u32[]{:S(2)}) collective-permute-start(bf16[1,1,128,1024]{3,2,1,0:T(8,128)(2,1)S(1)} %get-tuple-element.91), channel_id=1, source_target_pairs={{0,4},{1,5},{2,6},{3,7},{4,0},{5,1},{6,2},{7,3},{8,12},{9,13},{10,... | collective-permute-start | bytes 786440 | tf_op jit(solution)/shard_map/ppermute | solution.py:739
  162.0 1.9 collective-permute-start.25
  163.9 4.3 %collective-permute-done.25.refs_1_ = f32[8,2048]{1,0:T(8,128)S(1)} collective-permute-done((f32[8,2048]{1,0:T(8,128)S(1)}, f32[8,2048]{1,0:T(8,128)S(1)}, u32[]{:S(2)}, u32[]{:S(2)}) %collective-permute-start.25) | collective-permute-done | bytes 65568 | tf_op jit(solution)/shard_map/ppermute | solution.py:739
  168.7 7.3 %collective-permute-done.26.refs_1_ = f32[8,2048]{1,0:T(8,128)S(1)} collective-permute-done((f32[8,2048]{1,0:T(8,128)S(1)}, f32[8,2048]{1,0:T(8,128)S(1)}, u32[]{:S(2)}, u32[]{:S(2)}) %collective-permute-start.26) | collective-permute-done | bytes 65568 | tf_op jit(solution)/shard_map/ppermute | solution.py:739
  179.7 6.0 %all-to-all-start.3 = ((bf16[8,128,384]{2,1,0:T(8,128)(2,1)}), bf16[8,128,384]{2,1,0:T(8,128)(2,1)S(1)}, u32[]{:S(2)}, u32[]{:S(2)}) async-start(bf16[8,128,384]{2,1,0:T(8,128)(2,1)} %merge.1), calls=%async_computation.3 | async-start | bytes 1572864 | tf_op jit(solution)/shard_map/all_to_all | solution.py:745
  187.5 2.5 %collective-permute-done.27.refs_1_ = f32[8,2048]{1,0:T(8,128)S(1)} collective-permute-done((f32[8,2048]{1,0:T(8,128)S(1)}, f32[8,2048]{1,0:T(8,128)S(1)}, u32[]{:S(2)}, u32[]{:S(2)}) %collective-permute-start.27) | collective-permute-done | bytes 65568 | tf_op jit(solution)/shard_map/ppermute | solution.py:742
  191.1 5.6 %collective-permute-done.20 = f32[1,128]{1,0:T(1,128)S(1)} collective-permute-done((f32[1,128]{1,0:T(1,128)S(1)}, f32[1,128]{1,0:T(1,128)S(1)}, u32[]{:S(2)}, u32[]{:S(2)}) %collective-permute-start.20) | collective-permute-done | bytes 544 | tf_op jit(solution)/shard_map/ppermute | solution.py:875
  (183 shorter events, 46.7 us)
Async XLA Ops:
  2.8 15.6 %all-to-all-start = ((bf16[8,128,384]{2,1,0:T(8,128)(2,1)}), bf16[8,128,384]{2,1,0:T(8,128)(2,1)}, u32[]{:S(2)}, u32[]{:S(2)}) async-start(bf16[8,128,384]{2,1,0:T(8,128)(2,1)} %deal.2), calls=%async_computation | async-start | bytes 1572864 | tf_op jit(solution)/shard_map/all_to_all | solution.py:745
  18.7 27.7 %collective-permute-start.5 = (bf16[1,144,2048]{2,1,0:T(8,128)(2,1)S(1)}, bf16[1,144,2048]{2,1,0:T(8,128)(2,1)}, u32[]{:S(2)}, u32[]{:S(2)}) collective-permute-start(bf16[1,144,2048]{2,1,0:T(8,128)(2,1)S(1)} %stats.1.refs_0_), channel_id=1, source_target_pairs={{0,4},{1,5},{2,6},{3,7},{4,0},{5,1},{6,2},{7,3},{8,12},{9,13},{10,... | collective-permute-start | bytes 1769480 | tf_op jit(solution)/shard_map/ppermute | solution.py:739
  19.4 36.5 %collective-permute-start = (bf16[8,128,384]{2,1,0:T(8,128)(2,1)}, bf16[8,128,384]{2,1,0:T(8,128)(2,1)S(1)}, u32[]{:S(2)}, u32[]{:S(2)}) collective-permute-start(bf16[8,128,384]{2,1,0:T(8,128)(2,1)} %all-to-all-done.refs_2_.refs_3_), channel_id=1, source_target_pairs={{0,8},{1,9},{2,10},{3,11},{4,12},{5,13},{6,14},{7,15},{8,0},{9,1},... | collective-permute-start | bytes 2359304 | tf_op jit(solution)/shard_map/ppermute | solution.py:736
  23.2 42.2 %all-to-all-start.1 = ((bf16[8,1,128,256]{3,2,1,0:T(8,128)(2,1)}), bf16[8,1,128,256]{3,2,1,0:T(8,128)(2,1)S(1)}, u32[]{:S(2)}, u32[]{:S(2)}) async-start(bf16[8,1,128,256]{3,2,1,0:T(8,128)(2,1)} %bitcast.9), calls=%async_computation.1 | async-start | bytes 1048576 | tf_op jit(solution)/shard_map/all_to_all | solution.py:745
  28.1 29.9 %collective-permute-start.3 = (bf16[1,144,2048]{2,1,0:T(8,128)(2,1)S(1)}, bf16[1,144,2048]{2,1,0:T(8,128)(2,1)}, u32[]{:S(2)}, u32[]{:S(2)}) collective-permute-start(bf16[1,144,2048]{2,1,0:T(8,128)(2,1)S(1)} %stats.1.refs_0_), channel_id=1, source_target_pairs={{0,2},{1,3},{2,0},{3,1},{4,6},{5,7},{6,4},{7,5},{8,10},{9,11},{10,... | collective-permute-start | bytes 1769480 | tf_op jit(solution)/shard_map/ppermute | solution.py:739
  29.6 28.5 %collective-permute-start.1 = (bf16[8,128,384]{2,1,0:T(8,128)(2,1)}, bf16[8,128,384]{2,1,0:T(8,128)(2,1)S(1)}, u32[]{:S(2)}, u32[]{:S(2)}) collective-permute-start(bf16[8,128,384]{2,1,0:T(8,128)(2,1)} %all-to-all-done.refs_2_.refs_3_), channel_id=1, source_target_pairs={{0,16},{16,0},{1,17},{17,1},{2,18},{18,2},{3,19},{19,3},{4,20},{20... | collective-permute-start | bytes 2359304 | tf_op jit(solution)/shard_map/ppermute | solution.py:742
  46.5 15.7 %collective-permute-start.7 = (bf16[1,144,2048]{2,1,0:T(8,128)(2,1)}, bf16[1,144,2048]{2,1,0:T(8,128)(2,1)}, u32[]{:S(2)}, u32[]{:S(2)}) collective-permute-start(bf16[1,144,2048]{2,1,0:T(8,128)(2,1)} %collective-permute-done.5.refs_0_), channel_id=1, source_target_pairs={{0,2},{1,3},{2,0},{3,1},{4,6},{5,7},{6,4},{7,5},{8,10},{9,11},{10,... | collective-permute-start | bytes 1769480 | tf_op jit(solution)/shard_map/ppermute | solution.py:739
  55.8 19.6 %collective-permute-start.9 = (bf16[8,128,384]{2,1,0:T(8,128)(2,1)S(1)}, bf16[8,128,384]{2,1,0:T(8,128)(2,1)}, u32[]{:S(2)}, u32[]{:S(2)}) collective-permute-start(bf16[8,128,384]{2,1,0:T(8,128)(2,1)S(1)} %collective-permute-done.refs_1_.refs_9_), channel_id=1, source_target_pairs={{0,16},{16,0},{1,17},{17,1},{2,18},{18,2},{3,19},{19,3},{4,20},{20... | collective-permute-start | bytes 2359304 | tf_op jit(solution)/shard_map/ppermute | solution.py:742
  59.0 6.4 %collective-permute-start.4 = (bf16[1,144,2048]{2,1,0:T(8,128)(2,1)}, bf16[1,144,2048]{2,1,0:T(8,128)(2,1)S(1)}, u32[]{:S(2)}, u32[]{:S(2)}) collective-permute-start(bf16[1,144,2048]{2,1,0:T(8,128)(2,1)} %fence.6.refs_5_.refs_7_), channel_id=1, source_target_pairs={{0,1},{1,0},{2,3},{3,2},{4,5},{5,4},{6,7},{7,6},{8,9},{9,8},{10,11... | collective-permute-start | bytes 1769480 | tf_op jit(solution)/shard_map/ppermute | solution.py:739
  59.0 6.4 %collective-permute-start.2 = (bf16[1,144,2048]{2,1,0:T(8,128)(2,1)}, bf16[1,144,2048]{2,1,0:T(8,128)(2,1)S(1)}, u32[]{:S(2)}, u32[]{:S(2)}) collective-permute-start(bf16[1,144,2048]{2,1,0:T(8,128)(2,1)} %fence.5.refs_3_.refs_5_), channel_id=1, source_target_pairs={{0,1},{1,0},{2,3},{3,2},{4,5},{5,4},{6,7},{7,6},{8,9},{9,8},{10,11... | collective-permute-start | bytes 1769480 | tf_op jit(solution)/shard_map/ppermute | solution.py:739
  62.2 3.3 %collective-permute-start.8 = (bf16[1,144,2048]{2,1,0:T(8,128)(2,1)}, bf16[1,144,2048]{2,1,0:T(8,128)(2,1)}, u32[]{:S(2)}, u32[]{:S(2)}) collective-permute-start(bf16[1,144,2048]{2,1,0:T(8,128)(2,1)} %fence.8.refs_9_.refs_8_), channel_id=1, source_target_pairs={{0,1},{1,0},{2,3},{3,2},{4,5},{5,4},{6,7},{7,6},{8,9},{9,8},{10,11... | collective-permute-start | bytes 1769480 | tf_op jit(solution)/shard_map/ppermute | solution.py:739
  62.2 3.3 %collective-permute-start.6 = (bf16[1,144,2048]{2,1,0:T(8,128)(2,1)}, bf16[1,144,2048]{2,1,0:T(8,128)(2,1)}, u32[]{:S(2)}, u32[]{:S(2)}) collective-permute-start(bf16[1,144,2048]{2,1,0:T(8,128)(2,1)} %fence.7.refs_7_.refs_6_), channel_id=1, source_target_pairs={{0,1},{1,0},{2,3},{3,2},{4,5},{5,4},{6,7},{7,6},{8,9},{9,8},{10,11... | collective-permute-start | bytes 1769480 | tf_op jit(solution)/shard_map/ppermute | solution.py:739
  83.5 4.5 %collective-permute-start.10 = (f32[1,1,256]{2,1,0:T(1,128)S(1)}, f32[1,1,256]{2,1,0:T(1,128)S(1)}, u32[]{:S(2)}, u32[]{:S(2)}) collective-permute-start(f32[1,1,256]{2,1,0:T(1,128)S(1)} %get-tuple-element.63), channel_id=1, source_target_pairs={{0,8},{1,9},{2,10},{3,11},{4,12},{5,13},{6,14},{7,15},{8,0},{9,1},... | collective-permute-start | bytes 3080 | tf_op jit(solution)/shard_map/ppermute | solution.py:736
  90.7 5.8 %collective-permute-start.11 = (f32[1,1,256]{2,1,0:T(1,128)S(1)}, f32[1,1,256]{2,1,0:T(1,128)S(1)}, u32[]{:S(2)}, u32[]{:S(2)}) collective-permute-start(f32[1,1,256]{2,1,0:T(1,128)S(1)} %get-tuple-element.65), channel_id=1, source_target_pairs={{0,8},{1,9},{2,10},{3,11},{4,12},{5,13},{6,14},{7,15},{8,0},{9,1},... | collective-permute-start | bytes 3080 | tf_op jit(solution)/shard_map/ppermute | solution.py:736
  107.0 28.4 %collective-permute-start.21 = (bf16[8,128,384]{2,1,0:T(8,128)(2,1)}, bf16[8,128,384]{2,1,0:T(8,128)(2,1)}, u32[]{:S(2)}, u32[]{:S(2)}) collective-permute-start(bf16[8,128,384]{2,1,0:T(8,128)(2,1)} %get-tuple-element.97), channel_id=1, source_target_pairs={{0,16},{16,0},{1,17},{17,1},{2,18},{18,2},{3,19},{19,3},{4,20},{20... | collective-permute-start | bytes 2359304 | tf_op jit(solution)/shard_map/ppermute | solution.py:742
  113.4 17.2 %collective-permute-start.12 = (bf16[2,1,128,1024]{3,2,1,0:T(8,128)(2,1)}, bf16[2,1,128,1024]{3,2,1,0:T(8,128)(2,1)}, u32[]{:S(2)}, u32[]{:S(2)}) collective-permute-start(bf16[2,1,128,1024]{3,2,1,0:T(8,128)(2,1)} %get-tuple-element.76.refs_5_), channel_id=1, source_target_pairs={{0,1},{1,0},{2,3},{3,2},{4,5},{5,4},{6,7},{7,6},{8,9},{9,8},{10,11... | collective-permute-start | bytes 1572872 | tf_op jit(solution)/shard_map/ppermute | solution.py:739
  113.5 17.2 %collective-permute-start.13 = (bf16[2,1,128,1024]{3,2,1,0:T(8,128)(2,1)}, bf16[2,1,128,1024]{3,2,1,0:T(8,128)(2,1)}, u32[]{:S(2)}, u32[]{:S(2)}) collective-permute-start(bf16[2,1,128,1024]{3,2,1,0:T(8,128)(2,1)} %get-tuple-element.82), channel_id=1, source_target_pairs={{0,1},{1,0},{2,3},{3,2},{4,5},{5,4},{6,7},{7,6},{8,9},{9,8},{10,11... | collective-permute-start | bytes 1572872 | tf_op jit(solution)/shard_map/ppermute | solution.py:739
  114.0 16.7 %collective-permute-start.14 = (bf16[2,1,128,1024]{3,2,1,0:T(8,128)(2,1)}, bf16[2,1,128,1024]{3,2,1,0:T(8,128)(2,1)}, u32[]{:S(2)}, u32[]{:S(2)}) collective-permute-start(bf16[2,1,128,1024]{3,2,1,0:T(8,128)(2,1)} %get-tuple-element.83), channel_id=1, source_target_pairs={{0,1},{1,0},{2,3},{3,2},{4,5},{5,4},{6,7},{7,6},{8,9},{9,8},{10,11... | collective-permute-start | bytes 1572872 | tf_op jit(solution)/shard_map/ppermute | solution.py:739
  114.0 16.6 %collective-permute-start.15 = (bf16[2,1,128,1024]{3,2,1,0:T(8,128)(2,1)}, bf16[2,1,128,1024]{3,2,1,0:T(8,128)(2,1)}, u32[]{:S(2)}, u32[]{:S(2)}) collective-permute-start(bf16[2,1,128,1024]{3,2,1,0:T(8,128)(2,1)} %get-tuple-element.84), channel_id=1, source_target_pairs={{0,1},{1,0},{2,3},{3,2},{4,5},{5,4},{6,7},{7,6},{8,9},{9,8},{10,11... | collective-permute-start | bytes 1572872 | tf_op jit(solution)/shard_map/ppermute | solution.py:739
  114.5 26.8 %all-to-all-start.2 = ((bf16[8,1,128,256]{3,2,1,0:T(8,128)(2,1)}), bf16[8,1,128,256]{3,2,1,0:T(8,128)(2,1)}, u32[]{:S(2)}, u32[]{:S(2)}) async-start(bf16[8,1,128,256]{3,2,1,0:T(8,128)(2,1)} %copy-done.36), calls=%async_computation.2 | async-start | bytes 1048576 | tf_op jit(solution)/shard_map/all_to_all | solution.py:745
  133.4 14.3 %collective-permute-start.16 = (bf16[2,1,128,1024]{3,2,1,0:T(8,128)(2,1)}, bf16[2,1,128,1024]{3,2,1,0:T(8,128)(2,1)}, u32[]{:S(2)}, u32[]{:S(2)}) collective-permute-start(bf16[2,1,128,1024]{3,2,1,0:T(8,128)(2,1)} %get-tuple-element.87), channel_id=1, source_target_pairs={{0,2},{1,3},{2,0},{3,1},{4,6},{5,7},{6,4},{7,5},{8,10},{9,11},{10,... | collective-permute-start | bytes 1572872 | tf_op jit(solution)/shard_map/ppermute | solution.py:739
  134.8 20.0 %collective-permute-start.17 = (bf16[2,1,128,1024]{3,2,1,0:T(8,128)(2,1)}, bf16[2,1,128,1024]{3,2,1,0:T(8,128)(2,1)}, u32[]{:S(2)}, u32[]{:S(2)}) collective-permute-start(bf16[2,1,128,1024]{3,2,1,0:T(8,128)(2,1)} %get-tuple-element.88), channel_id=1, source_target_pairs={{0,4},{1,5},{2,6},{3,7},{4,0},{5,1},{6,2},{7,3},{8,12},{9,13},{10,... | collective-permute-start | bytes 1572872 | tf_op jit(solution)/shard_map/ppermute | solution.py:739
  137.6 39.9 %collective-permute-start.22 = (bf16[8,128,384]{2,1,0:T(8,128)(2,1)}, bf16[8,128,384]{2,1,0:T(8,128)(2,1)S(1)}, u32[]{:S(2)}, u32[]{:S(2)}) collective-permute-start(bf16[8,128,384]{2,1,0:T(8,128)(2,1)} %fence.9), channel_id=1, source_target_pairs={{0,16},{16,0},{1,17},{17,1},{2,18},{18,2},{3,19},{19,3},{4,20},{20... | collective-permute-start | bytes 2359304 | tf_op jit(solution)/shard_map/ppermute | solution.py:742
  138.7 38.7 %collective-permute-start.23 = (bf16[8,128,384]{2,1,0:T(8,128)(2,1)S(1)}, bf16[8,128,384]{2,1,0:T(8,128)(2,1)S(1)}, u32[]{:S(2)}, u32[]{:S(2)}) collective-permute-start(bf16[8,128,384]{2,1,0:T(8,128)(2,1)S(1)} %copy-done.19), channel_id=1, source_target_pairs={{0,8},{1,9},{2,10},{3,11},{4,12},{5,13},{6,14},{7,15},{8,0},{9,1},... | collective-permute-start | bytes 2359304 | tf_op jit(solution)/shard_map/ppermute | solution.py:736
  157.4 18.6 %collective-permute-start.18 = (bf16[1,1,128,1024]{3,2,1,0:T(8,128)(2,1)S(1)}, bf16[1,1,128,1024]{3,2,1,0:T(8,128)(2,1)S(1)}, u32[]{:S(2)}, u32[]{:S(2)}) collective-permute-start(bf16[1,1,128,1024]{3,2,1,0:T(8,128)(2,1)S(1)} %get-tuple-element.91), channel_id=1, source_target_pairs={{0,4},{1,5},{2,6},{3,7},{4,0},{5,1},{6,2},{7,3},{8,12},{9,13},{10,... | collective-permute-start | bytes 786440 | tf_op jit(solution)/shard_map/ppermute | solution.py:739
  159.9 16.1 %collective-permute-start.19 = (bf16[1,1,128,1024]{3,2,1,0:T(8,128)(2,1)S(1)}, bf16[1,1,128,1024]{3,2,1,0:T(8,128)(2,1)S(1)}, u32[]{:S(2)}, u32[]{:S(2)}) collective-permute-start(bf16[1,1,128,1024]{3,2,1,0:T(8,128)(2,1)S(1)} %get-tuple-element.92), channel_id=1, source_target_pairs={{0,2},{1,3},{2,0},{3,1},{4,6},{5,7},{6,4},{7,5},{8,10},{9,11},{10,... | collective-permute-start | bytes 786440 | tf_op jit(solution)/shard_map/ppermute | solution.py:739
  162.0 6.3 %collective-permute-start.25 = (f32[8,2048]{1,0:T(8,128)S(1)}, f32[8,2048]{1,0:T(8,128)S(1)}, u32[]{:S(2)}, u32[]{:S(2)}) collective-permute-start(f32[8,2048]{1,0:T(8,128)S(1)} %added.7.refs_0_), channel_id=1, source_target_pairs={{0,2},{1,3},{2,0},{3,1},{4,6},{5,7},{6,4},{7,5},{8,10},{9,11},{10,... | collective-permute-start | bytes 196616 | tf_op jit(solution)/shard_map/ppermute | solution.py:739
  168.3 7.7 %collective-permute-start.26 = (f32[8,2048]{1,0:T(8,128)S(1)}, f32[8,2048]{1,0:T(8,128)S(1)}, u32[]{:S(2)}, u32[]{:S(2)}) collective-permute-start(f32[8,2048]{1,0:T(8,128)S(1)} %added.8.refs_0_), channel_id=1, source_target_pairs={{0,4},{1,5},{2,6},{3,7},{4,0},{5,1},{6,2},{7,3},{8,12},{9,13},{10,... | collective-permute-start | bytes 196616 | tf_op jit(solution)/shard_map/ppermute | solution.py:739
  179.7 18.5 %all-to-all-start.3 = ((bf16[8,128,384]{2,1,0:T(8,128)(2,1)}), bf16[8,128,384]{2,1,0:T(8,128)(2,1)S(1)}, u32[]{:S(2)}, u32[]{:S(2)}) async-start(bf16[8,128,384]{2,1,0:T(8,128)(2,1)} %merge.1), calls=%async_computation.3 | async-start | bytes 1572864 | tf_op jit(solution)/shard_map/all_to_all | solution.py:745
  185.7 4.3 %collective-permute-start.27 = (f32[8,2048]{1,0:T(8,128)S(1)}, f32[8,2048]{1,0:T(8,128)S(1)}, u32[]{:S(2)}, u32[]{:S(2)}) collective-permute-start(f32[8,2048]{1,0:T(8,128)S(1)} %added.9.refs_4_.refs_0_), channel_id=1, source_target_pairs={{0,16},{16,0},{1,17},{17,1},{2,18},{18,2},{3,19},{19,3},{4,20},{20... | collective-permute-start | bytes 196616 | tf_op jit(solution)/shard_map/ppermute | solution.py:742
  186.2 10.6 %collective-permute-start.20 = (f32[1,128]{1,0:T(1,128)S(1)}, f32[1,128]{1,0:T(1,128)S(1)}, u32[]{:S(2)}, u32[]{:S(2)}) collective-permute-start(f32[1,128]{1,0:T(1,128)S(1)} %slice.48), channel_id=1, source_target_pairs={{8,0},{9,1},{10,2},{11,3},{12,4},{13,5},{14,6},{15,7},{24,16},{25,... | collective-permute-start | bytes 1544 | tf_op jit(solution)/shard_map/ppermute | solution.py:875
  190.0 7.6 %collective-permute-start.28 = (f32[8,2048]{1,0:T(8,128)S(1)}, f32[8,2048]{1,0:T(8,128)S(1)}, u32[]{:S(2)}, u32[]{:S(2)}) collective-permute-start(f32[8,2048]{1,0:T(8,128)S(1)} %added.10.refs_0_), channel_id=1, source_target_pairs={{0,8},{1,9},{2,10},{3,11},{4,12},{5,13},{6,14},{7,15},{8,0},{9,1},... | collective-permute-start | bytes 196616 | tf_op jit(solution)/shard_map/ppermute | solution.py:736
  (50 other events, 485.4 us)

commit v2 on v1

--- a/solution.py
+++ b/solution.py
@@ -121,13 +121,18 @@
     return out[0::2], out[1::2]
 
 
-def merge_kernel(own_ref, got_ref, away_ref, out_ref):
-    value = own_ref[...].astype(f32) + got_ref[...].astype(f32) + away_ref[...].astype(f32)
-    out_ref[...] = value.astype(bf16)
+def merge_kernel(own_ref, away_ref, *refs):
+    *got_refs, out_ref = refs
+    start = 0
+    for ref in got_refs:
+        rows = slice(start, start + ref.shape[1])
+        value = own_ref[:, rows, :].astype(f32) + ref[...].astype(f32) + away_ref[:, rows, :].astype(f32)
+        out_ref[:, rows, :] = value.astype(bf16)
+        start = rows.stop
 
 
 def merge(own, got, away, waits=()):
-    return call(merge_kernel, [(own.shape, bf16)], (own, got, away), waits=waits, name="merge")[0]
+    return call(merge_kernel, [(own.shape, bf16)], (own, away, *got), waits=waits, name="merge")[0]
 
 
 def finish_kernel(where_ref, *refs):
@@ -619,63 +624,67 @@
     return call(kernel, out_shape, (normed, gp, sums, *weights), waits=waits, name="weight_back")
 
 
-def norm_back_kernel(where_ref, stats_ref, means_ref, gp_ref, gain_ref, *refs, orders, odd, with_high):
+def norm_back_kernel(where_ref, stats_ref, means_ref, gp_ref, gain_ref, *refs, orders, with_high):
     count = len(orders[0])
-    x_refs, refs = refs[:count], refs[count:]
-    *w_refs, high_ref, a_low, a_high, b_low, b_high, some_ref, gn_ref = refs
-    half_count, total, block, half_width = a_low.shape
-    out_refs = ((a_low, a_high), (b_low, b_high))
+    x_refs, refs = refs[: 2 * count], refs[2 * count :]
+    *w_refs, high_ref = refs[:-10]
+    all_out_refs, (some_ref, gn_ref) = refs[-10:-2], refs[-2:]
+    half_count, total, block, half_width = all_out_refs[0].shape
     features = 2 * half_width
     together = gn_ref.shape[0] // block
-    for r in range(total):
-        for d in range(0, count, together):
-            tokens = []
-            for n in range(together):
-                place = where_ref[3] ^ (orders[0][d + n] | odd)
-                tokens.append(pl.ds(pl.multiple_of(place * block, 16), block))
-                some_ref[n * block : (n + 1) * block, :] = gp_ref[r, tokens[n], :]
-            lane = 0
-            for w_ref in w_refs:
-                rows = w_ref.shape[0]
-                gn_ref[:, lane : lane + rows] = lax.dot_general(
-                    some_ref[...], w_ref[...], (((1,), (1,)), ((), ())), preferred_element_type=f32
-                )
-                lane += rows
-            for n in range(together):
-                mean, inv = stats_ref[r, 0, tokens[n], :], stats_ref[r, 1, tokens[n], :]
-                first, second = (
-                    jnp.sum(means_ref[r, m, tokens[n], :], axis=-1, keepdims=True) * (1.0 / features) for m in range(2)
-                )
-                slope = inv * inv * second
-                rest = inv * first - slope * mean
-                for part in range(2):
-                    at_d = orders[part].index(orders[0][d + n])
-                    out_ref = out_refs[part][at_d // half_count]
-                    start = pl.multiple_of((where_ref[0] ^ part) * half_width, LANES)
-                    if with_high:
-                        high = high_ref[r, where_ref[0] ^ part, tokens[n], :].astype(f32)
-                    for j in range(half_width // LANES):
-                        at = slice(part * half_width + LANES * j, part * half_width + LANES * (j + 1))
-                        value = inv * (gn_ref[n * block : (n + 1) * block, at] * gain_ref[:, at])
-                        x = x_refs[d + n][r, :block, pl.ds(start + LANES * j, LANES)].astype(f32)
-                        value -= slope * x + rest
+    for odd in (1, 0):
+        out_refs = all_out_refs[4 * (1 - odd) : 4 * (2 - odd)]
+        for r in range(total):
+            for d in range(0, count, together):
+                tokens = []
+                for n in range(together):
+                    place = where_ref[3] ^ (orders[0][d + n] | odd)
+                    tokens.append(pl.ds(pl.multiple_of(place * block, 16), block))
+                    some_ref[n * block : (n + 1) * block, :] = gp_ref[r, tokens[n], :]
+                lane = 0
+                for w_ref in w_refs:
+                    rows = w_ref.shape[0]
+                    gn_ref[:, lane : lane + rows] = lax.dot_general(
+                        some_ref[...], w_ref[...], (((1,), (1,)), ((), ())), preferred_element_type=f32
+                    )
+                    lane += rows
+                for n in range(together):
+                    x_ref = x_refs[orders[0][d + n] | odd]
+                    mean, inv = stats_ref[r, 0, tokens[n], :], stats_ref[r, 1, tokens[n], :]
+                    first, second = (
+                        jnp.sum(means_ref[r, m, tokens[n], :], axis=-1, keepdims=True) * (1.0 / features)
+                        for m in range(2)
+                    )
+                    slope = inv * inv * second
+                    rest = inv * first - slope * mean
+                    for part in range(2):
+                        at_d = orders[part].index(orders[0][d + n])
+                        out_ref = out_refs[2 * part + at_d // half_count]
+                        start = pl.multiple_of((where_ref[0] ^ part) * half_width, LANES)
                         if with_high:
-                            value += jnp.where(where_ref[3] == j, high, 0.0)
-                        out_ref[at_d % half_count, r, :, LANES * j : LANES * (j + 1)] = value.astype(bf16)
-
-
-def norm_back(where, blocks, orders, odd, stats, means, gp, weights, gain, high, with_high, waits):
-    count = len(blocks)
+                            high = high_ref[r, where_ref[0] ^ part, tokens[n], :].astype(f32)
+                        for j in range(half_width // LANES):
+                            at = slice(part * half_width + LANES * j, part * half_width + LANES * (j + 1))
+                            value = inv * (gn_ref[n * block : (n + 1) * block, at] * gain_ref[:, at])
+                            x = x_ref[r, :block, pl.ds(start + LANES * j, LANES)].astype(f32)
+                            value -= slope * x + rest
+                            if with_high:
+                                value += jnp.where(where_ref[3] == j, high, 0.0)
+                            out_ref[at_d % half_count, r, :, LANES * j : LANES * (j + 1)] = value.astype(bf16)
+
+
+def norm_back(where, blocks, orders, stats, means, gp, weights, gain, high, with_high, waits):
     rows, block, features = blocks[0].shape
     block -= STATS
     together = 2 * LANES // block
-    return call(
-        functools.partial(norm_back_kernel, orders=orders, odd=odd, with_high=with_high),
-        [((count // 2, rows, block, features // 2), bf16)] * 4,
+    out = call(
+        functools.partial(norm_back_kernel, orders=orders, with_high=with_high),
+        [((len(blocks) // 4, rows, block, features // 2), bf16)] * 8,
         (stats, means, gp, gain, *blocks, *weights, high), (where,), waits,
         scratch=[((together * block, gp.shape[2]), bf16), ((together * block, features), f32)],
         name="norm_back",
     )
+    return out[:4], out[4:]
 
 
 def totals_kernel(where_ref, sums_ref, own_ref, other_ref, gain_ref, shift_ref, out_ref, *, chunk):
@@ -808,64 +817,61 @@
 
     mask = (jnp.arange(group) == place)[:, None]
 
-    def norm_part(odd, waits):
-        out = norm_back(
-            where, [blocks[d | odd] for d in orders[0]], orders, odd, token_stats, means, gp, weights, gain_row, high_own, aligned,
-            waits,
-        )
-        if aligned:
-            return out
+    splits = 2 if paired else 1
+    by_feature_other, *away = weight_back(normed, gp, sums, weights, 1, group, [(row_block,)] * splits, ())
+    away_got = swapped(away[1]) if paired else None
+
+    sent, kept = norm_back(
+        where, blocks, orders, token_stats, means, gp, weights, gain_row, high_own, aligned, (by_feature_other,)
+    )
+    if not aligned:
         spread = high_own.swapaxes(1, 2).reshape(rows, group, block_len, chunks, 1, piece).swapaxes(0, 1)
         spread = jnp.where(mask, spread.astype(f32), 0.0).reshape(group, rows, block_len, features)
         spread = halves_turned(spread)[place ^ jnp.arange(group)]
         halves = (spread[..., : features // 2], spread[..., features // 2 :])
-        add = [add[d | odd] for add, order in zip(halves, orders) for d in order]
         n = group // 4
-        return [(v.astype(f32) + jnp.stack(add[i * n : (i + 1) * n])).astype(bf16) for i, v in enumerate(out)]
-
-    pieces = 1
-    cuts = [(row_block // pieces,) * pieces] * (2 if paired else 1)
-    by_feature_other, *away = weight_back(normed, gp, sums, weights, 1, group, cuts, ())
-    away_got = [swapped(value) for value in away[pieces:]]
-    sent = norm_part(1, (by_feature_other,))
+
+        def with_high(arrays, odd):
+            add = [half[d | odd] for half, order in zip(halves, orders) for d in order]
+            return [(v.astype(f32) + jnp.stack(add[i * n : (i + 1) * n])).astype(bf16) for i, v in enumerate(arrays)]
+
+        sent, kept = with_high(sent, 1), with_high(kept, 0)
     got = [flipped(value, 1) for value in sent]
-    by_feature_own, *here = weight_back(normed, gp, sums, weights, 0, group, cuts, sent[:1])
-    kept = norm_part(0, (by_feature_own,))
-    kept, sent = halve(kept, got, kept[:1])
+    if paired:
+        away = added(away[0], away_got, kept[:1])
+    else:
+        away = lax.psum_scatter(away[0], "dp", scatter_dimension=2, tiled=True)
+    z_got = across(away)
+    kept, sent = halve(kept, got)
     bit_pairs = list(zip(*(w[::-1] for w in ways)))
     got = [flipped(value, bit) for value, bit in zip(sent, bit_pairs.pop(0))]
-    hidden_got = shared(hidden_own)
+    cuts = [(row_block,), (row_block // 2,) * 2][:splits]
+    by_feature_own, *here = weight_back(normed, gp, sums, weights, 0, group, cuts, (away,))
     if paired:
-        away = [added(a, b, kept[:1]) for a, b in zip(away, away_got)]
-        here_got = [swapped(fence(value, away)) for value in here[pieces:]]
+        here_got = [swapped(value) for value in here[1:]]
     else:
-        away, here = ([lax.psum_scatter(x, "dp", scatter_dimension=2, tiled=True) for x in v] for v in (away, here))
-    z_got = [across(value) for value in away]
-
-    hidden = collected([hidden_got.reshape(group, -1, width)], bf16).reshape(rows, block_len, features)
-    for way in bit_pairs:
-        kept, sent = halve(kept, got, (hidden,))
-        got = [flipped(value, bit) for value, bit in zip(sent, way)]
-    grad_inputs = finish(where, kept, got)
+        here = lax.psum_scatter(here[0], "dp", scatter_dimension=2, tiled=True)
+    hidden = collected([shared(hidden_own).reshape(group, -1, width)], bf16).reshape(rows, block_len, features)
 
     if aligned:
         totals = call(
             functools.partial(totals_kernel, chunk=chunk), [((8, features), f32)],
-            (sums, by_feature_own, by_feature_other, gain_row, shift_row), (where,), kept[:1], name="totals",
+            (sums, by_feature_own, by_feature_other, gain_row, shift_row), (where,), name="totals",
         )[0]
     else:
         spread = jnp.where(mask, sums[:4, :width].reshape(4, chunks, 1, piece), 0.0).reshape(4, features)
         product, shift_sum = jnp.concatenate([by_feature_own, by_feature_other], axis=1)
         gain_sum = (product - shift_row[0] * shift_sum) / gain_row[0]
         totals = jnp.concatenate([spread, halves_turned(jnp.stack([gain_sum, shift_sum]))], axis=0)
+    for way in bit_pairs:
+        kept, sent = halve(kept, got, (hidden,))
+        got = [flipped(value, bit) for value, bit in zip(sent, way)]
+    grad_inputs = finish(where, kept, got)
     for bit in [1 << b for b in range(group.bit_length() - 1)]:
         totals = added(totals, flipped(totals, bit))
     waits = (grad_inputs, totals)
-    grad_weight = []
-    for i in range(pieces):
-        value = merge(here[i], here_got[i], z_got[i], waits) if paired else added(here[i], z_got[i], waits)
-        grad_weight.append(shared(value))
-    grad_weight = collected(grad_weight, f32)
+    value = merge(here[0], here_got, z_got, waits) if paired else added(here, z_got, waits)
+    grad_weight = collected([shared(value)], f32)
     totals = added(totals, swapped(totals)) if ranks == 2 else lax.psum(totals, "dp")
     totals = added(totals, across(totals))
 

time: 202 us -> 197 us (0.975)
  waiting for transfers between devices: 71.4 us -> 63.1 us
  local copies, waits for them, and re-layouts: 15.6 us -> 22.2 us
  Pallas kernels: 58.8 us -> 56.1 us
    unnamed x98 -> x112, local copies, waits for them, and re-layouts: 12.2 us -> 19.4 us
    ppermute x18, waiting for transfers between devices: 42.6 us -> 37.7 us  [flipped(): return lax.ppermute(value, 'fsdp', [(j, j ^ bit) for j in range(sections)])]
    ppermute x5 -> x6, starting transfers between devices: 5.26 us -> 8.19 us  [swapped(): return lax.ppermute(value, 'dp', [(0, 1), (1, 0)])]
    pallas_call x26 -> x25, Pallas kernels: 58.8 us -> 56.1 us  [call(): pl.pallas_call(body, in_specs=[in_smem] * len(scalars) + [in_vmem] * len(...]
    all_to_all x4, starting transfers between devices: 20.6 us -> 18.2 us  [shared(): lax.all_to_all(value, 'fsdp', 0, 0, tiled=True, axis_index_groups=groups)]
    ppermute x18, starting transfers between devices: 12.8 us -> 10.7 us  [flipped(): return lax.ppermute(value, 'fsdp', [(j, j ^ bit) for j in range(sections)])]
    ppermute x5, starting transfers between devices: 10 us -> 12.1 us  [across(): lax.ppermute(value, 'fsdp', [(j, (j + group) % sections) for j in range(s...]
  transfers between devices with their start and end apart: 33 -> 34, of which waited for: 13 -> 13; matrix products, arithmetic and copies ran while one was open for 3% -> 3% of each run, Pallas kernels for 17% -> 16%
where the time goes in v2:
time: 197 us; the launch traced here: 196 us
  waiting for transfers between devices  63.1 us (32%)
  Pallas kernels  56.1 us (28%)
  starting transfers between devices  50.4 us (26%)
  local copies, waits for them, and re-layouts  22.2 us (11%)
  other arithmetic  3.33 us (2%)
    pallas_call x25, Pallas kernels, call(): pl.pallas_call(body, in_specs=[in_smem] * len(scalars) + [in_vmem] * len(...  56.1 us
    ppermute x18, waiting for transfers between devices, flipped(): return lax.ppermute(value, 'fsdp', [(j, j ^ bit) for j in range(sections)])  37.7 us
    unnamed x112, local copies, waits for them, and re-layouts  19.4 us
    all_to_all x4, starting transfers between devices, shared(): lax.all_to_all(value, 'fsdp', 0, 0, tiled=True, axis_index_groups=groups)  18.2 us
    ppermute x5, starting transfers between devices, across(): lax.ppermute(value, 'fsdp', [(j, (j + group) % sections) for j in range(s...  12.1 us
    all_to_all x4, waiting for transfers between devices, shared(): lax.all_to_all(value, 'fsdp', 0, 0, tiled=True, axis_index_groups=groups)  11.1 us
    ppermute x18, starting transfers between devices, flipped(): return lax.ppermute(value, 'fsdp', [(j, j ^ bit) for j in range(sections)])  10.7 us
    ppermute x6, starting transfers between devices, swapped(): return lax.ppermute(value, 'dp', [(0, 1), (1, 0)])  8.19 us
  transfers between devices with their start and end apart: 34, of which 13 were waited for; matrix products, arithmetic and copies ran while one was open for 3% of the time, Pallas kernels for 16%

profile of v2, /device:TPU:8, one launch (start us, length us, event | category | flops | bytes accessed | tf_op | source)
XLA Modules:
  0.0 196.3 jit_solution(11706714647861807652)
XLA Ops:
  2.8 4.4 %all-to-all-start = ((bf16[8,128,384]{2,1,0:T(8,128)(2,1)}), bf16[8,128,384]{2,1,0:T(8,128)(2,1)S(1)}, u32[]{:S(2)}, u32[]{:S(2)}) async-start(bf16[8,128,384]{2,1,0:T(8,128)(2,1)} %deal.2), calls=%async_computation | async-start | bytes 1572864 | tf_op jit(solution)/shard_map/all_to_all | solution.py:754
  7.2 11.1 %all-to-all-done.refs_2_.refs_3_ = bf16[8,128,384]{2,1,0:T(8,128)(2,1)S(1)} async-done(((bf16[8,128,384]{2,1,0:T(8,128)(2,1)}), bf16[8,128,384]{2,1,0:T(8,128)(2,1)S(1)}, u32[]{:S(2)}, u32[]{:S(2)}) %all-to-all-start) | async-done | bytes 786464 | tf_op jit(solution)/shard_map/all_to_all | solution.py:754
  19.3 2.6 %collective-permute-start = (bf16[8,128,384]{2,1,0:T(8,128)(2,1)S(1)}, bf16[8,128,384]{2,1,0:T(8,128)(2,1)S(1)}, u32[]{:S(2)}, u32[]{:S(2)}) collective-permute-start(bf16[8,128,384]{2,1,0:T(8,128)(2,1)S(1)} %all-to-all-done.refs_2_.refs_3_), channel_id=1, source_target_pairs={{0,8},{1,9},{2,10},{3,11},{4,12},{5,13},{6,14},{7,15},{8,0},{9,1},... | collective-permute-start | bytes 2359304 | tf_op jit(solution)/shard_map/ppermute | solution.py:745
  22.7 4.9 %all-to-all-start.1 = ((bf16[8,1,128,256]{3,2,1,0:T(8,128)(2,1)}), bf16[8,1,128,256]{3,2,1,0:T(8,128)(2,1)S(1)}, u32[]{:S(2)}, u32[]{:S(2)}) async-start(bf16[8,1,128,256]{3,2,1,0:T(8,128)(2,1)} %bitcast.9), calls=%async_computation.1 | async-start | bytes 1048576 | tf_op jit(solution)/shard_map/all_to_all | solution.py:754
  29.1 1.5 collective-permute-start.1
  30.6 15.8 %collective-permute-done.5.refs_0_ = bf16[1,144,2048]{2,1,0:T(8,128)(2,1)} collective-permute-done((bf16[1,144,2048]{2,1,0:T(8,128)(2,1)S(1)}, bf16[1,144,2048]{2,1,0:T(8,128)(2,1)}, u32[]{:S(2)}, u32[]{:S(2)}) %collective-permute-start.5) | collective-permute-done | bytes 589856 | tf_op jit(solution)/shard_map/ppermute | solution.py:748
  46.4 1.6 collective-permute-start.7
  48.8 6.3 %collective-permute-done.refs_1_.refs_9_ = bf16[8,128,384]{2,1,0:T(8,128)(2,1)S(1)} collective-permute-done((bf16[8,128,384]{2,1,0:T(8,128)(2,1)S(1)}, bf16[8,128,384]{2,1,0:T(8,128)(2,1)S(1)}, u32[]{:S(2)}, u32[]{:S(2)}) %collective-permute-start) | collective-permute-done | bytes 786464 | tf_op jit(solution)/shard_map/ppermute | solution.py:745
  58.7 3.4 %collective-permute-done.7.refs_0_ = bf16[1,144,2048]{2,1,0:T(8,128)(2,1)} collective-permute-done((bf16[1,144,2048]{2,1,0:T(8,128)(2,1)}, bf16[1,144,2048]{2,1,0:T(8,128)(2,1)}, u32[]{:S(2)}, u32[]{:S(2)}) %collective-permute-start.7) | collective-permute-done | bytes 589856 | tf_op jit(solution)/shard_map/ppermute | solution.py:748
  65.6 4.5 %norm.1 = (bf16[1,1024,2048]{2,1,0:T(8,128)(2,1)S(1)}, f32[1,2,1024,128]{3,2,1,0:T(8,128)S(1)}, f32[1,1088,128]{2,1,0:T(8,128)S(1)}, bf16[1,2,1024,128]{3,2,1,0:T(8,128)(2,1)S(1)}) custom-call(s32[5]{0:T(128)S(1)} %stack.23.refs_0_, f32[1,2048]{1,0:T(1,128)S(1)} %bitcast.47, f32[1,2048]{1,0:T(1,128)S(1)} %bitcast.50, bf16[1,144,2048]{2,1,0:T(8,128)(2,1)S(1)} %copy-done.12, ...), custom_call_target="tpu_custom_call" | custom-call | tf_op jit(solution)/shard_map/norm/pallas_call | solution.py:41
  70.9 3.2 %project.1 = (f32[1,6,1024,128]{3,2,1,0:T(8,128)S(1)}, f32[16,768]{1,0:T(8,128)S(1)}, bf16[1024,768]{1,0:T(8,128)(2,1)S(1)}) custom-call(s32[5]{0:T(128)S(1)} %copy-done.46, bf16[1,1024,2048]{2,1,0:T(8,128)(2,1)S(1)} %get-tuple-element.55.refs_1_.refs_0_, bf16[16,2048]{1,0:T(8,128)(2,1)S(1)} %pad.4.refs_2_, bf16[8,128,384]{2,1,0:T(8,128)(2,1)S(1)} %copy-done.14, ...), custom_call_target="tpu_custom_call" | custom-call | tf_op jit(solution)/shard_map/project/pallas_call | solution.py:41
  74.1 7.8 %blocks_forward.1 = (f32[1,6,1088,128]{3,2,1,0:T(8,128)S(1)}, f32[1,2,1088,128]{3,2,1,0:T(8,128)S(1)}, f32[1,2,336,128]{3,2,1,0:T(8,128)S(1)}, f32[1,1,256]{2,1,...) custom-call(s32[5]{0:T(128)S(1)} %copy-done.46, ...), custom_call_target="tpu_custom_call" | custom-call | tf_op jit(solution)/shard_map/blocks_forward/pallas_call | solution.py:41
  82.0 2.5 %collective-permute-start.10 = (f32[1,1,256]{2,1,0:T(1,128)S(1)}, f32[1,1,256]{2,1,0:T(1,128)S(1)}, u32[]{:S(2)}, u32[]{:S(2)}) collective-permute-start(f32[1,1,256]{2,1,0:T(1,128)S(1)} %get-tuple-element.64), channel_id=1, source_target_pairs={{0,8},{1,9},{2,10},{3,11},{4,12},{5,13},{6,14},{7,15},{8,0},{9,1},... | collective-permute-start | bytes 3080 | tf_op jit(solution)/shard_map/ppermute | solution.py:745
  86.5 2.7 %entry.1 = (f32[1,2,200,128]{3,2,1,0:T(8,128)S(1)}, f32[1,1,256]{2,1,0:T(1,128)S(1)}) custom-call(f32[1,6,1088,128]{3,2,1,0:T(8,128)S(1)} %get-tuple-element.59.refs_0_.refs_1_, f32[1,1088,128]{2,1,0:T(8,128)S(1)} %get-tuple-element.58.refs_6_.refs_1_.refs_2_, f32[1,2,1088,128]{3,2,1,0:T(8,128)S(1)} %get-tuple-element.60.refs_2_.refs_3_, ...), custom_call_target="tpu_custom_call" | custom-call | tf_op jit(solution)/shard_map/entry/pallas_call | solution.py:41
  89.2 2.5 %collective-permute-start.11 = (f32[1,1,256]{2,1,0:T(1,128)S(1)}, f32[1,1,256]{2,1,0:T(1,128)S(1)}, u32[]{:S(2)}, u32[]{:S(2)}) collective-permute-start(f32[1,1,256]{2,1,0:T(1,128)S(1)} %get-tuple-element.66), channel_id=1, source_target_pairs={{0,8},{1,9},{2,10},{3,11},{4,12},{5,13},{6,14},{7,15},{8,0},{9,1},... | collective-permute-start | bytes 3080 | tf_op jit(solution)/shard_map/ppermute | solution.py:745
  91.7 4.1 %lead_forward.1.refs_4_ = f32[1,2,816,128]{3,2,1,0:T(8,128)S(1)} custom-call(f32[1,6,1088,128]{3,2,1,0:T(8,128)S(1)} %get-tuple-element.59.refs_0_.refs_1_, f32[1,1088,128]{2,1,0:T(8,128)S(1)} %get-tuple-element.58.refs_6_.refs_1_.refs_2_, f32[1,256]{1,0:T(1,128)S(1)} %copy-done.48, f32[1,1,256]{2,1,0:T(1,128)S(1)} %get-tuple-element.61.refs_3_, ...), custom_call_target="tpu_custom_call" | custom-call | tf_op jit(solution)/shard_map/lead_forward/pallas_call | solution.py:41
  95.8 6.4 %backward.1 = (bf16[1,1024,768]{2,1,0:T(8,128)(2,1)S(1)}, bf16[8,1,128,256]{3,2,1,0:T(8,128)(2,1)S(1)}, bf16[1,2,1024,128]{3,2,1,0:T(8,128)(2,1)S(1)}, f32[8,768...) custom-call(s32[5]{0:T(128)S(1)} %copy-done.47, ...), custom_call_target="tpu_custom_call" | custom-call | tf_op jit(solution)/shard_map/backward/pallas_call | solution.py:41
  102.2 3.1 %weight_back.2 = (f32[2,1024]{1,0:T(2,128)S(1)}, bf16[8,128,384]{2,1,0:T(8,128)(2,1)S(1)}, bf16[8,128,384]{2,1,0:T(8,128)(2,1)}) custom-call(bf16[1,1024,2048]{2,1,0:T(8,128)(2,1)S(1)} %get-tuple-element.55.refs_1_.refs_0_, bf16[1,1024,768]{2,1,0:T(8,128)(2,1)S(1)} %get-tuple-element.71.refs_1_.refs_3_, f32[8,768]{1,0:T(8,128)S(1)} %get-tuple-element.75.refs_2_.refs_1_, ...), custom_call_target="tpu_custom_call" | custom-call | tf_op jit(solution)/shard_map/weight_back/pallas_call | solution.py:41
  106.9 7.6 %norm_back.1 = (bf16[2,1,128,1024]{3,2,1,0:T(8,128)(2,1)}, bf16[2,1,128,1024]{3,2,1,0:T(8,128)(2,1)}, bf16[2,1,128,1024]{3,2,1,0:T(8,128)(2,1)}, bf16[2,1,128,10...) custom-call(s32[5]{0:T(128)S(1)} %copy-done.47, ...), custom_call_target="tpu_custom_call" | custom-call | tf_op jit(solution)/shard_map/norm_back/pallas_call | solution.py:41
  117.9 4.2 %all-to-all-start.2 = ((bf16[8,1,128,256]{3,2,1,0:T(8,128)(2,1)}), bf16[8,1,128,256]{3,2,1,0:T(8,128)(2,1)S(1)}, u32[]{:S(2)}, u32[]{:S(2)}) async-start(bf16[8,1,128,256]{3,2,1,0:T(8,128)(2,1)} %copy-done.35), calls=%async_computation.2 | async-start | bytes 1048576 | tf_op jit(solution)/shard_map/all_to_all | solution.py:754
  125.3 3.0 %halve.2 = (bf16[2,1,128,1024]{3,2,1,0:T(8,128)(2,1)S(1)}, bf16[2,1,128,1024]{3,2,1,0:T(8,128)(2,1)S(1)}, bf16[2,1,128,1024]{3,2,1,0:T(8,128)(2,1)S(1)}, bf16[2,1,128,1024]{3,2,1,0:T(8,128)(2,1)}) custom-call(bf16[2,1,128,1024]{3,2,1,0:T(8,128)(2,1)S(1)} %get-tuple-element.77.refs_0_.refs_2_, bf16[2,1,128,1024]{3,2,1,0:T(8,128)(2,1)S(1)} %copy-done.38, ...), custom_call_target="tpu_custom_call" | custom-call | tf_op jit(solution)/shard_map/halve/pallas_call | solution.py:41
  135.3 2.1 %collective-permute-start.22 = (bf16[8,128,384]{2,1,0:T(8,128)(2,1)S(1)}, bf16[8,128,384]{2,1,0:T(8,128)(2,1)}, u32[]{:S(2)}, u32[]{:S(2)}) collective-permute-start(bf16[8,128,384]{2,1,0:T(8,128)(2,1)S(1)} %added.6.refs_5_), channel_id=1, source_target_pairs={{0,8},{1,9},{2,10},{3,11},{4,12},{5,13},{6,14},{7,15},{8,0},{9,1},... | collective-permute-start | bytes 2359304 | tf_op jit(solution)/shard_map/ppermute | solution.py:745
  138.8 3.1 %weight_back.3 = (f32[2,1024]{1,0:T(2,128)S(1)}, bf16[8,128,384]{2,1,0:T(8,128)(2,1)S(1)}, bf16[8,64,384]{2,1,0:T(8,128)(2,1)}, bf16[8,64,384]{2,1,0:T(8,128)(2,1)}) custom-call(bf16[1,1024,2048]{2,1,0:T(8,128)(2,1)S(1)} %copy-done.2, bf16[1,1024,768]{2,1,0:T(8,128)(2,1)S(1)} %copy-done.10, f32[8,768]{1,0:T(8,128)S(1)} %get-tuple-element.75.refs_2_.refs_1_, ...), custom_call_target="tpu_custom_call" | custom-call | tf_op jit(solution)/shard_map/weight_back/pallas_call | solution.py:41
  145.4 3.6 %collective-permute-done.26.refs_1_ = f32[8,2048]{1,0:T(8,128)S(1)} collective-permute-done((f32[8,2048]{1,0:T(8,128)S(1)}, f32[8,2048]{1,0:T(8,128)S(1)}, u32[]{:S(2)}, u32[]{:S(2)}) %collective-permute-start.26) | collective-permute-done | bytes 65568 | tf_op jit(solution)/shard_map/ppermute | solution.py:748
  156.9 7.8 %collective-permute-done.27.refs_1_ = f32[8,2048]{1,0:T(8,128)S(1)} collective-permute-done((f32[8,2048]{1,0:T(8,128)S(1)}, f32[8,2048]{1,0:T(8,128)S(1)}, u32[]{:S(2)}, u32[]{:S(2)}) %collective-permute-start.27) | collective-permute-done | bytes 65568 | tf_op jit(solution)/shard_map/ppermute | solution.py:748
  165.2 3.9 %collective-permute-done.18.refs_3_ = bf16[1,1,128,1024]{3,2,1,0:T(8,128)(2,1)S(1)} collective-permute-done((bf16[1,1,128,1024]{3,2,1,0:T(8,128)(2,1)S(1)}, bf16[1,1,128,1024]{3,2,1,0:T(8,128)(2,1)S(1)}, u32[]{:S(2)}, u32[]{:S(2)}) %collective-permute-start.18) | collective-permute-done | bytes 262176 | tf_op jit(solution)/shard_map/ppermute | solution.py:748
  169.2 1.9 collective-permute-done.19.refs_4_
  173.5 2.4 %merge.1 = bf16[8,128,384]{2,1,0:T(8,128)(2,1)} custom-call(bf16[8,128,384]{2,1,0:T(8,128)(2,1)S(1)} %copy-done.22, bf16[8,128,384]{2,1,0:T(8,128)(2,1)} %collective-permute-done.22.refs_1_, bf16[8,64,384]{2,1,0:T(8,128)(2,1)S(1)} %collective-permute-done.23.refs_2_, bf16[8,64,384]{2,1,0:T(8,128)(2,1)S(1)} %collective-permute-done.24.refs_3_, ...), custom_call_target="tpu_custom_call" | custom-call | tf_op jit(solution)/shard_map/merge/pallas_call | solution.py:41
  175.9 4.7 %all-to-all-start.3 = ((bf16[8,128,384]{2,1,0:T(8,128)(2,1)}), bf16[8,128,384]{2,1,0:T(8,128)(2,1)S(1)}, u32[]{:S(2)}, u32[]{:S(2)}) async-start(bf16[8,128,384]{2,1,0:T(8,128)(2,1)} %merge.1), calls=%async_computation.3 | async-start | bytes 1572864 | tf_op jit(solution)/shard_map/all_to_all | solution.py:754
  180.6 2.6 %collective-permute-start.28 = (f32[8,2048]{1,0:T(8,128)S(1)}, f32[8,2048]{1,0:T(8,128)S(1)}, u32[]{:S(2)}, u32[]{:S(2)}) collective-permute-start(f32[8,2048]{1,0:T(8,128)S(1)} %added.9.refs_5_.refs_0_), channel_id=1, source_target_pairs={{0,16},{16,0},{1,17},{17,1},{2,18},{18,2},{3,19},{19,3},{4,20},{20... | collective-permute-start | bytes 196616 | tf_op jit(solution)/shard_map/ppermute | solution.py:751
  185.7 2.5 %collective-permute-start.29 = (f32[8,2048]{1,0:T(8,128)S(1)}, f32[8,2048]{1,0:T(8,128)S(1)}, u32[]{:S(2)}, u32[]{:S(2)}) collective-permute-start(f32[8,2048]{1,0:T(8,128)S(1)} %added.10.refs_0_), channel_id=1, source_target_pairs={{0,8},{1,9},{2,10},{3,11},{4,12},{5,13},{6,14},{7,15},{8,0},{9,1},... | collective-permute-start | bytes 196616 | tf_op jit(solution)/shard_map/ppermute | solution.py:745
  188.2 5.3 %collective-permute-done.20 = f32[1,128]{1,0:T(1,128)S(1)} collective-permute-done((f32[1,128]{1,0:T(1,128)S(1)}, f32[1,128]{1,0:T(1,128)S(1)}, u32[]{:S(2)}, u32[]{:S(2)}) %collective-permute-start.20) | collective-permute-done | bytes 544 | tf_op jit(solution)/shard_map/ppermute | solution.py:881
  (197 shorter events, 52.2 us)
Async XLA Ops:
  2.8 15.5 %all-to-all-start = ((bf16[8,128,384]{2,1,0:T(8,128)(2,1)}), bf16[8,128,384]{2,1,0:T(8,128)(2,1)S(1)}, u32[]{:S(2)}, u32[]{:S(2)}) async-start(bf16[8,128,384]{2,1,0:T(8,128)(2,1)} %deal.2), calls=%async_computation | async-start | bytes 1572864 | tf_op jit(solution)/shard_map/all_to_all | solution.py:754
  18.6 27.8 %collective-permute-start.5 = (bf16[1,144,2048]{2,1,0:T(8,128)(2,1)S(1)}, bf16[1,144,2048]{2,1,0:T(8,128)(2,1)}, u32[]{:S(2)}, u32[]{:S(2)}) collective-permute-start(bf16[1,144,2048]{2,1,0:T(8,128)(2,1)S(1)} %stats.1.refs_0_), channel_id=1, source_target_pairs={{0,4},{1,5},{2,6},{3,7},{4,0},{5,1},{6,2},{7,3},{8,12},{9,13},{10,... | collective-permute-start | bytes 1769480 | tf_op jit(solution)/shard_map/ppermute | solution.py:748
  19.3 35.8 %collective-permute-start = (bf16[8,128,384]{2,1,0:T(8,128)(2,1)S(1)}, bf16[8,128,384]{2,1,0:T(8,128)(2,1)S(1)}, u32[]{:S(2)}, u32[]{:S(2)}) collective-permute-start(bf16[8,128,384]{2,1,0:T(8,128)(2,1)S(1)} %all-to-all-done.refs_2_.refs_3_), channel_id=1, source_target_pairs={{0,8},{1,9},{2,10},{3,11},{4,12},{5,13},{6,14},{7,15},{8,0},{9,1},... | collective-permute-start | bytes 2359304 | tf_op jit(solution)/shard_map/ppermute | solution.py:745
  22.7 42.7 %all-to-all-start.1 = ((bf16[8,1,128,256]{3,2,1,0:T(8,128)(2,1)}), bf16[8,1,128,256]{3,2,1,0:T(8,128)(2,1)S(1)}, u32[]{:S(2)}, u32[]{:S(2)}) async-start(bf16[8,1,128,256]{3,2,1,0:T(8,128)(2,1)} %bitcast.9), calls=%async_computation.1 | async-start | bytes 1048576 | tf_op jit(solution)/shard_map/all_to_all | solution.py:754
  27.6 29.6 %collective-permute-start.3 = (bf16[1,144,2048]{2,1,0:T(8,128)(2,1)S(1)}, bf16[1,144,2048]{2,1,0:T(8,128)(2,1)}, u32[]{:S(2)}, u32[]{:S(2)}) collective-permute-start(bf16[1,144,2048]{2,1,0:T(8,128)(2,1)S(1)} %stats.1.refs_0_), channel_id=1, source_target_pairs={{0,2},{1,3},{2,0},{3,1},{4,6},{5,7},{6,4},{7,5},{8,10},{9,11},{10,... | collective-permute-start | bytes 1769480 | tf_op jit(solution)/shard_map/ppermute | solution.py:748
  29.1 28.2 %collective-permute-start.1 = (bf16[8,128,384]{2,1,0:T(8,128)(2,1)S(1)}, bf16[8,128,384]{2,1,0:T(8,128)(2,1)S(1)}, u32[]{:S(2)}, u32[]{:S(2)}) collective-permute-start(bf16[8,128,384]{2,1,0:T(8,128)(2,1)S(1)} %all-to-all-done.refs_2_.refs_3_), channel_id=1, source_target_pairs={{0,16},{16,0},{1,17},{17,1},{2,18},{18,2},{3,19},{19,3},{4,20},{20... | collective-permute-start | bytes 2359304 | tf_op jit(solution)/shard_map/ppermute | solution.py:751
  46.4 15.7 %collective-permute-start.7 = (bf16[1,144,2048]{2,1,0:T(8,128)(2,1)}, bf16[1,144,2048]{2,1,0:T(8,128)(2,1)}, u32[]{:S(2)}, u32[]{:S(2)}) collective-permute-start(bf16[1,144,2048]{2,1,0:T(8,128)(2,1)} %collective-permute-done.5.refs_0_), channel_id=1, source_target_pairs={{0,2},{1,3},{2,0},{3,1},{4,6},{5,7},{6,4},{7,5},{8,10},{9,11},{10,... | collective-permute-start | bytes 1769480 | tf_op jit(solution)/shard_map/ppermute | solution.py:748
  55.1 19.0 %collective-permute-start.9 = (bf16[8,128,384]{2,1,0:T(8,128)(2,1)S(1)}, bf16[8,128,384]{2,1,0:T(8,128)(2,1)}, u32[]{:S(2)}, u32[]{:S(2)}) collective-permute-start(bf16[8,128,384]{2,1,0:T(8,128)(2,1)S(1)} %collective-permute-done.refs_1_.refs_9_), channel_id=1, source_target_pairs={{0,16},{16,0},{1,17},{17,1},{2,18},{18,2},{3,19},{19,3},{4,20},{20... | collective-permute-start | bytes 2359304 | tf_op jit(solution)/shard_map/ppermute | solution.py:751
  58.2 7.2 %collective-permute-start.4 = (bf16[1,144,2048]{2,1,0:T(8,128)(2,1)}, bf16[1,144,2048]{2,1,0:T(8,128)(2,1)S(1)}, u32[]{:S(2)}, u32[]{:S(2)}) collective-permute-start(bf16[1,144,2048]{2,1,0:T(8,128)(2,1)} %fence.5.refs_5_.refs_7_), channel_id=1, source_target_pairs={{0,1},{1,0},{2,3},{3,2},{4,5},{5,4},{6,7},{7,6},{8,9},{9,8},{10,11... | collective-permute-start | bytes 1769480 | tf_op jit(solution)/shard_map/ppermute | solution.py:748
  58.2 7.2 %collective-permute-start.2 = (bf16[1,144,2048]{2,1,0:T(8,128)(2,1)}, bf16[1,144,2048]{2,1,0:T(8,128)(2,1)S(1)}, u32[]{:S(2)}, u32[]{:S(2)}) collective-permute-start(bf16[1,144,2048]{2,1,0:T(8,128)(2,1)} %fence.4.refs_3_.refs_5_), channel_id=1, source_target_pairs={{0,1},{1,0},{2,3},{3,2},{4,5},{5,4},{6,7},{7,6},{8,9},{9,8},{10,11... | collective-permute-start | bytes 1769480 | tf_op jit(solution)/shard_map/ppermute | solution.py:748
  62.2 3.3 %collective-permute-start.6 = (bf16[1,144,2048]{2,1,0:T(8,128)(2,1)}, bf16[1,144,2048]{2,1,0:T(8,128)(2,1)}, u32[]{:S(2)}, u32[]{:S(2)}) collective-permute-start(bf16[1,144,2048]{2,1,0:T(8,128)(2,1)} %fence.6.refs_7_.refs_9_), channel_id=1, source_target_pairs={{0,1},{1,0},{2,3},{3,2},{4,5},{5,4},{6,7},{7,6},{8,9},{9,8},{10,11... | collective-permute-start | bytes 1769480 | tf_op jit(solution)/shard_map/ppermute | solution.py:748
  82.0 4.5 %collective-permute-start.10 = (f32[1,1,256]{2,1,0:T(1,128)S(1)}, f32[1,1,256]{2,1,0:T(1,128)S(1)}, u32[]{:S(2)}, u32[]{:S(2)}) collective-permute-start(f32[1,1,256]{2,1,0:T(1,128)S(1)} %get-tuple-element.64), channel_id=1, source_target_pairs={{0,8},{1,9},{2,10},{3,11},{4,12},{5,13},{6,14},{7,15},{8,0},{9,1},... | collective-permute-start | bytes 3080 | tf_op jit(solution)/shard_map/ppermute | solution.py:745
  89.2 6.5 %collective-permute-start.11 = (f32[1,1,256]{2,1,0:T(1,128)S(1)}, f32[1,1,256]{2,1,0:T(1,128)S(1)}, u32[]{:S(2)}, u32[]{:S(2)}) collective-permute-start(f32[1,1,256]{2,1,0:T(1,128)S(1)} %get-tuple-element.66), channel_id=1, source_target_pairs={{0,8},{1,9},{2,10},{3,11},{4,12},{5,13},{6,14},{7,15},{8,0},{9,1},... | collective-permute-start | bytes 3080 | tf_op jit(solution)/shard_map/ppermute | solution.py:745
  105.3 26.6 %collective-permute-start.21 = (bf16[8,128,384]{2,1,0:T(8,128)(2,1)}, bf16[8,128,384]{2,1,0:T(8,128)(2,1)S(1)}, u32[]{:S(2)}, u32[]{:S(2)}) collective-permute-start(bf16[8,128,384]{2,1,0:T(8,128)(2,1)} %get-tuple-element.95), channel_id=1, source_target_pairs={{0,16},{16,0},{1,17},{17,1},{2,18},{18,2},{3,19},{19,3},{4,20},{20... | collective-permute-start | bytes 2359304 | tf_op jit(solution)/shard_map/ppermute | solution.py:751
  116.9 5.2 %collective-permute-start.12 = (bf16[2,1,128,1024]{3,2,1,0:T(8,128)(2,1)}, bf16[2,1,128,1024]{3,2,1,0:T(8,128)(2,1)}, u32[]{:S(2)}, u32[]{:S(2)}) collective-permute-start(bf16[2,1,128,1024]{3,2,1,0:T(8,128)(2,1)} %get-tuple-element.81), channel_id=1, source_target_pairs={{0,1},{1,0},{2,3},{3,2},{4,5},{5,4},{6,7},{7,6},{8,9},{9,8},{10,11... | collective-permute-start | bytes 1572872 | tf_op jit(solution)/shard_map/ppermute | solution.py:748
  116.9 5.2 %collective-permute-start.13 = (bf16[2,1,128,1024]{3,2,1,0:T(8,128)(2,1)}, bf16[2,1,128,1024]{3,2,1,0:T(8,128)(2,1)}, u32[]{:S(2)}, u32[]{:S(2)}) collective-permute-start(bf16[2,1,128,1024]{3,2,1,0:T(8,128)(2,1)} %get-tuple-element.82), channel_id=1, source_target_pairs={{0,1},{1,0},{2,3},{3,2},{4,5},{5,4},{6,7},{7,6},{8,9},{9,8},{10,11... | collective-permute-start | bytes 1572872 | tf_op jit(solution)/shard_map/ppermute | solution.py:748
  117.4 4.7 %collective-permute-start.14 = (bf16[2,1,128,1024]{3,2,1,0:T(8,128)(2,1)}, bf16[2,1,128,1024]{3,2,1,0:T(8,128)(2,1)}, u32[]{:S(2)}, u32[]{:S(2)}) collective-permute-start(bf16[2,1,128,1024]{3,2,1,0:T(8,128)(2,1)} %get-tuple-element.83), channel_id=1, source_target_pairs={{0,1},{1,0},{2,3},{3,2},{4,5},{5,4},{6,7},{7,6},{8,9},{9,8},{10,11... | collective-permute-start | bytes 1572872 | tf_op jit(solution)/shard_map/ppermute | solution.py:748
  117.4 4.7 %collective-permute-start.15 = (bf16[2,1,128,1024]{3,2,1,0:T(8,128)(2,1)}, bf16[2,1,128,1024]{3,2,1,0:T(8,128)(2,1)}, u32[]{:S(2)}, u32[]{:S(2)}) collective-permute-start(bf16[2,1,128,1024]{3,2,1,0:T(8,128)(2,1)} %get-tuple-element.84), channel_id=1, source_target_pairs={{0,1},{1,0},{2,3},{3,2},{4,5},{5,4},{6,7},{7,6},{8,9},{9,8},{10,11... | collective-permute-start | bytes 1572872 | tf_op jit(solution)/shard_map/ppermute | solution.py:748
  117.9 33.9 %all-to-all-start.2 = ((bf16[8,1,128,256]{3,2,1,0:T(8,128)(2,1)}), bf16[8,1,128,256]{3,2,1,0:T(8,128)(2,1)S(1)}, u32[]{:S(2)}, u32[]{:S(2)}) async-start(bf16[8,1,128,256]{3,2,1,0:T(8,128)(2,1)} %copy-done.35), calls=%async_computation.2 | async-start | bytes 1048576 | tf_op jit(solution)/shard_map/all_to_all | solution.py:754
  129.9 19.6 %collective-permute-start.16 = (bf16[2,1,128,1024]{3,2,1,0:T(8,128)(2,1)S(1)}, bf16[2,1,128,1024]{3,2,1,0:T(8,128)(2,1)S(1)}, u32[]{:S(2)}, u32[]{:S(2)}) collective-permute-start(bf16[2,1,128,1024]{3,2,1,0:T(8,128)(2,1)S(1)} %get-tuple-element.87), channel_id=1, source_target_pairs={{0,2},{1,3},{2,0},{3,1},{4,6},{5,7},{6,4},{7,5},{8,10},{9,11},{10,... | collective-permute-start | bytes 1572872 | tf_op jit(solution)/shard_map/ppermute | solution.py:748
  131.3 21.4 %collective-permute-start.17 = (bf16[2,1,128,1024]{3,2,1,0:T(8,128)(2,1)}, bf16[2,1,128,1024]{3,2,1,0:T(8,128)(2,1)}, u32[]{:S(2)}, u32[]{:S(2)}) collective-permute-start(bf16[2,1,128,1024]{3,2,1,0:T(8,128)(2,1)} %get-tuple-element.88), channel_id=1, source_target_pairs={{0,4},{1,5},{2,6},{3,7},{4,0},{5,1},{6,2},{7,3},{8,12},{9,13},{10,... | collective-permute-start | bytes 1572872 | tf_op jit(solution)/shard_map/ppermute | solution.py:748
  135.3 37.2 %collective-permute-start.22 = (bf16[8,128,384]{2,1,0:T(8,128)(2,1)S(1)}, bf16[8,128,384]{2,1,0:T(8,128)(2,1)}, u32[]{:S(2)}, u32[]{:S(2)}) collective-permute-start(bf16[8,128,384]{2,1,0:T(8,128)(2,1)S(1)} %added.6.refs_5_), channel_id=1, source_target_pairs={{0,8},{1,9},{2,10},{3,11},{4,12},{5,13},{6,14},{7,15},{8,0},{9,1},... | collective-permute-start | bytes 2359304 | tf_op jit(solution)/shard_map/ppermute | solution.py:745
  144.7 4.3 %collective-permute-start.26 = (f32[8,2048]{1,0:T(8,128)S(1)}, f32[8,2048]{1,0:T(8,128)S(1)}, u32[]{:S(2)}, u32[]{:S(2)}) collective-permute-start(f32[8,2048]{1,0:T(8,128)S(1)} %added.7.refs_0_), channel_id=1, source_target_pairs={{0,2},{1,3},{2,0},{3,1},{4,6},{5,7},{6,4},{7,5},{8,10},{9,11},{10,... | collective-permute-start | bytes 196616 | tf_op jit(solution)/shard_map/ppermute | solution.py:748
  144.9 27.6 %collective-permute-start.23 = (bf16[8,64,384]{2,1,0:T(8,128)(2,1)}, bf16[8,64,384]{2,1,0:T(8,128)(2,1)S(1)}, u32[]{:S(2)}, u32[]{:S(2)}) collective-permute-start(bf16[8,64,384]{2,1,0:T(8,128)(2,1)} %get-tuple-element.97), channel_id=1, source_target_pairs={{0,16},{16,0},{1,17},{17,1},{2,18},{18,2},{3,19},{19,3},{4,20},{20... | collective-permute-start | bytes 1179656 | tf_op jit(solution)/shard_map/ppermute | solution.py:751
  149.0 23.5 %collective-permute-start.24 = (bf16[8,64,384]{2,1,0:T(8,128)(2,1)}, bf16[8,64,384]{2,1,0:T(8,128)(2,1)S(1)}, u32[]{:S(2)}, u32[]{:S(2)}) collective-permute-start(bf16[8,64,384]{2,1,0:T(8,128)(2,1)} %get-tuple-element.98), channel_id=1, source_target_pairs={{0,16},{16,0},{1,17},{17,1},{2,18},{18,2},{3,19},{19,3},{4,20},{20... | collective-permute-start | bytes 1179656 | tf_op jit(solution)/shard_map/ppermute | solution.py:751
  150.3 14.3 %collective-permute-start.27 = (f32[8,2048]{1,0:T(8,128)S(1)}, f32[8,2048]{1,0:T(8,128)S(1)}, u32[]{:S(2)}, u32[]{:S(2)}) collective-permute-start(f32[8,2048]{1,0:T(8,128)S(1)} %added.8.refs_0_), channel_id=1, source_target_pairs={{0,4},{1,5},{2,6},{3,7},{4,0},{5,1},{6,2},{7,3},{8,12},{9,13},{10,... | collective-permute-start | bytes 196616 | tf_op jit(solution)/shard_map/ppermute | solution.py:748
  156.3 12.9 %collective-permute-start.18 = (bf16[1,1,128,1024]{3,2,1,0:T(8,128)(2,1)S(1)}, bf16[1,1,128,1024]{3,2,1,0:T(8,128)(2,1)S(1)}, u32[]{:S(2)}, u32[]{:S(2)}) collective-permute-start(bf16[1,1,128,1024]{3,2,1,0:T(8,128)(2,1)S(1)} %get-tuple-element.91), channel_id=1, source_target_pairs={{0,4},{1,5},{2,6},{3,7},{4,0},{5,1},{6,2},{7,3},{8,12},{9,13},{10,... | collective-permute-start | bytes 786440 | tf_op jit(solution)/shard_map/ppermute | solution.py:748
  164.7 6.4 %collective-permute-start.19 = (bf16[1,1,128,1024]{3,2,1,0:T(8,128)(2,1)S(1)}, bf16[1,1,128,1024]{3,2,1,0:T(8,128)(2,1)S(1)}, u32[]{:S(2)}, u32[]{:S(2)}) collective-permute-start(bf16[1,1,128,1024]{3,2,1,0:T(8,128)(2,1)S(1)} %get-tuple-element.92), channel_id=1, source_target_pairs={{0,2},{1,3},{2,0},{3,1},{4,6},{5,7},{6,4},{7,5},{8,10},{9,11},{10,... | collective-permute-start | bytes 786440 | tf_op jit(solution)/shard_map/ppermute | solution.py:748
  175.9 19.0 %all-to-all-start.3 = ((bf16[8,128,384]{2,1,0:T(8,128)(2,1)}), bf16[8,128,384]{2,1,0:T(8,128)(2,1)S(1)}, u32[]{:S(2)}, u32[]{:S(2)}) async-start(bf16[8,128,384]{2,1,0:T(8,128)(2,1)} %merge.1), calls=%async_computation.3 | async-start | bytes 1572864 | tf_op jit(solution)/shard_map/all_to_all | solution.py:754
  180.6 5.0 %collective-permute-start.28 = (f32[8,2048]{1,0:T(8,128)S(1)}, f32[8,2048]{1,0:T(8,128)S(1)}, u32[]{:S(2)}, u32[]{:S(2)}) collective-permute-start(f32[8,2048]{1,0:T(8,128)S(1)} %added.9.refs_5_.refs_0_), channel_id=1, source_target_pairs={{0,16},{16,0},{1,17},{17,1},{2,18},{18,2},{3,19},{19,3},{4,20},{20... | collective-permute-start | bytes 196616 | tf_op jit(solution)/shard_map/ppermute | solution.py:751
  183.3 10.2 %collective-permute-start.20 = (f32[1,128]{1,0:T(1,128)S(1)}, f32[1,128]{1,0:T(1,128)S(1)}, u32[]{:S(2)}, u32[]{:S(2)}) collective-permute-start(f32[1,128]{1,0:T(1,128)S(1)} %slice.48), channel_id=1, source_target_pairs={{8,0},{9,1},{10,2},{11,3},{12,4},{13,5},{14,6},{15,7},{24,16},{25,... | collective-permute-start | bytes 1544 | tf_op jit(solution)/shard_map/ppermute | solution.py:881
  185.7 8.6 %collective-permute-start.29 = (f32[8,2048]{1,0:T(8,128)S(1)}, f32[8,2048]{1,0:T(8,128)S(1)}, u32[]{:S(2)}, u32[]{:S(2)}) collective-permute-start(f32[8,2048]{1,0:T(8,128)S(1)} %added.10.refs_0_), channel_id=1, source_target_pairs={{0,8},{1,9},{2,10},{3,11},{4,12},{5,13},{6,14},{7,15},{8,0},{9,1},... | collective-permute-start | bytes 196616 | tf_op jit(solution)/shard_map/ppermute | solution.py:745
  (58 other events, 489.4 us)

commit v3 on v2

--- a/solution.py
+++ b/solution.py
@@ -18,6 +18,7 @@
 EARLY = REACH - BLOCK
 COVERED = EARLY + 2 * BLOCK
 STATS = 16
+SPARE = 16
 UNROLL = 8
 f32 = jnp.float32
 bf16 = jnp.bfloat16
@@ -94,7 +95,8 @@
 
 
 def add_kernel(a_ref, b_ref, out_ref):
-    out_ref[...] = (a_ref[...].astype(f32) + b_ref[...].astype(f32)).astype(out_ref.dtype)
+    b = b_ref[...] if b_ref.shape == a_ref.shape else b_ref[:, : a_ref.shape[1]]
+    out_ref[...] = (a_ref[...].astype(f32) + b.astype(f32)).astype(out_ref.dtype)
 
 
 def added(a, b, waits=()):
@@ -105,19 +107,27 @@
     return [ref.at[i] for ref in refs for i in range(ref.shape[0])]
 
 
-def halve_kernel(*refs):
+def halve_kernel(*refs, width):
     *in_refs, first_stays, first_goes, second_stays, second_goes = refs
     n = len(in_refs) // 4
     parts = [blocks_of(in_refs[n * i : n * (i + 1)]) for i in range(4)]
-    outs = (blocks_of((first_stays, first_goes)), blocks_of((second_stays, second_goes)))
-    for kept, got, out in zip(parts[:2], parts[2:], outs):
-        for kept_ref, got_ref, out_ref in zip(kept, got, out):
-            out_ref[...] = (kept_ref[...].astype(f32) + got_ref[...].astype(f32)).astype(bf16)
-
-
-def halve(kept, got, waits=()):
+    for part, (stays, goes) in enumerate(((first_stays, first_goes), (second_stays, second_goes))):
+        out = blocks_of([stays, goes])
+        for out_ref, a_ref, b_ref in zip(out, parts[part], parts[2 + part]):
+            out_ref[:, :, :width] = (a_ref[:, :, :width].astype(f32) + b_ref[:, :, :width].astype(f32)).astype(bf16)
+            there = a_ref.shape[2]
+            if there > width:
+                out_ref[:, :, width:there] = a_ref[:, :, width:]
+                out_ref[:, :, there:] = b_ref[:, :, width:]
+
+
+def halve(kept, got, width, waits=()):
     n = sum(value.shape[0] for value in kept) // 4
-    out = call(halve_kernel, [((n, *kept[0].shape[1:]), bf16)] * 4, (*kept, *got), waits=waits, name="halve")
+    *shape, there = kept[0].shape[1:]
+    out = call(
+        functools.partial(halve_kernel, width=width), [((n, *shape, 2 * there - width), bf16)] * 4, (*kept, *got),
+        waits=waits, name="halve",
+    )
     return out[0::2], out[1::2]
 
 
@@ -135,18 +145,26 @@
     return call(merge_kernel, [(own.shape, bf16)], (own, away, *got), waits=waits, name="merge")[0]
 
 
-def finish_kernel(where_ref, *refs):
-    *in_refs, out_ref = refs
-    width = in_refs[0].shape[-1]
+def finish_kernel(where_ref, *refs, sources):
+    in_refs, (out_ref, *hidden_ref) = refs[:4], refs[4:]
+    half_width = out_ref.shape[2] // 2
     for part in range(2):
         kept_ref, got_ref = in_refs[part], in_refs[2 + part]
-        lane = pl.ds(pl.multiple_of((where_ref[0] ^ part) * width, LANES), width)
-        out_ref[:, :, lane] = (kept_ref[0].astype(f32) + got_ref[0].astype(f32)).astype(bf16)
-
-
-def finish(where, kept, got, waits=()):
-    _, rows, block, width = kept[0].shape
-    return call(finish_kernel, [((rows, block, 2 * width), bf16)], (*kept, *got), (where,), waits, name="finish")[0]
+        value = kept_ref[0, :, :, :half_width].astype(f32) + got_ref[0, :, :, :half_width].astype(f32)
+        lane = pl.multiple_of((where_ref[0] ^ part) * half_width, LANES)
+        out_ref[:, :, pl.ds(lane, half_width)] = value.astype(bf16)
+        if hidden_ref:
+            tiles = [ref[0, :, :, at : at + LANES] for ref in (kept_ref, got_ref) for at in range(half_width, ref.shape[3], LANES)]
+            for value, source in zip(tiles, sources[part]):
+                lane = pl.multiple_of(part * half_width + (where_ref[3] ^ source) * LANES, LANES)
+                hidden_ref[0][:, :, pl.ds(lane, LANES)] = value
+
+
+def finish(where, kept, got, features, sources, waits=()):
+    _, rows, block, there = kept[0].shape
+    out_shape = [((rows, block, features), bf16)] * (1 + (there > features // 2))
+    kernel = functools.partial(finish_kernel, sources=sources)
+    return call(kernel, out_shape, (*kept, *got), (where,), waits, name="finish")
 
 
 def stats_kernel(x_ref, keep_ref, out_ref):
@@ -612,25 +630,30 @@
                 out_ref = next(outs)
                 for n in range(devices):
                     row = n * row_block + start
-                    out_ref[k * devices + n] = p[row : row + step, split * columns : (split + 1) * columns]
+                    out_ref[k * devices + n, :step] = p[row : row + step, split * columns : (split + 1) * columns]
+                    if out_ref.shape[1] > step:
+                        out_ref[k * devices + n, step:] = jnp.zeros((out_ref.shape[1] - step, columns), bf16)
                 start += step
 
 
-def weight_back(normed, gp, sums, weights, part, group, cuts, waits):
+def weight_back(normed, gp, sums, weights, part, group, cuts, waits, spare=0):
     features = normed.shape[2]
     columns = gp.shape[2] // len(cuts)
     kernel = functools.partial(weight_back_kernel, part=part, group=group, cuts=cuts)
     out_shape = [((2, features // 2), f32)] + [((group, step, columns), bf16) for rows in cuts for step in rows]
+    (count, step, width), dtype = out_shape[-1]
+    out_shape[-1] = ((count, step + spare, width), dtype)
     return call(kernel, out_shape, (normed, gp, sums, *weights), waits=waits, name="weight_back")
 
 
-def norm_back_kernel(where_ref, stats_ref, means_ref, gp_ref, gain_ref, *refs, orders, with_high):
+def norm_back_kernel(where_ref, stats_ref, means_ref, gp_ref, gain_ref, *refs, orders, with_hidden):
     count = len(orders[0])
     x_refs, refs = refs[: 2 * count], refs[2 * count :]
-    *w_refs, high_ref = refs[:-10]
+    *w_refs, high_ref, hidden_ref = refs[:-10]
     all_out_refs, (some_ref, gn_ref) = refs[-10:-2], refs[-2:]
-    half_count, total, block, half_width = all_out_refs[0].shape
-    features = 2 * half_width
+    half_count, total, block, _ = all_out_refs[0].shape
+    features = gain_ref.shape[1]
+    half_width = features // 2
     together = gn_ref.shape[0] // block
     for odd in (1, 0):
         out_refs = all_out_refs[4 * (1 - odd) : 4 * (2 - odd)]
@@ -661,26 +684,29 @@
                         at_d = orders[part].index(orders[0][d + n])
                         out_ref = out_refs[2 * part + at_d // half_count]
                         start = pl.multiple_of((where_ref[0] ^ part) * half_width, LANES)
-                        if with_high:
+                        if with_hidden:
                             high = high_ref[r, where_ref[0] ^ part, tokens[n], :].astype(f32)
                         for j in range(half_width // LANES):
                             at = slice(part * half_width + LANES * j, part * half_width + LANES * (j + 1))
                             value = inv * (gn_ref[n * block : (n + 1) * block, at] * gain_ref[:, at])
                             x = x_ref[r, :block, pl.ds(start + LANES * j, LANES)].astype(f32)
                             value -= slope * x + rest
-                            if with_high:
+                            if with_hidden:
                                 value += jnp.where(where_ref[3] == j, high, 0.0)
                             out_ref[at_d % half_count, r, :, LANES * j : LANES * (j + 1)] = value.astype(bf16)
-
-
-def norm_back(where, blocks, orders, stats, means, gp, weights, gain, high, with_high, waits):
+                        if with_hidden:
+                            hidden = hidden_ref[where_ref[3] ^ (orders[0][d + n] | odd), r]
+                            out_ref[at_d % half_count, r, :, half_width:] = hidden[:, LANES * part : LANES * (part + 1)]
+
+
+def norm_back(where, blocks, orders, stats, means, gp, weights, gain, high, hidden, with_hidden, waits):
     rows, block, features = blocks[0].shape
     block -= STATS
     together = 2 * LANES // block
     out = call(
-        functools.partial(norm_back_kernel, orders=orders, with_high=with_high),
-        [((len(blocks) // 4, rows, block, features // 2), bf16)] * 8,
-        (stats, means, gp, gain, *blocks, *weights, high), (where,), waits,
+        functools.partial(norm_back_kernel, orders=orders, with_hidden=with_hidden),
+        [((len(blocks) // 4, rows, block, features // 2 + with_hidden * LANES), bf16)] * 8,
+        (stats, means, gp, gain, *blocks, *weights, high, hidden), (where,), waits,
         scratch=[((together * block, gp.shape[2]), bf16), ((together * block, features), f32)],
         name="norm_back",
     )
@@ -818,11 +844,12 @@
     mask = (jnp.arange(group) == place)[:, None]
 
     splits = 2 if paired else 1
-    by_feature_other, *away = weight_back(normed, gp, sums, weights, 1, group, [(row_block,)] * splits, ())
+    by_feature_other, *away = weight_back(normed, gp, sums, weights, 1, group, [(row_block,)] * splits, (), SPARE * paired)
     away_got = swapped(away[1]) if paired else None
 
     sent, kept = norm_back(
-        where, blocks, orders, token_stats, means, gp, weights, gain_row, high_own, aligned, (by_feature_other,)
+        where, blocks, orders, token_stats, means, gp, weights, gain_row, high_own, hidden_own, aligned,
+        (by_feature_other,),
     )
     if not aligned:
         spread = high_own.swapaxes(1, 2).reshape(rows, group, block_len, chunks, 1, piece).swapaxes(0, 1)
@@ -842,7 +869,7 @@
     else:
         away = lax.psum_scatter(away[0], "dp", scatter_dimension=2, tiled=True)
     z_got = across(away)
-    kept, sent = halve(kept, got)
+    kept, sent = halve(kept, got, features // 2)
     bit_pairs = list(zip(*(w[::-1] for w in ways)))
     got = [flipped(value, bit) for value, bit in zip(sent, bit_pairs.pop(0))]
     cuts = [(row_block,), (row_block // 2,) * 2][:splits]
@@ -851,8 +878,6 @@
         here_got = [swapped(value) for value in here[1:]]
     else:
         here = lax.psum_scatter(here[0], "dp", scatter_dimension=2, tiled=True)
-    hidden = collected([shared(hidden_own).reshape(group, -1, width)], bf16).reshape(rows, block_len, features)
-
     if aligned:
         totals = call(
             functools.partial(totals_kernel, chunk=chunk), [((8, features), f32)],
@@ -864,12 +889,21 @@
         gain_sum = (product - shift_row[0] * shift_sum) / gain_row[0]
         totals = jnp.concatenate([spread, halves_turned(jnp.stack([gain_sum, shift_sum]))], axis=0)
     for way in bit_pairs:
-        kept, sent = halve(kept, got, (hidden,))
+        kept, sent = halve(kept, got, features // 2)
         got = [flipped(value, bit) for value, bit in zip(sent, way)]
-    grad_inputs = finish(where, kept, got)
+    sources = []
+    for way in ways:
+        sources.append([0])
+        for bit in (1, *way[::-1]):
+            sources[-1] += [d | bit for d in sources[-1]]
+    grad_inputs, *hidden = finish(where, kept, got, features, sources)
+    if aligned:
+        hidden = hidden[0]
+    else:
+        hidden = collected([shared(hidden_own).reshape(group, -1, width)], bf16).reshape(rows, block_len, features)
     for bit in [1 << b for b in range(group.bit_length() - 1)]:
         totals = added(totals, flipped(totals, bit))
-    waits = (grad_inputs, totals)
+    waits = (*got, totals)
     value = merge(here[0], here_got, z_got, waits) if paired else added(here, z_got, waits)
     grad_weight = collected([shared(value)], f32)
     totals = added(totals, swapped(totals)) if ranks == 2 else lax.psum(totals, "dp")

time: 197 us -> 185 us (0.939)
  waiting for transfers between devices: 63.1 us -> 84.3 us
  local copies, waits for them, and re-layouts: 22.2 us -> 3.65 us
  Pallas kernels: 56.1 us -> 47.7 us
  starting transfers between devices: 50.4 us -> 45.8 us
    unnamed x112 -> x26, local copies, waits for them, and re-layouts: 19.4 us -> 2.08 us
    ppermute x18, waiting for transfers between devices: 37.7 us -> 54.4 us  [flipped(): return lax.ppermute(value, 'fsdp', [(j, j ^ bit) for j in range(sections)])]
    pallas_call x25 -> x24, Pallas kernels: 56.1 us -> 47.7 us  [call(): pl.pallas_call(body, in_specs=[in_smem] * len(scalars) + [in_vmem] * len(...]
    all_to_all x4 -> x3, starting transfers between devices: 18.2 us -> 12.7 us  [shared(): lax.all_to_all(value, 'fsdp', 0, 0, tiled=True, axis_index_groups=groups)]
    ppermute x6, waiting for transfers between devices: 1.13 us -> 5.59 us  [swapped(): return lax.ppermute(value, 'dp', [(0, 1), (1, 0)])]
    all_to_all x4 -> x3, waiting for transfers between devices: 11.1 us -> 11.1 us  [shared(): lax.all_to_all(value, 'fsdp', 0, 0, tiled=True, axis_index_groups=groups)]
  transfers between devices with their start and end apart: 34 -> 33, of which waited for: 13 -> 22; matrix products, arithmetic and copies ran while one was open for 3% -> 2% of each run, Pallas kernels for 16% -> 13%
where the time goes in v3:
time: 185 us; the launch traced here: 184 us
  waiting for transfers between devices  84.3 us (46%)
  Pallas kernels  47.7 us (26%)
  starting transfers between devices  45.8 us (25%)
  local copies, waits for them, and re-layouts  3.65 us (2%)
  other arithmetic  2.06 us (1%)
    ppermute x18, waiting for transfers between devices, flipped(): return lax.ppermute(value, 'fsdp', [(j, j ^ bit) for j in range(sections)])  54.4 us
    pallas_call x24, Pallas kernels, call(): pl.pallas_call(body, in_specs=[in_smem] * len(scalars) + [in_vmem] * len(...  47.7 us
    all_to_all x3, starting transfers between devices, shared(): lax.all_to_all(value, 'fsdp', 0, 0, tiled=True, axis_index_groups=groups)  12.7 us
    ppermute x18, starting transfers between devices, flipped(): return lax.ppermute(value, 'fsdp', [(j, j ^ bit) for j in range(sections)])  12.2 us
    ppermute x5, starting transfers between devices, across(): lax.ppermute(value, 'fsdp', [(j, (j + group) % sections) for j in range(s...  12.2 us
    all_to_all x3, waiting for transfers between devices, shared(): lax.all_to_all(value, 'fsdp', 0, 0, tiled=True, axis_index_groups=groups)  11.1 us
    ppermute x5, waiting for transfers between devices, across(): lax.ppermute(value, 'fsdp', [(j, (j + group) % sections) for j in range(s...  7.6 us
    ppermute x6, starting transfers between devices, swapped(): return lax.ppermute(value, 'dp', [(0, 1), (1, 0)])  7.29 us
  transfers between devices with their start and end apart: 33, of which 22 were waited for; matrix products, arithmetic and copies ran while one was open for 2% of the time, Pallas kernels for 13%

profile of v3, /device:TPU:8, one launch (start us, length us, event | category | flops | bytes accessed | tf_op | source)
XLA Modules:
  0.0 184.4 jit_solution(16023859610677736047)
XLA Ops:
  2.8 4.4 %all-to-all-start = ((bf16[8,128,384]{2,1,0:T(8,128)(2,1)}), bf16[8,128,384]{2,1,0:T(8,128)(2,1)S(1)}, u32[]{:S(2)}, u32[]{:S(2)}) async-start(bf16[8,128,384]{2,1,0:T(8,128)(2,1)} %deal.2), calls=%async_computation | async-start | bytes 1572864 | tf_op jit(solution)/shard_map/all_to_all | solution.py:780
  7.2 11.1 %all-to-all-done.refs_2_.refs_3_ = bf16[8,128,384]{2,1,0:T(8,128)(2,1)S(1)} async-done(((bf16[8,128,384]{2,1,0:T(8,128)(2,1)}), bf16[8,128,384]{2,1,0:T(8,128)(2,1)S(1)}, u32[]{:S(2)}, u32[]{:S(2)}) %all-to-all-start) | async-done | bytes 786464 | tf_op jit(solution)/shard_map/all_to_all | solution.py:780
  19.3 2.6 %collective-permute-start = (bf16[8,128,384]{2,1,0:T(8,128)(2,1)S(1)}, bf16[8,128,384]{2,1,0:T(8,128)(2,1)S(1)}, u32[]{:S(2)}, u32[]{:S(2)}) collective-permute-start(bf16[8,128,384]{2,1,0:T(8,128)(2,1)S(1)} %all-to-all-done.refs_2_.refs_3_), channel_id=1, source_target_pairs={{0,8},{1,9},{2,10},{3,11},{4,12},{5,13},{6,14},{7,15},{8,0},{9,1},... | collective-permute-start | bytes 2359304 | tf_op jit(solution)/shard_map/ppermute | solution.py:771
  22.7 4.9 %all-to-all-start.1 = ((bf16[8,1,128,256]{3,2,1,0:T(8,128)(2,1)}), bf16[8,1,128,256]{3,2,1,0:T(8,128)(2,1)S(1)}, u32[]{:S(2)}, u32[]{:S(2)}) async-start(bf16[8,1,128,256]{3,2,1,0:T(8,128)(2,1)} %bitcast.9), calls=%async_computation.1 | async-start | bytes 1048576 | tf_op jit(solution)/shard_map/all_to_all | solution.py:780
  30.6 15.8 %collective-permute-done.5.refs_0_ = bf16[1,144,2048]{2,1,0:T(8,128)(2,1)} collective-permute-done((bf16[1,144,2048]{2,1,0:T(8,128)(2,1)S(1)}, bf16[1,144,2048]{2,1,0:T(8,128)(2,1)}, u32[]{:S(2)}, u32[]{:S(2)}) %collective-permute-start.5) | collective-permute-done | bytes 589856 | tf_op jit(solution)/shard_map/ppermute | solution.py:774
  48.8 6.3 %collective-permute-done.refs_1_.refs_9_ = bf16[8,128,384]{2,1,0:T(8,128)(2,1)S(1)} collective-permute-done((bf16[8,128,384]{2,1,0:T(8,128)(2,1)S(1)}, bf16[8,128,384]{2,1,0:T(8,128)(2,1)S(1)}, u32[]{:S(2)}, u32[]{:S(2)}) %collective-permute-start) | collective-permute-done | bytes 786464 | tf_op jit(solution)/shard_map/ppermute | solution.py:771
  58.1 4.1 %collective-permute-done.7.refs_0_ = bf16[1,144,2048]{2,1,0:T(8,128)(2,1)} collective-permute-done((bf16[1,144,2048]{2,1,0:T(8,128)(2,1)}, bf16[1,144,2048]{2,1,0:T(8,128)(2,1)}, u32[]{:S(2)}, u32[]{:S(2)}) %collective-permute-start.7) | collective-permute-done | bytes 589856 | tf_op jit(solution)/shard_map/ppermute | solution.py:774
  65.4 4.4 %norm.1 = (bf16[1,1024,2048]{2,1,0:T(8,128)(2,1)S(1)}, f32[1,2,1024,128]{3,2,1,0:T(8,128)S(1)}, f32[1,1088,128]{2,1,0:T(8,128)S(1)}, bf16[1,2,1024,128]{3,2,1,0:T(8,128)(2,1)S(1)}) custom-call(s32[5]{0:T(128)S(1)} %stack.23.refs_0_, f32[1,2048]{1,0:T(1,128)S(1)} %bitcast.42, f32[1,2048]{1,0:T(1,128)S(1)} %bitcast.45, bf16[1,144,2048]{2,1,0:T(8,128)(2,1)S(1)} %copy-done.6, ...), custom_call_target="tpu_custom_call" | custom-call | tf_op jit(solution)/shard_map/norm/pallas_call | solution.py:42
  69.8 3.2 %project.1 = (f32[1,6,1024,128]{3,2,1,0:T(8,128)S(1)}, f32[16,768]{1,0:T(8,128)S(1)}, bf16[1024,768]{1,0:T(8,128)(2,1)S(1)}) custom-call(s32[5]{0:T(128)S(1)} %stack.23.refs_0_, bf16[1,1024,2048]{2,1,0:T(8,128)(2,1)S(1)} %get-tuple-element.58.refs_1_.refs_0_, bf16[16,2048]{1,0:T(8,128)(2,1)S(1)} %pad.4.refs_2_, ...), custom_call_target="tpu_custom_call" | custom-call | tf_op jit(solution)/shard_map/project/pallas_call | solution.py:42
  73.1 7.8 %blocks_forward.1 = (f32[1,6,1088,128]{3,2,1,0:T(8,128)S(1)}, f32[1,2,1088,128]{3,2,1,0:T(8,128)S(1)}, f32[1,2,336,128]{3,2,1,0:T(8,128)S(1)}, f32[1,1,256]{2,1,...) custom-call(s32[5]{0:T(128)S(1)} %stack.23.refs_0_, ...), custom_call_target="tpu_custom_call" | custom-call | tf_op jit(solution)/shard_map/blocks_forward/pallas_call | solution.py:42
  80.9 3.4 %collective-permute-start.10 = (f32[1,1,256]{2,1,0:T(1,128)S(1)}, f32[1,1,256]{2,1,0:T(1,128)S(1)}, u32[]{:S(2)}, u32[]{:S(2)}) collective-permute-start(f32[1,1,256]{2,1,0:T(1,128)S(1)} %get-tuple-element.67), channel_id=1, source_target_pairs={{0,8},{1,9},{2,10},{3,11},{4,12},{5,13},{6,14},{7,15},{8,0},{9,1},... | collective-permute-start | bytes 3080 | tf_op jit(solution)/shard_map/ppermute | solution.py:771
  85.9 2.7 %entry.1 = (f32[1,2,200,128]{3,2,1,0:T(8,128)S(1)}, f32[1,1,256]{2,1,0:T(1,128)S(1)}) custom-call(f32[1,6,1088,128]{3,2,1,0:T(8,128)S(1)} %get-tuple-element.62.refs_0_.refs_1_, f32[1,1088,128]{2,1,0:T(8,128)S(1)} %get-tuple-element.61.refs_6_.refs_1_.refs_2_, f32[1,2,1088,128]{3,2,1,0:T(8,128)S(1)} %get-tuple-element.63.refs_2_.refs_3_, ...), custom_call_target="tpu_custom_call" | custom-call | tf_op jit(solution)/shard_map/entry/pallas_call | solution.py:42
  88.6 3.0 %collective-permute-start.11 = (f32[1,1,256]{2,1,0:T(1,128)S(1)}, f32[1,1,256]{2,1,0:T(1,128)S(1)}, u32[]{:S(2)}, u32[]{:S(2)}) collective-permute-start(f32[1,1,256]{2,1,0:T(1,128)S(1)} %get-tuple-element.69), channel_id=1, source_target_pairs={{0,8},{1,9},{2,10},{3,11},{4,12},{5,13},{6,14},{7,15},{8,0},{9,1},... | collective-permute-start | bytes 3080 | tf_op jit(solution)/shard_map/ppermute | solution.py:771
  91.6 4.1 %lead_forward.1.refs_4_ = f32[1,2,816,128]{3,2,1,0:T(8,128)S(1)} custom-call(f32[1,6,1088,128]{3,2,1,0:T(8,128)S(1)} %get-tuple-element.62.refs_0_.refs_1_, f32[1,1088,128]{2,1,0:T(8,128)S(1)} %get-tuple-element.61.refs_6_.refs_1_.refs_2_, f32[1,256]{1,0:T(1,128)S(1)} %fusion.7.refs_7_.refs_2_.refs_5_.refs_8_, f32[1,1,256]{2,1,0:T(1,128)S(1)} %get-tuple-element.64.refs_3_, ...), custom_call_target="tpu_custom_call" | custom-call | tf_op jit(solution)/shard_map/lead_forward/pallas_call | solution.py:42
  95.7 6.4 %backward.1 = (bf16[1,1024,768]{2,1,0:T(8,128)(2,1)S(1)}, bf16[8,1,128,256]{3,2,1,0:T(8,128)(2,1)S(1)}, bf16[1,2,1024,128]{3,2,1,0:T(8,128)(2,1)S(1)}, f32[8,768...) custom-call(s32[5]{0:T(128)S(1)} %stack.23.refs_0_, ...), custom_call_target="tpu_custom_call" | custom-call | tf_op jit(solution)/shard_map/backward/pallas_call | solution.py:42
  102.1 2.3 %weight_back.2 = (f32[2,1024]{1,0:T(2,128)S(1)}, bf16[8,128,384]{2,1,0:T(8,128)(2,1)S(1)}, bf16[8,144,384]{2,1,0:T(8,128)(2,1)S(1)}) custom-call(bf16[1,1024,2048]{2,1,0:T(8,128)(2,1)S(1)} %get-tuple-element.58.refs_1_.refs_0_, bf16[1,1024,768]{2,1,0:T(8,128)(2,1)S(1)} %get-tuple-element.72.refs_1_.refs_3_, f32[8,768]{1,0:T(8,128)S(1)} %get-tuple-element.77.refs_2_.refs_1_, ...), custom_call_target="tpu_custom_call" | custom-call | tf_op jit(solution)/shard_map/weight_back/pallas_call | solution.py:42
  104.4 1.6 collective-permute-start.21
  106.0 6.6 %norm_back.1 = (bf16[2,1,128,1152]{3,2,1,0:T(8,128)(2,1)S(1)}, bf16[2,1,128,1152]{3,2,1,0:T(8,128)(2,1)S(1)}, bf16[2,1,128,1152]{3,2,1,0:T(8,128)(2,1)S(1)}, bf1...) custom-call(s32[5]{0:T(128)S(1)} %stack.23.refs_0_, ...), custom_call_target="tpu_custom_call" | custom-call | tf_op jit(solution)/shard_map/norm_back/pallas_call | solution.py:42
  119.2 3.0 %collective-permute-done.21.refs_1_ = bf16[8,144,384]{2,1,0:T(8,128)(2,1)S(1)} collective-permute-done((bf16[8,144,384]{2,1,0:T(8,128)(2,1)S(1)}, bf16[8,144,384]{2,1,0:T(8,128)(2,1)S(1)}, u32[]{:S(2)}, u32[]{:S(2)}) %collective-permute-start.21) | collective-permute-done | bytes 884768 | tf_op jit(solution)/shard_map/ppermute | solution.py:777
  122.4 2.0 %collective-permute-start.22 = (bf16[8,128,384]{2,1,0:T(8,128)(2,1)S(1)}, bf16[8,128,384]{2,1,0:T(8,128)(2,1)S(1)}, u32[]{:S(2)}, u32[]{:S(2)}) collective-permute-start(bf16[8,128,384]{2,1,0:T(8,128)(2,1)S(1)} %added.6.refs_5_), channel_id=1, source_target_pairs={{0,8},{1,9},{2,10},{3,11},{4,12},{5,13},{6,14},{7,15},{8,0},{9,1},... | collective-permute-start | bytes 2359304 | tf_op jit(solution)/shard_map/ppermute | solution.py:771
  124.4 2.3 %weight_back.3 = (f32[2,1024]{1,0:T(2,128)S(1)}, bf16[8,128,384]{2,1,0:T(8,128)(2,1)S(1)}, bf16[8,64,384]{2,1,0:T(8,128)(2,1)S(1)}, bf16[8,64,384]{2,1,0:T(8,128)(2,1)S(1)}) custom-call(bf16[1,1024,2048]{2,1,0:T(8,128)(2,1)S(1)} %get-tuple-element.58.refs_1_.refs_0_, bf16[1,1024,768]{2,1,0:T(8,128)(2,1)S(1)} %get-tuple-element.72.refs_1_.refs_3_, ...), custom_call_target="tpu_custom_call" | custom-call | tf_op jit(solution)/shard_map/weight_back/pallas_call | solution.py:42
  128.6 1.7 collective-permute-start.26
  130.3 5.6 %collective-permute-done.26.refs_1_ = f32[8,2048]{1,0:T(8,128)S(1)} collective-permute-done((f32[8,2048]{1,0:T(8,128)S(1)}, f32[8,2048]{1,0:T(8,128)S(1)}, u32[]{:S(2)}, u32[]{:S(2)}) %collective-permute-start.26) | collective-permute-done | bytes 65568 | tf_op jit(solution)/shard_map/ppermute | solution.py:774
  138.1 6.9 %collective-permute-done.17.refs_3_ = bf16[2,1,128,1280]{3,2,1,0:T(8,128)(2,1)S(1)} collective-permute-done((bf16[2,1,128,1280]{3,2,1,0:T(8,128)(2,1)S(1)}, bf16[2,1,128,1280]{3,2,1,0:T(8,128)(2,1)S(1)}, u32[]{:S(2)}, u32[]{:S(2)}) %collective-permute-start.17) | collective-permute-done | bytes 655392 | tf_op jit(solution)/shard_map/ppermute | solution.py:774
  145.3 2.5 %collective-permute-start.18 = (bf16[1,1,128,1536]{3,2,1,0:T(8,128)(2,1)S(1)}, bf16[1,1,128,1536]{3,2,1,0:T(8,128)(2,1)S(1)}, u32[]{:S(2)}, u32[]{:S(2)}) collective-permute-start(bf16[1,1,128,1536]{3,2,1,0:T(8,128)(2,1)S(1)} %get-tuple-element.93), channel_id=1, source_target_pairs={{0,4},{1,5},{2,6},{3,7},{4,0},{5,1},{6,2},{7,3},{8,12},{9,13},{10,... | collective-permute-start | bytes 1179656 | tf_op jit(solution)/shard_map/ppermute | solution.py:774
  147.8 7.3 %collective-permute-done.27.refs_1_ = f32[8,2048]{1,0:T(8,128)S(1)} collective-permute-done((f32[8,2048]{1,0:T(8,128)S(1)}, f32[8,2048]{1,0:T(8,128)S(1)}, u32[]{:S(2)}, u32[]{:S(2)}) %collective-permute-start.27) | collective-permute-done | bytes 65568 | tf_op jit(solution)/shard_map/ppermute | solution.py:774
  155.7 6.7 %collective-permute-done.18.refs_3_.refs_4_ = bf16[1,1,128,1536]{3,2,1,0:T(8,128)(2,1)S(1)} collective-permute-done((bf16[1,1,128,1536]{3,2,1,0:T(8,128)(2,1)S(1)}, bf16[1,1,128,1536]{3,2,1,0:T(8,128)(2,1)S(1)}, u32[]{:S(2)}, u32[]{:S(2)}) %collective-permute-start.18) | collective-permute-done | bytes 393248 | tf_op jit(solution)/shard_map/ppermute | solution.py:774
  162.4 1.6 collective-permute-done.19.refs_4_.refs_5_
  165.2 3.5 %all-to-all-start.2 = ((bf16[8,128,384]{2,1,0:T(8,128)(2,1)}), bf16[8,128,384]{2,1,0:T(8,128)(2,1)S(1)}, u32[]{:S(2)}, u32[]{:S(2)}) async-start(bf16[8,128,384]{2,1,0:T(8,128)(2,1)} %merge.1), calls=%async_computation.2 | async-start | bytes 1572864 | tf_op jit(solution)/shard_map/all_to_all | solution.py:780
  170.5 2.5 %collective-permute-done.28.refs_1_ = f32[8,2048]{1,0:T(8,128)S(1)} collective-permute-done((f32[8,2048]{1,0:T(8,128)S(1)}, f32[8,2048]{1,0:T(8,128)S(1)}, u32[]{:S(2)}, u32[]{:S(2)}) %collective-permute-start.28) | collective-permute-done | bytes 65568 | tf_op jit(solution)/shard_map/ppermute | solution.py:777
  174.2 5.6 %collective-permute-done.20 = f32[1,128]{1,0:T(1,128)S(1)} collective-permute-done((f32[1,128]{1,0:T(1,128)S(1)}, f32[1,128]{1,0:T(1,128)S(1)}, u32[]{:S(2)}, u32[]{:S(2)}) %collective-permute-start.20) | collective-permute-done | bytes 544 | tf_op jit(solution)/shard_map/ppermute | solution.py:915
  181.4 1.7 finish.1
  (108 shorter events, 36.0 us)
Async XLA Ops:
  2.8 15.5 %all-to-all-start = ((bf16[8,128,384]{2,1,0:T(8,128)(2,1)}), bf16[8,128,384]{2,1,0:T(8,128)(2,1)S(1)}, u32[]{:S(2)}, u32[]{:S(2)}) async-start(bf16[8,128,384]{2,1,0:T(8,128)(2,1)} %deal.2), calls=%async_computation | async-start | bytes 1572864 | tf_op jit(solution)/shard_map/all_to_all | solution.py:780
  18.6 27.8 %collective-permute-start.5 = (bf16[1,144,2048]{2,1,0:T(8,128)(2,1)S(1)}, bf16[1,144,2048]{2,1,0:T(8,128)(2,1)}, u32[]{:S(2)}, u32[]{:S(2)}) collective-permute-start(bf16[1,144,2048]{2,1,0:T(8,128)(2,1)S(1)} %stats.1.refs_0_), channel_id=1, source_target_pairs={{0,4},{1,5},{2,6},{3,7},{4,0},{5,1},{6,2},{7,3},{8,12},{9,13},{10,... | collective-permute-start | bytes 1769480 | tf_op jit(solution)/shard_map/ppermute | solution.py:774
  19.3 35.8 %collective-permute-start = (bf16[8,128,384]{2,1,0:T(8,128)(2,1)S(1)}, bf16[8,128,384]{2,1,0:T(8,128)(2,1)S(1)}, u32[]{:S(2)}, u32[]{:S(2)}) collective-permute-start(bf16[8,128,384]{2,1,0:T(8,128)(2,1)S(1)} %all-to-all-done.refs_2_.refs_3_), channel_id=1, source_target_pairs={{0,8},{1,9},{2,10},{3,11},{4,12},{5,13},{6,14},{7,15},{8,0},{9,1},... | collective-permute-start | bytes 2359304 | tf_op jit(solution)/shard_map/ppermute | solution.py:771
  22.7 40.9 %all-to-all-start.1 = ((bf16[8,1,128,256]{3,2,1,0:T(8,128)(2,1)}), bf16[8,1,128,256]{3,2,1,0:T(8,128)(2,1)S(1)}, u32[]{:S(2)}, u32[]{:S(2)}) async-start(bf16[8,1,128,256]{3,2,1,0:T(8,128)(2,1)} %bitcast.9), calls=%async_computation.1 | async-start | bytes 1048576 | tf_op jit(solution)/shard_map/all_to_all | solution.py:780
  27.6 29.1 %collective-permute-start.3 = (bf16[1,144,2048]{2,1,0:T(8,128)(2,1)S(1)}, bf16[1,144,2048]{2,1,0:T(8,128)(2,1)}, u32[]{:S(2)}, u32[]{:S(2)}) collective-permute-start(bf16[1,144,2048]{2,1,0:T(8,128)(2,1)S(1)} %stats.1.refs_0_), channel_id=1, source_target_pairs={{0,2},{1,3},{2,0},{3,1},{4,6},{5,7},{6,4},{7,5},{8,10},{9,11},{10,... | collective-permute-start | bytes 1769480 | tf_op jit(solution)/shard_map/ppermute | solution.py:774
  29.1 27.6 %collective-permute-start.1 = (bf16[8,128,384]{2,1,0:T(8,128)(2,1)S(1)}, bf16[8,128,384]{2,1,0:T(8,128)(2,1)S(1)}, u32[]{:S(2)}, u32[]{:S(2)}) collective-permute-start(bf16[8,128,384]{2,1,0:T(8,128)(2,1)S(1)} %all-to-all-done.refs_2_.refs_3_), channel_id=1, source_target_pairs={{0,16},{16,0},{1,17},{17,1},{2,18},{18,2},{3,19},{19,3},{4,20},{20... | collective-permute-start | bytes 2359304 | tf_op jit(solution)/shard_map/ppermute | solution.py:777
  46.4 15.7 %collective-permute-start.7 = (bf16[1,144,2048]{2,1,0:T(8,128)(2,1)}, bf16[1,144,2048]{2,1,0:T(8,128)(2,1)}, u32[]{:S(2)}, u32[]{:S(2)}) collective-permute-start(bf16[1,144,2048]{2,1,0:T(8,128)(2,1)} %collective-permute-done.5.refs_0_), channel_id=1, source_target_pairs={{0,2},{1,3},{2,0},{3,1},{4,6},{5,7},{6,4},{7,5},{8,10},{9,11},{10,... | collective-permute-start | bytes 1769480 | tf_op jit(solution)/shard_map/ppermute | solution.py:774
  55.1 18.0 %collective-permute-start.9 = (bf16[8,128,384]{2,1,0:T(8,128)(2,1)S(1)}, bf16[8,128,384]{2,1,0:T(8,128)(2,1)}, u32[]{:S(2)}, u32[]{:S(2)}) collective-permute-start(bf16[8,128,384]{2,1,0:T(8,128)(2,1)S(1)} %collective-permute-done.refs_1_.refs_9_), channel_id=1, source_target_pairs={{0,16},{16,0},{1,17},{17,1},{2,18},{18,2},{3,19},{19,3},{4,20},{20... | collective-permute-start | bytes 2359304 | tf_op jit(solution)/shard_map/ppermute | solution.py:777
  57.6 6.0 %collective-permute-start.4 = (bf16[1,144,2048]{2,1,0:T(8,128)(2,1)}, bf16[1,144,2048]{2,1,0:T(8,128)(2,1)}, u32[]{:S(2)}, u32[]{:S(2)}) collective-permute-start(bf16[1,144,2048]{2,1,0:T(8,128)(2,1)} %fence.5.refs_5_.refs_7_), channel_id=1, source_target_pairs={{0,1},{1,0},{2,3},{3,2},{4,5},{5,4},{6,7},{7,6},{8,9},{9,8},{10,11... | collective-permute-start | bytes 1769480 | tf_op jit(solution)/shard_map/ppermute | solution.py:774
  57.6 6.1 %collective-permute-start.2 = (bf16[1,144,2048]{2,1,0:T(8,128)(2,1)}, bf16[1,144,2048]{2,1,0:T(8,128)(2,1)S(1)}, u32[]{:S(2)}, u32[]{:S(2)}) collective-permute-start(bf16[1,144,2048]{2,1,0:T(8,128)(2,1)} %fence.4.refs_3_.refs_5_), channel_id=1, source_target_pairs={{0,1},{1,0},{2,3},{3,2},{4,5},{5,4},{6,7},{7,6},{8,9},{9,8},{10,11... | collective-permute-start | bytes 1769480 | tf_op jit(solution)/shard_map/ppermute | solution.py:774
  62.2 2.3 %collective-permute-start.8 = (bf16[1,144,2048]{2,1,0:T(8,128)(2,1)}, bf16[1,144,2048]{2,1,0:T(8,128)(2,1)}, u32[]{:S(2)}, u32[]{:S(2)}) collective-permute-start(bf16[1,144,2048]{2,1,0:T(8,128)(2,1)} %fence.7.refs_9_.refs_11_), channel_id=1, source_target_pairs={{0,1},{1,0},{2,3},{3,2},{4,5},{5,4},{6,7},{7,6},{8,9},{9,8},{10,11... | collective-permute-start | bytes 1769480 | tf_op jit(solution)/shard_map/ppermute | solution.py:774
  62.2 3.2 %collective-permute-start.6 = (bf16[1,144,2048]{2,1,0:T(8,128)(2,1)}, bf16[1,144,2048]{2,1,0:T(8,128)(2,1)}, u32[]{:S(2)}, u32[]{:S(2)}) collective-permute-start(bf16[1,144,2048]{2,1,0:T(8,128)(2,1)} %fence.6.refs_7_.refs_9_), channel_id=1, source_target_pairs={{0,1},{1,0},{2,3},{3,2},{4,5},{5,4},{6,7},{7,6},{8,9},{9,8},{10,11... | collective-permute-start | bytes 1769480 | tf_op jit(solution)/shard_map/ppermute | solution.py:774
  80.9 5.0 %collective-permute-start.10 = (f32[1,1,256]{2,1,0:T(1,128)S(1)}, f32[1,1,256]{2,1,0:T(1,128)S(1)}, u32[]{:S(2)}, u32[]{:S(2)}) collective-permute-start(f32[1,1,256]{2,1,0:T(1,128)S(1)} %get-tuple-element.67), channel_id=1, source_target_pairs={{0,8},{1,9},{2,10},{3,11},{4,12},{5,13},{6,14},{7,15},{8,0},{9,1},... | collective-permute-start | bytes 3080 | tf_op jit(solution)/shard_map/ppermute | solution.py:771
  88.6 7.1 %collective-permute-start.11 = (f32[1,1,256]{2,1,0:T(1,128)S(1)}, f32[1,1,256]{2,1,0:T(1,128)S(1)}, u32[]{:S(2)}, u32[]{:S(2)}) collective-permute-start(f32[1,1,256]{2,1,0:T(1,128)S(1)} %get-tuple-element.69), channel_id=1, source_target_pairs={{0,8},{1,9},{2,10},{3,11},{4,12},{5,13},{6,14},{7,15},{8,0},{9,1},... | collective-permute-start | bytes 3080 | tf_op jit(solution)/shard_map/ppermute | solution.py:771
  104.4 17.7 %collective-permute-start.21 = (bf16[8,144,384]{2,1,0:T(8,128)(2,1)S(1)}, bf16[8,144,384]{2,1,0:T(8,128)(2,1)S(1)}, u32[]{:S(2)}, u32[]{:S(2)}) collective-permute-start(bf16[8,144,384]{2,1,0:T(8,128)(2,1)S(1)} %get-tuple-element.99), channel_id=1, source_target_pairs={{0,16},{16,0},{1,17},{17,1},{2,18},{18,2},{3,19},{19,3},{4,20},{20... | collective-permute-start | bytes 2654216 | tf_op jit(solution)/shard_map/ppermute | solution.py:777
  112.6 2.1 %collective-permute-start.12 = (bf16[2,1,128,1152]{3,2,1,0:T(8,128)(2,1)S(1)}, bf16[2,1,128,1152]{3,2,1,0:T(8,128)(2,1)S(1)}, u32[]{:S(2)}, u32[]{:S(2)}) collective-permute-start(bf16[2,1,128,1152]{3,2,1,0:T(8,128)(2,1)S(1)} %get-tuple-element.83), channel_id=1, source_target_pairs={{0,1},{1,0},{2,3},{3,2},{4,5},{5,4},{6,7},{7,6},{8,9},{9,8},{10,11... | collective-permute-start | bytes 1769480 | tf_op jit(solution)/shard_map/ppermute | solution.py:774
  112.7 2.8 %collective-permute-start.13 = (bf16[2,1,128,1152]{3,2,1,0:T(8,128)(2,1)S(1)}, bf16[2,1,128,1152]{3,2,1,0:T(8,128)(2,1)S(1)}, u32[]{:S(2)}, u32[]{:S(2)}) collective-permute-start(bf16[2,1,128,1152]{3,2,1,0:T(8,128)(2,1)S(1)} %get-tuple-element.84), channel_id=1, source_target_pairs={{0,1},{1,0},{2,3},{3,2},{4,5},{5,4},{6,7},{7,6},{8,9},{9,8},{10,11... | collective-permute-start | bytes 1769480 | tf_op jit(solution)/shard_map/ppermute | solution.py:774
  113.2 3.2 %collective-permute-start.14 = (bf16[2,1,128,1152]{3,2,1,0:T(8,128)(2,1)S(1)}, bf16[2,1,128,1152]{3,2,1,0:T(8,128)(2,1)S(1)}, u32[]{:S(2)}, u32[]{:S(2)}) collective-permute-start(bf16[2,1,128,1152]{3,2,1,0:T(8,128)(2,1)S(1)} %get-tuple-element.85), channel_id=1, source_target_pairs={{0,1},{1,0},{2,3},{3,2},{4,5},{5,4},{6,7},{7,6},{8,9},{9,8},{10,11... | collective-permute-start | bytes 1769480 | tf_op jit(solution)/shard_map/ppermute | solution.py:774
  113.2 3.9 %collective-permute-start.15 = (bf16[2,1,128,1152]{3,2,1,0:T(8,128)(2,1)S(1)}, bf16[2,1,128,1152]{3,2,1,0:T(8,128)(2,1)S(1)}, u32[]{:S(2)}, u32[]{:S(2)}) collective-permute-start(bf16[2,1,128,1152]{3,2,1,0:T(8,128)(2,1)S(1)} %get-tuple-element.86), channel_id=1, source_target_pairs={{0,1},{1,0},{2,3},{3,2},{4,5},{5,4},{6,7},{7,6},{8,9},{9,8},{10,11... | collective-permute-start | bytes 1769480 | tf_op jit(solution)/shard_map/ppermute | solution.py:774
  117.7 19.2 %collective-permute-start.16 = (bf16[2,1,128,1280]{3,2,1,0:T(8,128)(2,1)S(1)}, bf16[2,1,128,1280]{3,2,1,0:T(8,128)(2,1)S(1)}, u32[]{:S(2)}, u32[]{:S(2)}) collective-permute-start(bf16[2,1,128,1280]{3,2,1,0:T(8,128)(2,1)S(1)} %get-tuple-element.89), channel_id=1, source_target_pairs={{0,2},{1,3},{2,0},{3,1},{4,6},{5,7},{6,4},{7,5},{8,10},{9,11},{10,... | collective-permute-start | bytes 1966088 | tf_op jit(solution)/shard_map/ppermute | solution.py:774
  119.2 25.8 %collective-permute-start.17 = (bf16[2,1,128,1280]{3,2,1,0:T(8,128)(2,1)S(1)}, bf16[2,1,128,1280]{3,2,1,0:T(8,128)(2,1)S(1)}, u32[]{:S(2)}, u32[]{:S(2)}) collective-permute-start(bf16[2,1,128,1280]{3,2,1,0:T(8,128)(2,1)S(1)} %get-tuple-element.90), channel_id=1, source_target_pairs={{0,4},{1,5},{2,6},{3,7},{4,0},{5,1},{6,2},{7,3},{8,12},{9,13},{10,... | collective-permute-start | bytes 1966088 | tf_op jit(solution)/shard_map/ppermute | solution.py:774
  122.4 41.6 %collective-permute-start.22 = (bf16[8,128,384]{2,1,0:T(8,128)(2,1)S(1)}, bf16[8,128,384]{2,1,0:T(8,128)(2,1)S(1)}, u32[]{:S(2)}, u32[]{:S(2)}) collective-permute-start(bf16[8,128,384]{2,1,0:T(8,128)(2,1)S(1)} %added.6.refs_5_), channel_id=1, source_target_pairs={{0,8},{1,9},{2,10},{3,11},{4,12},{5,13},{6,14},{7,15},{8,0},{9,1},... | collective-permute-start | bytes 2359304 | tf_op jit(solution)/shard_map/ppermute | solution.py:771
  128.6 7.3 %collective-permute-start.26 = (f32[8,2048]{1,0:T(8,128)S(1)}, f32[8,2048]{1,0:T(8,128)S(1)}, u32[]{:S(2)}, u32[]{:S(2)}) collective-permute-start(f32[8,2048]{1,0:T(8,128)S(1)} %added.7.refs_0_), channel_id=1, source_target_pairs={{0,2},{1,3},{2,0},{3,1},{4,6},{5,7},{6,4},{7,5},{8,10},{9,11},{10,... | collective-permute-start | bytes 196616 | tf_op jit(solution)/shard_map/ppermute | solution.py:774
  135.9 19.2 %collective-permute-start.27 = (f32[8,2048]{1,0:T(8,128)S(1)}, f32[8,2048]{1,0:T(8,128)S(1)}, u32[]{:S(2)}, u32[]{:S(2)}) collective-permute-start(f32[8,2048]{1,0:T(8,128)S(1)} %added.8.refs_0_), channel_id=1, source_target_pairs={{0,4},{1,5},{2,6},{3,7},{4,0},{5,1},{6,2},{7,3},{8,12},{9,13},{10,... | collective-permute-start | bytes 196616 | tf_op jit(solution)/shard_map/ppermute | solution.py:774
  136.0 19.7 %collective-permute-start.23 = (bf16[8,64,384]{2,1,0:T(8,128)(2,1)S(1)}, bf16[8,64,384]{2,1,0:T(8,128)(2,1)S(1)}, u32[]{:S(2)}, u32[]{:S(2)}) collective-permute-start(bf16[8,64,384]{2,1,0:T(8,128)(2,1)S(1)} %get-tuple-element.101), channel_id=1, source_target_pairs={{0,16},{16,0},{1,17},{17,1},{2,18},{18,2},{3,19},{19,3},{4,20},{20... | collective-permute-start | bytes 1179656 | tf_op jit(solution)/shard_map/ppermute | solution.py:777
  136.8 18.9 %collective-permute-start.24 = (bf16[8,64,384]{2,1,0:T(8,128)(2,1)S(1)}, bf16[8,64,384]{2,1,0:T(8,128)(2,1)S(1)}, u32[]{:S(2)}, u32[]{:S(2)}) collective-permute-start(bf16[8,64,384]{2,1,0:T(8,128)(2,1)S(1)} %get-tuple-element.102), channel_id=1, source_target_pairs={{0,16},{16,0},{1,17},{17,1},{2,18},{18,2},{3,19},{19,3},{4,20},{20... | collective-permute-start | bytes 1179656 | tf_op jit(solution)/shard_map/ppermute | solution.py:777
  145.3 17.1 %collective-permute-start.18 = (bf16[1,1,128,1536]{3,2,1,0:T(8,128)(2,1)S(1)}, bf16[1,1,128,1536]{3,2,1,0:T(8,128)(2,1)S(1)}, u32[]{:S(2)}, u32[]{:S(2)}) collective-permute-start(bf16[1,1,128,1536]{3,2,1,0:T(8,128)(2,1)S(1)} %get-tuple-element.93), channel_id=1, source_target_pairs={{0,4},{1,5},{2,6},{3,7},{4,0},{5,1},{6,2},{7,3},{8,12},{9,13},{10,... | collective-permute-start | bytes 1179656 | tf_op jit(solution)/shard_map/ppermute | solution.py:774
  155.1 8.9 %collective-permute-start.19 = (bf16[1,1,128,1536]{3,2,1,0:T(8,128)(2,1)S(1)}, bf16[1,1,128,1536]{3,2,1,0:T(8,128)(2,1)S(1)}, u32[]{:S(2)}, u32[]{:S(2)}) collective-permute-start(bf16[1,1,128,1536]{3,2,1,0:T(8,128)(2,1)S(1)} %get-tuple-element.94), channel_id=1, source_target_pairs={{0,2},{1,3},{2,0},{3,1},{4,6},{5,7},{6,4},{7,5},{8,10},{9,11},{10,... | collective-permute-start | bytes 1179656 | tf_op jit(solution)/shard_map/ppermute | solution.py:774
  165.2 17.9 %all-to-all-start.2 = ((bf16[8,128,384]{2,1,0:T(8,128)(2,1)}), bf16[8,128,384]{2,1,0:T(8,128)(2,1)S(1)}, u32[]{:S(2)}, u32[]{:S(2)}) async-start(bf16[8,128,384]{2,1,0:T(8,128)(2,1)} %merge.1), calls=%async_computation.2 | async-start | bytes 1572864 | tf_op jit(solution)/shard_map/all_to_all | solution.py:780
  168.7 4.3 %collective-permute-start.28 = (f32[8,2048]{1,0:T(8,128)S(1)}, f32[8,2048]{1,0:T(8,128)S(1)}, u32[]{:S(2)}, u32[]{:S(2)}) collective-permute-start(f32[8,2048]{1,0:T(8,128)S(1)} %added.9.refs_6_.refs_0_), channel_id=1, source_target_pairs={{0,16},{16,0},{1,17},{17,1},{2,18},{18,2},{3,19},{19,3},{4,20},{20... | collective-permute-start | bytes 196616 | tf_op jit(solution)/shard_map/ppermute | solution.py:777
  169.2 10.5 %collective-permute-start.20 = (f32[1,128]{1,0:T(1,128)S(1)}, f32[1,128]{1,0:T(1,128)S(1)}, u32[]{:S(2)}, u32[]{:S(2)}) collective-permute-start(f32[1,128]{1,0:T(1,128)S(1)} %slice.48), channel_id=1, source_target_pairs={{8,0},{9,1},{10,2},{11,3},{12,4},{13,5},{14,6},{15,7},{24,16},{25,... | collective-permute-start | bytes 1544 | tf_op jit(solution)/shard_map/ppermute | solution.py:915
  173.0 7.7 %collective-permute-start.29 = (f32[8,2048]{1,0:T(8,128)S(1)}, f32[8,2048]{1,0:T(8,128)S(1)}, u32[]{:S(2)}, u32[]{:S(2)}) collective-permute-start(f32[8,2048]{1,0:T(8,128)S(1)} %added.10.refs_0_), channel_id=1, source_target_pairs={{0,8},{1,9},{2,10},{3,11},{4,12},{5,13},{6,14},{7,15},{8,0},{9,1},... | collective-permute-start | bytes 196616 | tf_op jit(solution)/shard_map/ppermute | solution.py:771
  (14 other events, 240.3 us)

commit v4 on v3

--- a/solution.py
+++ b/solution.py
@@ -20,6 +20,7 @@
 STATS = 16
 SPARE = 16
 UNROLL = 8
+TOGETHER = 8
 f32 = jnp.float32
 bf16 = jnp.bfloat16
 
@@ -460,20 +461,41 @@
     return token_terms(prev_ref[i, at, :], c, yf, yr, x, g, keep_ref[r, at, :], hfv[i], hrv[i])
 
 
-def run_back(a_ref, b_ref, d_ref, carried, count):
+def composed(a, b):
+    p, q = (value.reshape(-1, TOGETHER, LANES) for value in (a, b))
+    row = lax.broadcasted_iota(jnp.int32, p.shape, 1)
+    step = 1
+    while step < TOGETHER:
+        there = row < TOGETHER - step
+        q += jnp.where(there, p * pltpu.roll(q, TOGETHER - step, 1), 0.0)
+        p *= jnp.where(there, pltpu.roll(p, TOGETHER - step, 1), 1.0)
+        step *= 2
+    return p.reshape(a.shape), q.reshape(a.shape)
+
+
+def entering(p, q, d):
+    left = pltpu.roll((p * d + q).reshape(-1, TOGETHER, LANES), TOGETHER - 1, 1)
+    row = lax.broadcasted_iota(jnp.int32, left.shape, 1)
+    return jnp.where(row < TOGETHER - 1, left, d.reshape(left.shape)).reshape(d.shape)
+
+
+def run_back(p_ref, q_ref, d_ref, carried, count):
+    carried = [jnp.broadcast_to(d, (TOGETHER, LANES)) for d in carried]
+
     def body(j, carried):
-        base = pl.multiple_of(count - UNROLL * (j + 1), UNROLL)
+        base = pl.multiple_of(count - UNROLL * TOGETHER * (j + 1), UNROLL * TOGETHER)
         for u in reversed(range(UNROLL)):
-            row = pl.ds(base + u, 1)
+            at = base + u * TOGETHER
             now = []
             for i, d in enumerate(carried):
                 if d_ref is not None:
-                    d_ref[i, row, :] = d
-                now.append(a_ref[i, row, :] * d + b_ref[i, row, :])
+                    d_ref[i, pl.ds(at, TOGETHER), :] = d
+                now.append(p_ref[i, pl.ds(at, 1), :] * d + q_ref[i, pl.ds(at, 1), :])
             carried = now
         return carried
 
-    return lax.fori_loop(0, count // UNROLL, body, carried)
+    carried = lax.fori_loop(0, count // (UNROLL * TOGETHER), body, carried)
+    return [d[0:1] for d in carried]
 
 
 def entry_kernel(
@@ -491,8 +513,8 @@
         for k in range(blocks):
             for i in range(tiles):
                 t = block_terms(p_ref, keep_ref, prev_ref, x_ref, g_ref, hfv, hrv, r, k, i)
-                a_ref[i, BLOCK * k : BLOCK * (k + 1), :] = t["a"]
-                b_ref[i, BLOCK * k : BLOCK * (k + 1), :] = t["b"]
+                rows_here = slice(BLOCK * k, BLOCK * (k + 1))
+                a_ref[i, rows_here, :], b_ref[i, rows_here, :] = composed(t["a"], t["b"])
         carried = run_back(a_ref, b_ref, None, [jnp.zeros((1, LANES), f32)] * tiles, blocks * BLOCK)
         for i in range(tiles):
             back_ref[r, :, LANES * i : LANES * (i + 1)] = carried[i]
@@ -544,7 +566,8 @@
                 for n in range(devices):
                     hidden_ref[k * devices + n, r, :, lanes] = t["hidden"][n * block : (n + 1) * block].astype(bf16)
                 high_ref[r, i, out, :] = t["high"].astype(bf16)
-                for ref, name in zip((a_ref, b_ref, gg_ref, e_ref, omf_ref, dr_ref), ("a", "b", "gg", "e", "omf", "dr")):
+                a_ref[i, out, :], b_ref[i, out, :] = composed(t["a"], t["b"])
+                for ref, name in zip((gg_ref, e_ref, omf_ref, dr_ref), ("gg", "e", "omf", "dr")):
                     ref[i, out, :] = t[name]
                 final_ref[r, :, lanes] = t["cell"][-1:]
 
@@ -557,7 +580,7 @@
             first, second = jnp.zeros((BLOCK, LANES), f32), jnp.zeros((BLOCK, LANES), f32)
             for i in range(tiles):
                 prev = prev_ref[i, at, :]
-                u = d_ref[i, out, :] + gg_ref[i, out, :]
+                u = entering(a_ref[i, out, :], b_ref[i, out, :], d_ref[i, out, :]) + gg_ref[i, out, :]
                 df, dr = u * e_ref[i, out, :], dr_ref[i, out, :]
                 dc = u * omf_ref[i, out, :]
                 for m, value in enumerate((dc, df, dr)):
@@ -907,7 +930,7 @@
     value = merge(here[0], here_got, z_got, waits) if paired else added(here, z_got, waits)
     grad_weight = collected([shared(value)], f32)
     totals = added(totals, swapped(totals)) if ranks == 2 else lax.psum(totals, "dp")
-    totals = added(totals, across(totals))
+    totals = added(totals, across(totals), (grad_inputs,))
 
     own_width = features // sections
     if piece == own_width and chunks == 2:

time: 185 us -> 184 us (level)
  transfers between devices with their start and end apart: 33 -> 33, of which waited for: 22 -> 21; matrix products, arithmetic and copies ran while one was open for 2% -> 2% of each run, Pallas kernels for 13% -> 13%
where the time goes in v4:
time: 184 us; the launch traced here: 183 us
  waiting for transfers between devices  83.8 us (46%)
  Pallas kernels  45.9 us (25%)
  starting transfers between devices  45.8 us (25%)
  local copies, waits for them, and re-layouts  4.69 us (3%)
  other arithmetic  2.06 us (1%)
    ppermute x18, waiting for transfers between devices, flipped(): return lax.ppermute(value, 'fsdp', [(j, j ^ bit) for j in range(sections)])  54.4 us
    pallas_call x24, Pallas kernels, call(): pl.pallas_call(body, in_specs=[in_smem] * len(scalars) + [in_vmem] * len(...  45.9 us
    all_to_all x3, starting transfers between devices, shared(): lax.all_to_all(value, 'fsdp', 0, 0, tiled=True, axis_index_groups=groups)  12.7 us
    ppermute x18, starting transfers between devices, flipped(): return lax.ppermute(value, 'fsdp', [(j, j ^ bit) for j in range(sections)])  12.2 us
    ppermute x5, starting transfers between devices, across(): lax.ppermute(value, 'fsdp', [(j, (j + group) % sections) for j in range(s...  12.2 us
    all_to_all x3, waiting for transfers between devices, shared(): lax.all_to_all(value, 'fsdp', 0, 0, tiled=True, axis_index_groups=groups)  11.1 us
    ppermute x6, starting transfers between devices, swapped(): return lax.ppermute(value, 'dp', [(0, 1), (1, 0)])  7.29 us
    ppermute x5, waiting for transfers between devices, across(): lax.ppermute(value, 'fsdp', [(j, (j + group) % sections) for j in range(s...  7.15 us
  transfers between devices with their start and end apart: 33, of which 21 were waited for; matrix products, arithmetic and copies ran while one was open for 2% of the time, Pallas kernels for 13%

profile of v4, /device:TPU:8, one launch (start us, length us, event | category | flops | bytes accessed | tf_op | source)
XLA Modules:
  0.0 183.2 jit_solution(12401636854626045959)
XLA Ops:
  2.8 4.4 %all-to-all-start = ((bf16[8,128,384]{2,1,0:T(8,128)(2,1)}), bf16[8,128,384]{2,1,0:T(8,128)(2,1)S(1)}, u32[]{:S(2)}, u32[]{:S(2)}) async-start(bf16[8,128,384]{2,1,0:T(8,128)(2,1)} %deal.2), calls=%async_computation | async-start | bytes 1572864 | tf_op jit(solution)/shard_map/all_to_all | solution.py:803
  7.2 11.1 %all-to-all-done.refs_2_.refs_3_ = bf16[8,128,384]{2,1,0:T(8,128)(2,1)S(1)} async-done(((bf16[8,128,384]{2,1,0:T(8,128)(2,1)}), bf16[8,128,384]{2,1,0:T(8,128)(2,1)S(1)}, u32[]{:S(2)}, u32[]{:S(2)}) %all-to-all-start) | async-done | bytes 786464 | tf_op jit(solution)/shard_map/all_to_all | solution.py:803
  19.3 2.6 %collective-permute-start = (bf16[8,128,384]{2,1,0:T(8,128)(2,1)S(1)}, bf16[8,128,384]{2,1,0:T(8,128)(2,1)S(1)}, u32[]{:S(2)}, u32[]{:S(2)}) collective-permute-start(bf16[8,128,384]{2,1,0:T(8,128)(2,1)S(1)} %all-to-all-done.refs_2_.refs_3_), channel_id=1, source_target_pairs={{0,8},{1,9},{2,10},{3,11},{4,12},{5,13},{6,14},{7,15},{8,0},{9,1},... | collective-permute-start | bytes 2359304 | tf_op jit(solution)/shard_map/ppermute | solution.py:794
  22.7 4.9 %all-to-all-start.1 = ((bf16[8,1,128,256]{3,2,1,0:T(8,128)(2,1)}), bf16[8,1,128,256]{3,2,1,0:T(8,128)(2,1)S(1)}, u32[]{:S(2)}, u32[]{:S(2)}) async-start(bf16[8,1,128,256]{3,2,1,0:T(8,128)(2,1)} %bitcast.9), calls=%async_computation.1 | async-start | bytes 1048576 | tf_op jit(solution)/shard_map/all_to_all | solution.py:803
  30.6 15.8 %collective-permute-done.5.refs_0_ = bf16[1,144,2048]{2,1,0:T(8,128)(2,1)} collective-permute-done((bf16[1,144,2048]{2,1,0:T(8,128)(2,1)S(1)}, bf16[1,144,2048]{2,1,0:T(8,128)(2,1)}, u32[]{:S(2)}, u32[]{:S(2)}) %collective-permute-start.5) | collective-permute-done | bytes 589856 | tf_op jit(solution)/shard_map/ppermute | solution.py:797
  48.8 6.3 %collective-permute-done.refs_1_.refs_9_ = bf16[8,128,384]{2,1,0:T(8,128)(2,1)S(1)} collective-permute-done((bf16[8,128,384]{2,1,0:T(8,128)(2,1)S(1)}, bf16[8,128,384]{2,1,0:T(8,128)(2,1)S(1)}, u32[]{:S(2)}, u32[]{:S(2)}) %collective-permute-start) | collective-permute-done | bytes 786464 | tf_op jit(solution)/shard_map/ppermute | solution.py:794
  58.1 4.1 %collective-permute-done.7.refs_0_ = bf16[1,144,2048]{2,1,0:T(8,128)(2,1)} collective-permute-done((bf16[1,144,2048]{2,1,0:T(8,128)(2,1)}, bf16[1,144,2048]{2,1,0:T(8,128)(2,1)}, u32[]{:S(2)}, u32[]{:S(2)}) %collective-permute-start.7) | collective-permute-done | bytes 589856 | tf_op jit(solution)/shard_map/ppermute | solution.py:797
  65.4 4.4 %norm.1 = (bf16[1,1024,2048]{2,1,0:T(8,128)(2,1)S(1)}, f32[1,2,1024,128]{3,2,1,0:T(8,128)S(1)}, f32[1,1088,128]{2,1,0:T(8,128)S(1)}, bf16[1,2,1024,128]{3,2,1,0:T(8,128)(2,1)S(1)}) custom-call(s32[5]{0:T(128)S(1)} %stack.23.refs_0_, f32[1,2048]{1,0:T(1,128)S(1)} %bitcast.42, f32[1,2048]{1,0:T(1,128)S(1)} %bitcast.45, bf16[1,144,2048]{2,1,0:T(8,128)(2,1)S(1)} %copy-done.6, ...), custom_call_target="tpu_custom_call" | custom-call | tf_op jit(solution)/shard_map/norm/pallas_call | solution.py:43
  69.8 3.2 %project.1 = (f32[1,6,1024,128]{3,2,1,0:T(8,128)S(1)}, f32[16,768]{1,0:T(8,128)S(1)}, bf16[1024,768]{1,0:T(8,128)(2,1)S(1)}) custom-call(s32[5]{0:T(128)S(1)} %stack.23.refs_0_, bf16[1,1024,2048]{2,1,0:T(8,128)(2,1)S(1)} %get-tuple-element.58.refs_1_.refs_0_, bf16[16,2048]{1,0:T(8,128)(2,1)S(1)} %pad.4.refs_2_, ...), custom_call_target="tpu_custom_call" | custom-call | tf_op jit(solution)/shard_map/project/pallas_call | solution.py:43
  73.1 7.8 %blocks_forward.1 = (f32[1,6,1088,128]{3,2,1,0:T(8,128)S(1)}, f32[1,2,1088,128]{3,2,1,0:T(8,128)S(1)}, f32[1,2,336,128]{3,2,1,0:T(8,128)S(1)}, f32[1,1,256]{2,1,...) custom-call(s32[5]{0:T(128)S(1)} %stack.23.refs_0_, ...), custom_call_target="tpu_custom_call" | custom-call | tf_op jit(solution)/shard_map/blocks_forward/pallas_call | solution.py:43
  80.9 3.4 %collective-permute-start.10 = (f32[1,1,256]{2,1,0:T(1,128)S(1)}, f32[1,1,256]{2,1,0:T(1,128)S(1)}, u32[]{:S(2)}, u32[]{:S(2)}) collective-permute-start(f32[1,1,256]{2,1,0:T(1,128)S(1)} %get-tuple-element.67), channel_id=1, source_target_pairs={{0,8},{1,9},{2,10},{3,11},{4,12},{5,13},{6,14},{7,15},{8,0},{9,1},... | collective-permute-start | bytes 3080 | tf_op jit(solution)/shard_map/ppermute | solution.py:794
  85.9 2.3 %entry.1 = (f32[1,2,200,128]{3,2,1,0:T(8,128)S(1)}, f32[1,1,256]{2,1,0:T(1,128)S(1)}) custom-call(f32[1,6,1088,128]{3,2,1,0:T(8,128)S(1)} %get-tuple-element.62.refs_0_.refs_1_, f32[1,1088,128]{2,1,0:T(8,128)S(1)} %get-tuple-element.61.refs_6_.refs_1_.refs_2_, f32[1,2,1088,128]{3,2,1,0:T(8,128)S(1)} %get-tuple-element.63.refs_2_.refs_3_, ...), custom_call_target="tpu_custom_call" | custom-call | tf_op jit(solution)/shard_map/entry/pallas_call | solution.py:43
  88.2 3.0 %collective-permute-start.11 = (f32[1,1,256]{2,1,0:T(1,128)S(1)}, f32[1,1,256]{2,1,0:T(1,128)S(1)}, u32[]{:S(2)}, u32[]{:S(2)}) collective-permute-start(f32[1,1,256]{2,1,0:T(1,128)S(1)} %get-tuple-element.69), channel_id=1, source_target_pairs={{0,8},{1,9},{2,10},{3,11},{4,12},{5,13},{6,14},{7,15},{8,0},{9,1},... | collective-permute-start | bytes 3080 | tf_op jit(solution)/shard_map/ppermute | solution.py:794
  91.2 4.1 %lead_forward.1.refs_4_ = f32[1,2,816,128]{3,2,1,0:T(8,128)S(1)} custom-call(f32[1,6,1088,128]{3,2,1,0:T(8,128)S(1)} %get-tuple-element.62.refs_0_.refs_1_, f32[1,1088,128]{2,1,0:T(8,128)S(1)} %get-tuple-element.61.refs_6_.refs_1_.refs_2_, f32[1,256]{1,0:T(1,128)S(1)} %fusion.7.refs_7_.refs_2_.refs_5_.refs_8_, f32[1,1,256]{2,1,0:T(1,128)S(1)} %get-tuple-element.64.refs_3_, ...), custom_call_target="tpu_custom_call" | custom-call | tf_op jit(solution)/shard_map/lead_forward/pallas_call | solution.py:43
  95.3 5.0 %backward.1 = (bf16[1,1024,768]{2,1,0:T(8,128)(2,1)S(1)}, bf16[8,1,128,256]{3,2,1,0:T(8,128)(2,1)S(1)}, bf16[1,2,1024,128]{3,2,1,0:T(8,128)(2,1)S(1)}, f32[8,768...) custom-call(s32[5]{0:T(128)S(1)} %stack.23.refs_0_, ...), custom_call_target="tpu_custom_call" | custom-call | tf_op jit(solution)/shard_map/backward/pallas_call | solution.py:43
  100.4 2.3 %weight_back.2 = (f32[2,1024]{1,0:T(2,128)S(1)}, bf16[8,128,384]{2,1,0:T(8,128)(2,1)S(1)}, bf16[8,144,384]{2,1,0:T(8,128)(2,1)S(1)}) custom-call(bf16[1,1024,2048]{2,1,0:T(8,128)(2,1)S(1)} %get-tuple-element.58.refs_1_.refs_0_, bf16[1,1024,768]{2,1,0:T(8,128)(2,1)S(1)} %get-tuple-element.72.refs_1_.refs_3_, f32[8,768]{1,0:T(8,128)S(1)} %get-tuple-element.77.refs_2_.refs_1_, ...), custom_call_target="tpu_custom_call" | custom-call | tf_op jit(solution)/shard_map/weight_back/pallas_call | solution.py:43
  102.6 1.6 collective-permute-start.21
  104.2 6.6 %norm_back.1 = (bf16[2,1,128,1152]{3,2,1,0:T(8,128)(2,1)S(1)}, bf16[2,1,128,1152]{3,2,1,0:T(8,128)(2,1)S(1)}, bf16[2,1,128,1152]{3,2,1,0:T(8,128)(2,1)S(1)}, bf1...) custom-call(s32[5]{0:T(128)S(1)} %stack.23.refs_0_, ...), custom_call_target="tpu_custom_call" | custom-call | tf_op jit(solution)/shard_map/norm_back/pallas_call | solution.py:43
  117.4 3.0 %collective-permute-done.21.refs_1_ = bf16[8,144,384]{2,1,0:T(8,128)(2,1)S(1)} collective-permute-done((bf16[8,144,384]{2,1,0:T(8,128)(2,1)S(1)}, bf16[8,144,384]{2,1,0:T(8,128)(2,1)S(1)}, u32[]{:S(2)}, u32[]{:S(2)}) %collective-permute-start.21) | collective-permute-done | bytes 884768 | tf_op jit(solution)/shard_map/ppermute | solution.py:800
  120.6 2.0 %collective-permute-start.22 = (bf16[8,128,384]{2,1,0:T(8,128)(2,1)S(1)}, bf16[8,128,384]{2,1,0:T(8,128)(2,1)S(1)}, u32[]{:S(2)}, u32[]{:S(2)}) collective-permute-start(bf16[8,128,384]{2,1,0:T(8,128)(2,1)S(1)} %added.6.refs_5_), channel_id=1, source_target_pairs={{0,8},{1,9},{2,10},{3,11},{4,12},{5,13},{6,14},{7,15},{8,0},{9,1},... | collective-permute-start | bytes 2359304 | tf_op jit(solution)/shard_map/ppermute | solution.py:794
  122.6 2.3 %weight_back.3 = (f32[2,1024]{1,0:T(2,128)S(1)}, bf16[8,128,384]{2,1,0:T(8,128)(2,1)S(1)}, bf16[8,64,384]{2,1,0:T(8,128)(2,1)S(1)}, bf16[8,64,384]{2,1,0:T(8,128)(2,1)S(1)}) custom-call(bf16[1,1024,2048]{2,1,0:T(8,128)(2,1)S(1)} %get-tuple-element.58.refs_1_.refs_0_, bf16[1,1024,768]{2,1,0:T(8,128)(2,1)S(1)} %get-tuple-element.72.refs_1_.refs_3_, ...), custom_call_target="tpu_custom_call" | custom-call | tf_op jit(solution)/shard_map/weight_back/pallas_call | solution.py:43
  126.8 1.7 collective-permute-start.26
  128.5 5.6 %collective-permute-done.26.refs_1_ = f32[8,2048]{1,0:T(8,128)S(1)} collective-permute-done((f32[8,2048]{1,0:T(8,128)S(1)}, f32[8,2048]{1,0:T(8,128)S(1)}, u32[]{:S(2)}, u32[]{:S(2)}) %collective-permute-start.26) | collective-permute-done | bytes 65568 | tf_op jit(solution)/shard_map/ppermute | solution.py:797
  136.3 6.9 %collective-permute-done.17.refs_3_ = bf16[2,1,128,1280]{3,2,1,0:T(8,128)(2,1)S(1)} collective-permute-done((bf16[2,1,128,1280]{3,2,1,0:T(8,128)(2,1)S(1)}, bf16[2,1,128,1280]{3,2,1,0:T(8,128)(2,1)S(1)}, u32[]{:S(2)}, u32[]{:S(2)}) %collective-permute-start.17) | collective-permute-done | bytes 655392 | tf_op jit(solution)/shard_map/ppermute | solution.py:797
  143.5 2.5 %collective-permute-start.18 = (bf16[1,1,128,1536]{3,2,1,0:T(8,128)(2,1)S(1)}, bf16[1,1,128,1536]{3,2,1,0:T(8,128)(2,1)S(1)}, u32[]{:S(2)}, u32[]{:S(2)}) collective-permute-start(bf16[1,1,128,1536]{3,2,1,0:T(8,128)(2,1)S(1)} %get-tuple-element.93), channel_id=1, source_target_pairs={{0,4},{1,5},{2,6},{3,7},{4,0},{5,1},{6,2},{7,3},{8,12},{9,13},{10,... | collective-permute-start | bytes 1179656 | tf_op jit(solution)/shard_map/ppermute | solution.py:797
  146.0 7.3 %collective-permute-done.27.refs_1_ = f32[8,2048]{1,0:T(8,128)S(1)} collective-permute-done((f32[8,2048]{1,0:T(8,128)S(1)}, f32[8,2048]{1,0:T(8,128)S(1)}, u32[]{:S(2)}, u32[]{:S(2)}) %collective-permute-start.27) | collective-permute-done | bytes 65568 | tf_op jit(solution)/shard_map/ppermute | solution.py:797
  153.9 6.7 %collective-permute-done.18.refs_3_.refs_4_ = bf16[1,1,128,1536]{3,2,1,0:T(8,128)(2,1)S(1)} collective-permute-done((bf16[1,1,128,1536]{3,2,1,0:T(8,128)(2,1)S(1)}, bf16[1,1,128,1536]{3,2,1,0:T(8,128)(2,1)S(1)}, u32[]{:S(2)}, u32[]{:S(2)}) %collective-permute-start.18) | collective-permute-done | bytes 393248 | tf_op jit(solution)/shard_map/ppermute | solution.py:797
  160.6 1.6 collective-permute-done.19.refs_4_.refs_5_
  163.4 3.5 %all-to-all-start.2 = ((bf16[8,128,384]{2,1,0:T(8,128)(2,1)}), bf16[8,128,384]{2,1,0:T(8,128)(2,1)S(1)}, u32[]{:S(2)}, u32[]{:S(2)}) async-start(bf16[8,128,384]{2,1,0:T(8,128)(2,1)} %merge.1), calls=%async_computation.2 | async-start | bytes 1572864 | tf_op jit(solution)/shard_map/all_to_all | solution.py:803
  168.8 2.5 %collective-permute-done.28.refs_1_ = f32[8,2048]{1,0:T(8,128)S(1)} collective-permute-done((f32[8,2048]{1,0:T(8,128)S(1)}, f32[8,2048]{1,0:T(8,128)S(1)}, u32[]{:S(2)}, u32[]{:S(2)}) %collective-permute-start.28) | collective-permute-done | bytes 65568 | tf_op jit(solution)/shard_map/ppermute | solution.py:800
  172.4 5.6 %collective-permute-done.20 = f32[1,128]{1,0:T(1,128)S(1)} collective-permute-done((f32[1,128]{1,0:T(1,128)S(1)}, f32[1,128]{1,0:T(1,128)S(1)}, u32[]{:S(2)}, u32[]{:S(2)}) %collective-permute-start.20) | collective-permute-done | bytes 544 | tf_op jit(solution)/shard_map/ppermute | solution.py:938
  178.5 1.7 finish.1
  (110 shorter events, 36.6 us)
Async XLA Ops:
  2.8 15.5 %all-to-all-start = ((bf16[8,128,384]{2,1,0:T(8,128)(2,1)}), bf16[8,128,384]{2,1,0:T(8,128)(2,1)S(1)}, u32[]{:S(2)}, u32[]{:S(2)}) async-start(bf16[8,128,384]{2,1,0:T(8,128)(2,1)} %deal.2), calls=%async_computation | async-start | bytes 1572864 | tf_op jit(solution)/shard_map/all_to_all | solution.py:803
  18.6 27.8 %collective-permute-start.5 = (bf16[1,144,2048]{2,1,0:T(8,128)(2,1)S(1)}, bf16[1,144,2048]{2,1,0:T(8,128)(2,1)}, u32[]{:S(2)}, u32[]{:S(2)}) collective-permute-start(bf16[1,144,2048]{2,1,0:T(8,128)(2,1)S(1)} %stats.1.refs_0_), channel_id=1, source_target_pairs={{0,4},{1,5},{2,6},{3,7},{4,0},{5,1},{6,2},{7,3},{8,12},{9,13},{10,... | collective-permute-start | bytes 1769480 | tf_op jit(solution)/shard_map/ppermute | solution.py:797
  19.3 35.8 %collective-permute-start = (bf16[8,128,384]{2,1,0:T(8,128)(2,1)S(1)}, bf16[8,128,384]{2,1,0:T(8,128)(2,1)S(1)}, u32[]{:S(2)}, u32[]{:S(2)}) collective-permute-start(bf16[8,128,384]{2,1,0:T(8,128)(2,1)S(1)} %all-to-all-done.refs_2_.refs_3_), channel_id=1, source_target_pairs={{0,8},{1,9},{2,10},{3,11},{4,12},{5,13},{6,14},{7,15},{8,0},{9,1},... | collective-permute-start | bytes 2359304 | tf_op jit(solution)/shard_map/ppermute | solution.py:794
  22.7 40.9 %all-to-all-start.1 = ((bf16[8,1,128,256]{3,2,1,0:T(8,128)(2,1)}), bf16[8,1,128,256]{3,2,1,0:T(8,128)(2,1)S(1)}, u32[]{:S(2)}, u32[]{:S(2)}) async-start(bf16[8,1,128,256]{3,2,1,0:T(8,128)(2,1)} %bitcast.9), calls=%async_computation.1 | async-start | bytes 1048576 | tf_op jit(solution)/shard_map/all_to_all | solution.py:803
  27.6 29.1 %collective-permute-start.3 = (bf16[1,144,2048]{2,1,0:T(8,128)(2,1)S(1)}, bf16[1,144,2048]{2,1,0:T(8,128)(2,1)}, u32[]{:S(2)}, u32[]{:S(2)}) collective-permute-start(bf16[1,144,2048]{2,1,0:T(8,128)(2,1)S(1)} %stats.1.refs_0_), channel_id=1, source_target_pairs={{0,2},{1,3},{2,0},{3,1},{4,6},{5,7},{6,4},{7,5},{8,10},{9,11},{10,... | collective-permute-start | bytes 1769480 | tf_op jit(solution)/shard_map/ppermute | solution.py:797
  29.1 27.6 %collective-permute-start.1 = (bf16[8,128,384]{2,1,0:T(8,128)(2,1)S(1)}, bf16[8,128,384]{2,1,0:T(8,128)(2,1)S(1)}, u32[]{:S(2)}, u32[]{:S(2)}) collective-permute-start(bf16[8,128,384]{2,1,0:T(8,128)(2,1)S(1)} %all-to-all-done.refs_2_.refs_3_), channel_id=1, source_target_pairs={{0,16},{16,0},{1,17},{17,1},{2,18},{18,2},{3,19},{19,3},{4,20},{20... | collective-permute-start | bytes 2359304 | tf_op jit(solution)/shard_map/ppermute | solution.py:800
  46.4 15.7 %collective-permute-start.7 = (bf16[1,144,2048]{2,1,0:T(8,128)(2,1)}, bf16[1,144,2048]{2,1,0:T(8,128)(2,1)}, u32[]{:S(2)}, u32[]{:S(2)}) collective-permute-start(bf16[1,144,2048]{2,1,0:T(8,128)(2,1)} %collective-permute-done.5.refs_0_), channel_id=1, source_target_pairs={{0,2},{1,3},{2,0},{3,1},{4,6},{5,7},{6,4},{7,5},{8,10},{9,11},{10,... | collective-permute-start | bytes 1769480 | tf_op jit(solution)/shard_map/ppermute | solution.py:797
  55.1 18.0 %collective-permute-start.9 = (bf16[8,128,384]{2,1,0:T(8,128)(2,1)S(1)}, bf16[8,128,384]{2,1,0:T(8,128)(2,1)}, u32[]{:S(2)}, u32[]{:S(2)}) collective-permute-start(bf16[8,128,384]{2,1,0:T(8,128)(2,1)S(1)} %collective-permute-done.refs_1_.refs_9_), channel_id=1, source_target_pairs={{0,16},{16,0},{1,17},{17,1},{2,18},{18,2},{3,19},{19,3},{4,20},{20... | collective-permute-start | bytes 2359304 | tf_op jit(solution)/shard_map/ppermute | solution.py:800
  57.6 6.1 %collective-permute-start.4 = (bf16[1,144,2048]{2,1,0:T(8,128)(2,1)}, bf16[1,144,2048]{2,1,0:T(8,128)(2,1)}, u32[]{:S(2)}, u32[]{:S(2)}) collective-permute-start(bf16[1,144,2048]{2,1,0:T(8,128)(2,1)} %fence.5.refs_5_.refs_7_), channel_id=1, source_target_pairs={{0,1},{1,0},{2,3},{3,2},{4,5},{5,4},{6,7},{7,6},{8,9},{9,8},{10,11... | collective-permute-start | bytes 1769480 | tf_op jit(solution)/shard_map/ppermute | solution.py:797
  57.6 6.1 %collective-permute-start.2 = (bf16[1,144,2048]{2,1,0:T(8,128)(2,1)}, bf16[1,144,2048]{2,1,0:T(8,128)(2,1)S(1)}, u32[]{:S(2)}, u32[]{:S(2)}) collective-permute-start(bf16[1,144,2048]{2,1,0:T(8,128)(2,1)} %fence.4.refs_3_.refs_5_), channel_id=1, source_target_pairs={{0,1},{1,0},{2,3},{3,2},{4,5},{5,4},{6,7},{7,6},{8,9},{9,8},{10,11... | collective-permute-start | bytes 1769480 | tf_op jit(solution)/shard_map/ppermute | solution.py:797
  62.2 2.3 %collective-permute-start.8 = (bf16[1,144,2048]{2,1,0:T(8,128)(2,1)}, bf16[1,144,2048]{2,1,0:T(8,128)(2,1)}, u32[]{:S(2)}, u32[]{:S(2)}) collective-permute-start(bf16[1,144,2048]{2,1,0:T(8,128)(2,1)} %fence.7.refs_9_.refs_11_), channel_id=1, source_target_pairs={{0,1},{1,0},{2,3},{3,2},{4,5},{5,4},{6,7},{7,6},{8,9},{9,8},{10,11... | collective-permute-start | bytes 1769480 | tf_op jit(solution)/shard_map/ppermute | solution.py:797
  62.2 3.2 %collective-permute-start.6 = (bf16[1,144,2048]{2,1,0:T(8,128)(2,1)}, bf16[1,144,2048]{2,1,0:T(8,128)(2,1)}, u32[]{:S(2)}, u32[]{:S(2)}) collective-permute-start(bf16[1,144,2048]{2,1,0:T(8,128)(2,1)} %fence.6.refs_7_.refs_9_), channel_id=1, source_target_pairs={{0,1},{1,0},{2,3},{3,2},{4,5},{5,4},{6,7},{7,6},{8,9},{9,8},{10,11... | collective-permute-start | bytes 1769480 | tf_op jit(solution)/shard_map/ppermute | solution.py:797
  80.9 5.0 %collective-permute-start.10 = (f32[1,1,256]{2,1,0:T(1,128)S(1)}, f32[1,1,256]{2,1,0:T(1,128)S(1)}, u32[]{:S(2)}, u32[]{:S(2)}) collective-permute-start(f32[1,1,256]{2,1,0:T(1,128)S(1)} %get-tuple-element.67), channel_id=1, source_target_pairs={{0,8},{1,9},{2,10},{3,11},{4,12},{5,13},{6,14},{7,15},{8,0},{9,1},... | collective-permute-start | bytes 3080 | tf_op jit(solution)/shard_map/ppermute | solution.py:794
  88.2 7.1 %collective-permute-start.11 = (f32[1,1,256]{2,1,0:T(1,128)S(1)}, f32[1,1,256]{2,1,0:T(1,128)S(1)}, u32[]{:S(2)}, u32[]{:S(2)}) collective-permute-start(f32[1,1,256]{2,1,0:T(1,128)S(1)} %get-tuple-element.69), channel_id=1, source_target_pairs={{0,8},{1,9},{2,10},{3,11},{4,12},{5,13},{6,14},{7,15},{8,0},{9,1},... | collective-permute-start | bytes 3080 | tf_op jit(solution)/shard_map/ppermute | solution.py:794
  102.6 17.7 %collective-permute-start.21 = (bf16[8,144,384]{2,1,0:T(8,128)(2,1)S(1)}, bf16[8,144,384]{2,1,0:T(8,128)(2,1)S(1)}, u32[]{:S(2)}, u32[]{:S(2)}) collective-permute-start(bf16[8,144,384]{2,1,0:T(8,128)(2,1)S(1)} %get-tuple-element.99), channel_id=1, source_target_pairs={{0,16},{16,0},{1,17},{17,1},{2,18},{18,2},{3,19},{19,3},{4,20},{20... | collective-permute-start | bytes 2654216 | tf_op jit(solution)/shard_map/ppermute | solution.py:800
  110.8 2.1 %collective-permute-start.12 = (bf16[2,1,128,1152]{3,2,1,0:T(8,128)(2,1)S(1)}, bf16[2,1,128,1152]{3,2,1,0:T(8,128)(2,1)S(1)}, u32[]{:S(2)}, u32[]{:S(2)}) collective-permute-start(bf16[2,1,128,1152]{3,2,1,0:T(8,128)(2,1)S(1)} %get-tuple-element.83), channel_id=1, source_target_pairs={{0,1},{1,0},{2,3},{3,2},{4,5},{5,4},{6,7},{7,6},{8,9},{9,8},{10,11... | collective-permute-start | bytes 1769480 | tf_op jit(solution)/shard_map/ppermute | solution.py:797
  110.9 2.8 %collective-permute-start.13 = (bf16[2,1,128,1152]{3,2,1,0:T(8,128)(2,1)S(1)}, bf16[2,1,128,1152]{3,2,1,0:T(8,128)(2,1)S(1)}, u32[]{:S(2)}, u32[]{:S(2)}) collective-permute-start(bf16[2,1,128,1152]{3,2,1,0:T(8,128)(2,1)S(1)} %get-tuple-element.84), channel_id=1, source_target_pairs={{0,1},{1,0},{2,3},{3,2},{4,5},{5,4},{6,7},{7,6},{8,9},{9,8},{10,11... | collective-permute-start | bytes 1769480 | tf_op jit(solution)/shard_map/ppermute | solution.py:797
  111.4 3.2 %collective-permute-start.14 = (bf16[2,1,128,1152]{3,2,1,0:T(8,128)(2,1)S(1)}, bf16[2,1,128,1152]{3,2,1,0:T(8,128)(2,1)S(1)}, u32[]{:S(2)}, u32[]{:S(2)}) collective-permute-start(bf16[2,1,128,1152]{3,2,1,0:T(8,128)(2,1)S(1)} %get-tuple-element.85), channel_id=1, source_target_pairs={{0,1},{1,0},{2,3},{3,2},{4,5},{5,4},{6,7},{7,6},{8,9},{9,8},{10,11... | collective-permute-start | bytes 1769480 | tf_op jit(solution)/shard_map/ppermute | solution.py:797
  111.5 3.9 %collective-permute-start.15 = (bf16[2,1,128,1152]{3,2,1,0:T(8,128)(2,1)S(1)}, bf16[2,1,128,1152]{3,2,1,0:T(8,128)(2,1)S(1)}, u32[]{:S(2)}, u32[]{:S(2)}) collective-permute-start(bf16[2,1,128,1152]{3,2,1,0:T(8,128)(2,1)S(1)} %get-tuple-element.86), channel_id=1, source_target_pairs={{0,1},{1,0},{2,3},{3,2},{4,5},{5,4},{6,7},{7,6},{8,9},{9,8},{10,11... | collective-permute-start | bytes 1769480 | tf_op jit(solution)/shard_map/ppermute | solution.py:797
  115.9 19.1 %collective-permute-start.16 = (bf16[2,1,128,1280]{3,2,1,0:T(8,128)(2,1)S(1)}, bf16[2,1,128,1280]{3,2,1,0:T(8,128)(2,1)S(1)}, u32[]{:S(2)}, u32[]{:S(2)}) collective-permute-start(bf16[2,1,128,1280]{3,2,1,0:T(8,128)(2,1)S(1)} %get-tuple-element.89), channel_id=1, source_target_pairs={{0,2},{1,3},{2,0},{3,1},{4,6},{5,7},{6,4},{7,5},{8,10},{9,11},{10,... | collective-permute-start | bytes 1966088 | tf_op jit(solution)/shard_map/ppermute | solution.py:797
  117.4 25.8 %collective-permute-start.17 = (bf16[2,1,128,1280]{3,2,1,0:T(8,128)(2,1)S(1)}, bf16[2,1,128,1280]{3,2,1,0:T(8,128)(2,1)S(1)}, u32[]{:S(2)}, u32[]{:S(2)}) collective-permute-start(bf16[2,1,128,1280]{3,2,1,0:T(8,128)(2,1)S(1)} %get-tuple-element.90), channel_id=1, source_target_pairs={{0,4},{1,5},{2,6},{3,7},{4,0},{5,1},{6,2},{7,3},{8,12},{9,13},{10,... | collective-permute-start | bytes 1966088 | tf_op jit(solution)/shard_map/ppermute | solution.py:797
  120.6 41.6 %collective-permute-start.22 = (bf16[8,128,384]{2,1,0:T(8,128)(2,1)S(1)}, bf16[8,128,384]{2,1,0:T(8,128)(2,1)S(1)}, u32[]{:S(2)}, u32[]{:S(2)}) collective-permute-start(bf16[8,128,384]{2,1,0:T(8,128)(2,1)S(1)} %added.6.refs_5_), channel_id=1, source_target_pairs={{0,8},{1,9},{2,10},{3,11},{4,12},{5,13},{6,14},{7,15},{8,0},{9,1},... | collective-permute-start | bytes 2359304 | tf_op jit(solution)/shard_map/ppermute | solution.py:794
  126.8 7.3 %collective-permute-start.26 = (f32[8,2048]{1,0:T(8,128)S(1)}, f32[8,2048]{1,0:T(8,128)S(1)}, u32[]{:S(2)}, u32[]{:S(2)}) collective-permute-start(f32[8,2048]{1,0:T(8,128)S(1)} %added.7.refs_0_), channel_id=1, source_target_pairs={{0,2},{1,3},{2,0},{3,1},{4,6},{5,7},{6,4},{7,5},{8,10},{9,11},{10,... | collective-permute-start | bytes 196616 | tf_op jit(solution)/shard_map/ppermute | solution.py:797
  134.1 19.2 %collective-permute-start.27 = (f32[8,2048]{1,0:T(8,128)S(1)}, f32[8,2048]{1,0:T(8,128)S(1)}, u32[]{:S(2)}, u32[]{:S(2)}) collective-permute-start(f32[8,2048]{1,0:T(8,128)S(1)} %added.8.refs_0_), channel_id=1, source_target_pairs={{0,4},{1,5},{2,6},{3,7},{4,0},{5,1},{6,2},{7,3},{8,12},{9,13},{10,... | collective-permute-start | bytes 196616 | tf_op jit(solution)/shard_map/ppermute | solution.py:797
  134.2 19.7 %collective-permute-start.23 = (bf16[8,64,384]{2,1,0:T(8,128)(2,1)S(1)}, bf16[8,64,384]{2,1,0:T(8,128)(2,1)S(1)}, u32[]{:S(2)}, u32[]{:S(2)}) collective-permute-start(bf16[8,64,384]{2,1,0:T(8,128)(2,1)S(1)} %get-tuple-element.101), channel_id=1, source_target_pairs={{0,16},{16,0},{1,17},{17,1},{2,18},{18,2},{3,19},{19,3},{4,20},{20... | collective-permute-start | bytes 1179656 | tf_op jit(solution)/shard_map/ppermute | solution.py:800
  135.0 18.9 %collective-permute-start.24 = (bf16[8,64,384]{2,1,0:T(8,128)(2,1)S(1)}, bf16[8,64,384]{2,1,0:T(8,128)(2,1)S(1)}, u32[]{:S(2)}, u32[]{:S(2)}) collective-permute-start(bf16[8,64,384]{2,1,0:T(8,128)(2,1)S(1)} %get-tuple-element.102), channel_id=1, source_target_pairs={{0,16},{16,0},{1,17},{17,1},{2,18},{18,2},{3,19},{19,3},{4,20},{20... | collective-permute-start | bytes 1179656 | tf_op jit(solution)/shard_map/ppermute | solution.py:800
  143.5 17.1 %collective-permute-start.18 = (bf16[1,1,128,1536]{3,2,1,0:T(8,128)(2,1)S(1)}, bf16[1,1,128,1536]{3,2,1,0:T(8,128)(2,1)S(1)}, u32[]{:S(2)}, u32[]{:S(2)}) collective-permute-start(bf16[1,1,128,1536]{3,2,1,0:T(8,128)(2,1)S(1)} %get-tuple-element.93), channel_id=1, source_target_pairs={{0,4},{1,5},{2,6},{3,7},{4,0},{5,1},{6,2},{7,3},{8,12},{9,13},{10,... | collective-permute-start | bytes 1179656 | tf_op jit(solution)/shard_map/ppermute | solution.py:797
  153.3 8.9 %collective-permute-start.19 = (bf16[1,1,128,1536]{3,2,1,0:T(8,128)(2,1)S(1)}, bf16[1,1,128,1536]{3,2,1,0:T(8,128)(2,1)S(1)}, u32[]{:S(2)}, u32[]{:S(2)}) collective-permute-start(bf16[1,1,128,1536]{3,2,1,0:T(8,128)(2,1)S(1)} %get-tuple-element.94), channel_id=1, source_target_pairs={{0,2},{1,3},{2,0},{3,1},{4,6},{5,7},{6,4},{7,5},{8,10},{9,11},{10,... | collective-permute-start | bytes 1179656 | tf_op jit(solution)/shard_map/ppermute | solution.py:797
  163.4 18.5 %all-to-all-start.2 = ((bf16[8,128,384]{2,1,0:T(8,128)(2,1)}), bf16[8,128,384]{2,1,0:T(8,128)(2,1)S(1)}, u32[]{:S(2)}, u32[]{:S(2)}) async-start(bf16[8,128,384]{2,1,0:T(8,128)(2,1)} %merge.1), calls=%async_computation.2 | async-start | bytes 1572864 | tf_op jit(solution)/shard_map/all_to_all | solution.py:803
  166.9 4.3 %collective-permute-start.28 = (f32[8,2048]{1,0:T(8,128)S(1)}, f32[8,2048]{1,0:T(8,128)S(1)}, u32[]{:S(2)}, u32[]{:S(2)}) collective-permute-start(f32[8,2048]{1,0:T(8,128)S(1)} %added.9.refs_6_.refs_0_), channel_id=1, source_target_pairs={{0,16},{16,0},{1,17},{17,1},{2,18},{18,2},{3,19},{19,3},{4,20},{20... | collective-permute-start | bytes 196616 | tf_op jit(solution)/shard_map/ppermute | solution.py:800
  167.5 10.5 %collective-permute-start.20 = (f32[1,128]{1,0:T(1,128)S(1)}, f32[1,128]{1,0:T(1,128)S(1)}, u32[]{:S(2)}, u32[]{:S(2)}) collective-permute-start(f32[1,128]{1,0:T(1,128)S(1)} %slice.48), channel_id=1, source_target_pairs={{8,0},{9,1},{10,2},{11,3},{12,4},{13,5},{14,6},{15,7},{24,16},{25,... | collective-permute-start | bytes 1544 | tf_op jit(solution)/shard_map/ppermute | solution.py:938
  171.2 8.9 %collective-permute-start.29 = (f32[8,2048]{1,0:T(8,128)S(1)}, f32[8,2048]{1,0:T(8,128)S(1)}, u32[]{:S(2)}, u32[]{:S(2)}) collective-permute-start(f32[8,2048]{1,0:T(8,128)S(1)} %added.10.refs_0_), channel_id=1, source_target_pairs={{0,8},{1,9},{2,10},{3,11},{4,12},{5,13},{6,14},{7,15},{8,0},{9,1},... | collective-permute-start | bytes 196616 | tf_op jit(solution)/shard_map/ppermute | solution.py:794
  (15 other events, 241.3 us)

commit v5 on v4

--- a/solution.py
+++ b/solution.py
@@ -825,9 +825,9 @@
     mine = shared(dealt(weight))
     theirs = across(mine)
     beside = swapped(mine) if paired else mine
-    blocks = {0: stats(inputs, (1 - resets).astype(f32)[:, None, :], (mine,))}
+    blocks = {0: stats(inputs, (1 - resets).astype(f32)[:, None, :], ())}
     for bit in bits[::-1]:
-        blocks |= {d | bit: flipped(value, bit) for d, value in blocks.items()}
+        blocks |= {d | bit: flipped(fence(value, (beside,)) if d else value, bit) for d, value in blocks.items()}
     blocks = {d: fence(value, (theirs, beside)) for d, value in blocks.items()}
     blocks |= {d | 1: flipped(value, 1) for d, value in blocks.items()}
     blocks = [blocks[d] for d in range(group)]

time: 184 us -> 183 us (level)
  blocking collectives: 0 us -> 15.4 us
  waiting for transfers between devices: 83.8 us -> 72.1 us
  starting transfers between devices: 45.8 us -> 40.8 us
  local copies, waits for them, and re-layouts: 4.69 us -> 6.62 us
    all_to_all x0 -> x1, blocking collectives: none -> 15.4 us  [shared(): lax.all_to_all(value, 'fsdp', 0, 0, tiled=True, axis_index_groups=groups)]
    all_to_all x3 -> x2, waiting for transfers between devices: 11.1 us -> 0.01 us  [shared(): lax.all_to_all(value, 'fsdp', 0, 0, tiled=True, axis_index_groups=groups)]
    all_to_all x3 -> x2, starting transfers between devices: 12.7 us -> 7.9 us  [shared(): lax.all_to_all(value, 'fsdp', 0, 0, tiled=True, axis_index_groups=groups)]
    unnamed x28 -> x35, local copies, waits for them, and re-layouts: 3.11 us -> 5.04 us
  transfers between devices with their start and end apart: 33 -> 32, of which waited for: 21 -> 18; matrix products, arithmetic and copies ran while one was open for 2% -> 2% of each run, Pallas kernels for 13% -> 13%
where the time goes in v5:
time: 183 us; the launch traced here: 182 us
  waiting for transfers between devices  72.1 us (39%)
  Pallas kernels  44.3 us (24%)
  starting transfers between devices  40.8 us (22%)
  blocking collectives  15.4 us (8%)
  local copies, waits for them, and re-layouts  6.62 us (4%)
  other arithmetic  2.06 us (1%)
    ppermute x18, waiting for transfers between devices, flipped(): return lax.ppermute(value, 'fsdp', [(j, j ^ bit) for j in range(sections)])  55.1 us
    pallas_call x24, Pallas kernels, call(): pl.pallas_call(body, in_specs=[in_smem] * len(scalars) + [in_vmem] * len(...  44.3 us
    all_to_all x1, blocking collectives, shared(): lax.all_to_all(value, 'fsdp', 0, 0, tiled=True, axis_index_groups=groups)  15.4 us
    ppermute x5, starting transfers between devices, across(): lax.ppermute(value, 'fsdp', [(j, (j + group) % sections) for j in range(s...  13.5 us
    ppermute x18, starting transfers between devices, flipped(): return lax.ppermute(value, 'fsdp', [(j, j ^ bit) for j in range(sections)])  12 us
    all_to_all x2, starting transfers between devices, shared(): lax.all_to_all(value, 'fsdp', 0, 0, tiled=True, axis_index_groups=groups)  7.9 us
    ppermute x6, waiting for transfers between devices, swapped(): return lax.ppermute(value, 'dp', [(0, 1), (1, 0)])  6.26 us
    ppermute x6, starting transfers between devices, swapped(): return lax.ppermute(value, 'dp', [(0, 1), (1, 0)])  6.2 us
  transfers between devices with their start and end apart: 32, of which 18 were waited for; matrix products, arithmetic and copies ran while one was open for 2% of the time, Pallas kernels for 13%

profile of v5, /device:TPU:8, one launch (start us, length us, event | category | flops | bytes accessed | tf_op | source)
XLA Modules:
  0.0 182.3 jit_solution(17248186897952865302)
XLA Ops:
  2.0 15.4 %all_to_all.15.refs_3_ = bf16[8,128,384]{2,1,0:T(8,128)(2,1)} all-to-all(bf16[8,128,384]{2,1,0:T(8,128)(2,1)S(1)} %deal.2), channel_id=1, replica_groups={{0,1,2,3,4,5,6,7},{8,9,10,11,12,13,14,15},{16,17,18,19,20,21,22,23},{24..., dimensions={0} | all-to-all | bytes 1572864 | tf_op jit(solution)/shard_map/all_to_all | solution.py:803
  17.3 1.5 collective-permute-start.1
  19.9 2.6 %collective-permute-start = (bf16[8,128,384]{2,1,0:T(8,128)(2,1)}, bf16[8,128,384]{2,1,0:T(8,128)(2,1)S(1)}, u32[]{:S(2)}, u32[]{:S(2)}) collective-permute-start(bf16[8,128,384]{2,1,0:T(8,128)(2,1)} %all_to_all.15.refs_3_), channel_id=1, source_target_pairs={{0,8},{1,9},{2,10},{3,11},{4,12},{5,13},{6,14},{7,15},{8,0},{9,1},... | collective-permute-start | bytes 2359304 | tf_op jit(solution)/shard_map/ppermute | solution.py:794
  24.9 4.0 %all-to-all-start.1 = ((bf16[8,1,128,256]{3,2,1,0:T(8,128)(2,1)}), bf16[8,1,128,256]{3,2,1,0:T(8,128)(2,1)S(1)}, u32[]{:S(2)}, u32[]{:S(2)}) async-start(bf16[8,1,128,256]{3,2,1,0:T(8,128)(2,1)} %bitcast.41), calls=%async_computation.1 | async-start | bytes 1048576 | tf_op jit(solution)/shard_map/all_to_all | solution.py:803
  28.9 17.4 %collective-permute-done.5.refs_0_ = bf16[1,144,2048]{2,1,0:T(8,128)(2,1)S(1)} collective-permute-done((bf16[1,144,2048]{2,1,0:T(8,128)(2,1)S(1)}, bf16[1,144,2048]{2,1,0:T(8,128)(2,1)S(1)}, u32[]{:S(2)}, u32[]{:S(2)}) %collective-permute-start.5) | collective-permute-done | bytes 589856 | tf_op jit(solution)/shard_map/ppermute | solution.py:797
  48.0 1.9 %collective-permute-start.7 = (bf16[1,144,2048]{2,1,0:T(8,128)(2,1)}, bf16[1,144,2048]{2,1,0:T(8,128)(2,1)}, u32[]{:S(2)}, u32[]{:S(2)}) collective-permute-start(bf16[1,144,2048]{2,1,0:T(8,128)(2,1)} %fence.8), channel_id=1, source_target_pairs={{0,2},{1,3},{2,0},{3,1},{4,6},{5,7},{6,4},{7,5},{8,10},{9,11},{10,... | collective-permute-start | bytes 1769480 | tf_op jit(solution)/shard_map/ppermute | solution.py:797
  50.7 5.2 %collective-permute-done.refs_1_.refs_9_ = bf16[8,128,384]{2,1,0:T(8,128)(2,1)S(1)} collective-permute-done((bf16[8,128,384]{2,1,0:T(8,128)(2,1)}, bf16[8,128,384]{2,1,0:T(8,128)(2,1)S(1)}, u32[]{:S(2)}, u32[]{:S(2)}) %collective-permute-start) | collective-permute-done | bytes 786464 | tf_op jit(solution)/shard_map/ppermute | solution.py:794
  57.4 6.0 %collective-permute-done.7.refs_0_ = bf16[1,144,2048]{2,1,0:T(8,128)(2,1)} collective-permute-done((bf16[1,144,2048]{2,1,0:T(8,128)(2,1)}, bf16[1,144,2048]{2,1,0:T(8,128)(2,1)}, u32[]{:S(2)}, u32[]{:S(2)}) %collective-permute-start.7) | collective-permute-done | bytes 589856 | tf_op jit(solution)/shard_map/ppermute | solution.py:797
  65.7 4.2 %norm.1 = (bf16[1,1024,2048]{2,1,0:T(8,128)(2,1)S(1)}, f32[1,2,1024,128]{3,2,1,0:T(8,128)S(1)}, f32[1,1088,128]{2,1,0:T(8,128)S(1)}, bf16[1,2,1024,128]{3,2,1,0:T(8,128)(2,1)S(1)}) custom-call(s32[5]{0:T(128)S(1)} %stack.23.refs_0_, f32[1,2048]{1,0:T(1,128)S(1)} %bitcast.43, f32[1,2048]{1,0:T(1,128)S(1)} %bitcast.46, bf16[1,144,2048]{2,1,0:T(8,128)(2,1)S(1)} %copy-done.8, ...), custom_call_target="tpu_custom_call" | custom-call | tf_op jit(solution)/shard_map/norm/pallas_call | solution.py:43
  70.0 3.9 %project.1 = (f32[1,6,1024,128]{3,2,1,0:T(8,128)S(1)}, f32[16,768]{1,0:T(8,128)S(1)}, bf16[1024,768]{1,0:T(8,128)(2,1)S(1)}) custom-call(s32[5]{0:T(128)S(1)} %stack.23.refs_0_, bf16[1,1024,2048]{2,1,0:T(8,128)(2,1)S(1)} %get-tuple-element.58.refs_1_.refs_0_, bf16[16,2048]{1,0:T(8,128)(2,1)S(1)} %pad.4.refs_2_, bf16[8,128,384]{2,1,0:T(8,128)(2,1)} %all_to_all.15.refs_3_, ...), custom_call_target="tpu_custom_call" | custom-call | tf_op jit(solution)/shard_map/project/pallas_call | solution.py:43
  73.9 7.8 %blocks_forward.1 = (f32[1,6,1088,128]{3,2,1,0:T(8,128)S(1)}, f32[1,2,1088,128]{3,2,1,0:T(8,128)S(1)}, f32[1,2,336,128]{3,2,1,0:T(8,128)S(1)}, f32[1,1,256]{2,1,...) custom-call(s32[5]{0:T(128)S(1)} %stack.23.refs_0_, ...), custom_call_target="tpu_custom_call" | custom-call | tf_op jit(solution)/shard_map/blocks_forward/pallas_call | solution.py:43
  81.7 3.2 %collective-permute-start.10 = (f32[1,1,256]{2,1,0:T(1,128)S(1)}, f32[1,1,256]{2,1,0:T(1,128)S(1)}, u32[]{:S(2)}, u32[]{:S(2)}) collective-permute-start(f32[1,1,256]{2,1,0:T(1,128)S(1)} %get-tuple-element.67), channel_id=1, source_target_pairs={{0,8},{1,9},{2,10},{3,11},{4,12},{5,13},{6,14},{7,15},{8,0},{9,1},... | collective-permute-start | bytes 3080 | tf_op jit(solution)/shard_map/ppermute | solution.py:794
  86.5 2.3 %entry.1 = (f32[1,2,200,128]{3,2,1,0:T(8,128)S(1)}, f32[1,1,256]{2,1,0:T(1,128)S(1)}) custom-call(f32[1,6,1088,128]{3,2,1,0:T(8,128)S(1)} %get-tuple-element.62.refs_0_.refs_1_, f32[1,1088,128]{2,1,0:T(8,128)S(1)} %get-tuple-element.61.refs_6_.refs_1_.refs_2_, f32[1,2,1088,128]{3,2,1,0:T(8,128)S(1)} %get-tuple-element.63.refs_2_.refs_3_, ...), custom_call_target="tpu_custom_call" | custom-call | tf_op jit(solution)/shard_map/entry/pallas_call | solution.py:43
  88.8 3.0 %collective-permute-start.11 = (f32[1,1,256]{2,1,0:T(1,128)S(1)}, f32[1,1,256]{2,1,0:T(1,128)S(1)}, u32[]{:S(2)}, u32[]{:S(2)}) collective-permute-start(f32[1,1,256]{2,1,0:T(1,128)S(1)} %get-tuple-element.69), channel_id=1, source_target_pairs={{0,8},{1,9},{2,10},{3,11},{4,12},{5,13},{6,14},{7,15},{8,0},{9,1},... | collective-permute-start | bytes 3080 | tf_op jit(solution)/shard_map/ppermute | solution.py:794
  91.8 4.1 %lead_forward.1.refs_4_ = f32[1,2,816,128]{3,2,1,0:T(8,128)S(1)} custom-call(f32[1,6,1088,128]{3,2,1,0:T(8,128)S(1)} %get-tuple-element.62.refs_0_.refs_1_, f32[1,1088,128]{2,1,0:T(8,128)S(1)} %get-tuple-element.61.refs_6_.refs_1_.refs_2_, f32[1,256]{1,0:T(1,128)S(1)} %fusion.7.refs_7_.refs_2_.refs_5_.refs_8_, f32[1,1,256]{2,1,0:T(1,128)S(1)} %get-tuple-element.64.refs_3_, ...), custom_call_target="tpu_custom_call" | custom-call | tf_op jit(solution)/shard_map/lead_forward/pallas_call | solution.py:43
  95.9 5.1 %backward.1 = (bf16[1,1024,768]{2,1,0:T(8,128)(2,1)S(1)}, bf16[8,1,128,256]{3,2,1,0:T(8,128)(2,1)S(1)}, bf16[1,2,1024,128]{3,2,1,0:T(8,128)(2,1)S(1)}, f32[8,768...) custom-call(s32[5]{0:T(128)S(1)} %stack.23.refs_0_, ...), custom_call_target="tpu_custom_call" | custom-call | tf_op jit(solution)/shard_map/backward/pallas_call | solution.py:43
  100.9 2.2 %weight_back.2 = (f32[2,1024]{1,0:T(2,128)S(1)}, bf16[8,128,384]{2,1,0:T(8,128)(2,1)S(1)}, bf16[8,144,384]{2,1,0:T(8,128)(2,1)S(1)}) custom-call(bf16[1,1024,2048]{2,1,0:T(8,128)(2,1)S(1)} %get-tuple-element.58.refs_1_.refs_0_, bf16[1,1024,768]{2,1,0:T(8,128)(2,1)S(1)} %get-tuple-element.72.refs_1_.refs_3_, f32[8,768]{1,0:T(8,128)S(1)} %get-tuple-element.77.refs_2_.refs_1_, ...), custom_call_target="tpu_custom_call" | custom-call | tf_op jit(solution)/shard_map/weight_back/pallas_call | solution.py:43
  103.7 6.2 %norm_back.1 = (bf16[2,1,128,1152]{3,2,1,0:T(8,128)(2,1)S(1)}, bf16[2,1,128,1152]{3,2,1,0:T(8,128)(2,1)S(1)}, bf16[2,1,128,1152]{3,2,1,0:T(8,128)(2,1)S(1)}, bf1...) custom-call(s32[5]{0:T(128)S(1)} %stack.23.refs_0_, ...), custom_call_target="tpu_custom_call" | custom-call | tf_op jit(solution)/shard_map/norm_back/pallas_call | solution.py:43
  116.0 4.8 %collective-permute-done.21.refs_1_ = bf16[8,144,384]{2,1,0:T(8,128)(2,1)S(1)} collective-permute-done((bf16[8,144,384]{2,1,0:T(8,128)(2,1)S(1)}, bf16[8,144,384]{2,1,0:T(8,128)(2,1)S(1)}, u32[]{:S(2)}, u32[]{:S(2)}) %collective-permute-start.21) | collective-permute-done | bytes 884768 | tf_op jit(solution)/shard_map/ppermute | solution.py:800
  121.0 2.5 %collective-permute-start.22 = (bf16[8,128,384]{2,1,0:T(8,128)(2,1)S(1)}, bf16[8,128,384]{2,1,0:T(8,128)(2,1)S(1)}, u32[]{:S(2)}, u32[]{:S(2)}) collective-permute-start(bf16[8,128,384]{2,1,0:T(8,128)(2,1)S(1)} %added.6.refs_5_), channel_id=1, source_target_pairs={{0,8},{1,9},{2,10},{3,11},{4,12},{5,13},{6,14},{7,15},{8,0},{9,1},... | collective-permute-start | bytes 2359304 | tf_op jit(solution)/shard_map/ppermute | solution.py:794
  123.5 2.2 %weight_back.3 = (f32[2,1024]{1,0:T(2,128)S(1)}, bf16[8,128,384]{2,1,0:T(8,128)(2,1)S(1)}, bf16[8,64,384]{2,1,0:T(8,128)(2,1)S(1)}, bf16[8,64,384]{2,1,0:T(8,128)(2,1)S(1)}) custom-call(bf16[1,1024,2048]{2,1,0:T(8,128)(2,1)S(1)} %get-tuple-element.58.refs_1_.refs_0_, bf16[1,1024,768]{2,1,0:T(8,128)(2,1)S(1)} %get-tuple-element.72.refs_1_.refs_3_, ...), custom_call_target="tpu_custom_call" | custom-call | tf_op jit(solution)/shard_map/weight_back/pallas_call | solution.py:43
  129.0 4.3 %collective-permute-done.26.refs_1_ = f32[8,2048]{1,0:T(8,128)S(1)} collective-permute-done((f32[8,2048]{1,0:T(8,128)S(1)}, f32[8,2048]{1,0:T(8,128)S(1)}, u32[]{:S(2)}, u32[]{:S(2)}) %collective-permute-start.26) | collective-permute-done | bytes 65568 | tf_op jit(solution)/shard_map/ppermute | solution.py:797
  133.4 1.6 collective-permute-start.23
  135.5 4.8 %collective-permute-done.17.refs_3_ = bf16[2,1,128,1280]{3,2,1,0:T(8,128)(2,1)S(1)} collective-permute-done((bf16[2,1,128,1280]{3,2,1,0:T(8,128)(2,1)S(1)}, bf16[2,1,128,1280]{3,2,1,0:T(8,128)(2,1)S(1)}, u32[]{:S(2)}, u32[]{:S(2)}) %collective-permute-start.17) | collective-permute-done | bytes 655392 | tf_op jit(solution)/shard_map/ppermute | solution.py:797
  140.5 2.5 %collective-permute-start.18 = (bf16[1,1,128,1536]{3,2,1,0:T(8,128)(2,1)S(1)}, bf16[1,1,128,1536]{3,2,1,0:T(8,128)(2,1)S(1)}, u32[]{:S(2)}, u32[]{:S(2)}) collective-permute-start(bf16[1,1,128,1536]{3,2,1,0:T(8,128)(2,1)S(1)} %get-tuple-element.93), channel_id=1, source_target_pairs={{0,4},{1,5},{2,6},{3,7},{4,0},{5,1},{6,2},{7,3},{8,12},{9,13},{10,... | collective-permute-start | bytes 1179656 | tf_op jit(solution)/shard_map/ppermute | solution.py:797
  143.1 8.8 %collective-permute-done.27.refs_1_ = f32[8,2048]{1,0:T(8,128)S(1)} collective-permute-done((f32[8,2048]{1,0:T(8,128)S(1)}, f32[8,2048]{1,0:T(8,128)S(1)}, u32[]{:S(2)}, u32[]{:S(2)}) %collective-permute-start.27) | collective-permute-done | bytes 65568 | tf_op jit(solution)/shard_map/ppermute | solution.py:797
  153.1 6.1 %collective-permute-done.18.refs_3_.refs_4_ = bf16[1,1,128,1536]{3,2,1,0:T(8,128)(2,1)S(1)} collective-permute-done((bf16[1,1,128,1536]{3,2,1,0:T(8,128)(2,1)S(1)}, bf16[1,1,128,1536]{3,2,1,0:T(8,128)(2,1)S(1)}, u32[]{:S(2)}, u32[]{:S(2)}) %collective-permute-start.18) | collective-permute-done | bytes 393248 | tf_op jit(solution)/shard_map/ppermute | solution.py:797
  159.2 1.6 collective-permute-done.19.refs_4_.refs_5_
  162.0 3.9 %all-to-all-start.2 = ((bf16[8,128,384]{2,1,0:T(8,128)(2,1)}), bf16[8,128,384]{2,1,0:T(8,128)(2,1)S(1)}, u32[]{:S(2)}, u32[]{:S(2)}) async-start(bf16[8,128,384]{2,1,0:T(8,128)(2,1)} %merge.1), calls=%async_computation.2 | async-start | bytes 1572864 | tf_op jit(solution)/shard_map/all_to_all | solution.py:803
  170.2 2.2 %collective-permute-start.29 = (f32[8,2048]{1,0:T(8,128)S(1)}, f32[8,2048]{1,0:T(8,128)S(1)}, u32[]{:S(2)}, u32[]{:S(2)}) collective-permute-start(f32[8,2048]{1,0:T(8,128)S(1)} %added.10.refs_0_), channel_id=1, source_target_pairs={{0,8},{1,9},{2,10},{3,11},{4,12},{5,13},{6,14},{7,15},{8,0},{9,1},... | collective-permute-start | bytes 196616 | tf_op jit(solution)/shard_map/ppermute | solution.py:794
  172.3 4.7 %collective-permute-done.20 = f32[1,128]{1,0:T(1,128)S(1)} collective-permute-done((f32[1,128]{1,0:T(1,128)S(1)}, f32[1,128]{1,0:T(1,128)S(1)}, u32[]{:S(2)}, u32[]{:S(2)}) %collective-permute-start.20) | collective-permute-done | bytes 544 | tf_op jit(solution)/shard_map/ppermute | solution.py:938
  177.5 1.7 finish.1
  (117 shorter events, 33.7 us)
Async XLA Ops:
  17.3 29.8 %collective-permute-start.1 = (bf16[8,128,384]{2,1,0:T(8,128)(2,1)}, bf16[8,128,384]{2,1,0:T(8,128)(2,1)S(1)}, u32[]{:S(2)}, u32[]{:S(2)}) collective-permute-start(bf16[8,128,384]{2,1,0:T(8,128)(2,1)} %all_to_all.15.refs_3_), channel_id=1, source_target_pairs={{0,16},{16,0},{1,17},{17,1},{2,18},{18,2},{3,19},{19,3},{4,20},{20... | collective-permute-start | bytes 2359304 | tf_op jit(solution)/shard_map/ppermute | solution.py:800
  19.2 27.0 %collective-permute-start.5 = (bf16[1,144,2048]{2,1,0:T(8,128)(2,1)S(1)}, bf16[1,144,2048]{2,1,0:T(8,128)(2,1)S(1)}, u32[]{:S(2)}, u32[]{:S(2)}) collective-permute-start(bf16[1,144,2048]{2,1,0:T(8,128)(2,1)S(1)} %stats.1.refs_0_), channel_id=1, source_target_pairs={{0,4},{1,5},{2,6},{3,7},{4,0},{5,1},{6,2},{7,3},{8,12},{9,13},{10,... | collective-permute-start | bytes 1769480 | tf_op jit(solution)/shard_map/ppermute | solution.py:797
  19.9 36.0 %collective-permute-start = (bf16[8,128,384]{2,1,0:T(8,128)(2,1)}, bf16[8,128,384]{2,1,0:T(8,128)(2,1)S(1)}, u32[]{:S(2)}, u32[]{:S(2)}) collective-permute-start(bf16[8,128,384]{2,1,0:T(8,128)(2,1)} %all_to_all.15.refs_3_), channel_id=1, source_target_pairs={{0,8},{1,9},{2,10},{3,11},{4,12},{5,13},{6,14},{7,15},{8,0},{9,1},... | collective-permute-start | bytes 2359304 | tf_op jit(solution)/shard_map/ppermute | solution.py:794
  22.5 34.3 %collective-permute-start.3 = (bf16[1,144,2048]{2,1,0:T(8,128)(2,1)S(1)}, bf16[1,144,2048]{2,1,0:T(8,128)(2,1)}, u32[]{:S(2)}, u32[]{:S(2)}) collective-permute-start(bf16[1,144,2048]{2,1,0:T(8,128)(2,1)S(1)} %stats.1.refs_0_), channel_id=1, source_target_pairs={{0,2},{1,3},{2,0},{3,1},{4,6},{5,7},{6,4},{7,5},{8,10},{9,11},{10,... | collective-permute-start | bytes 1769480 | tf_op jit(solution)/shard_map/ppermute | solution.py:797
  24.9 39.5 %all-to-all-start.1 = ((bf16[8,1,128,256]{3,2,1,0:T(8,128)(2,1)}), bf16[8,1,128,256]{3,2,1,0:T(8,128)(2,1)S(1)}, u32[]{:S(2)}, u32[]{:S(2)}) async-start(bf16[8,1,128,256]{3,2,1,0:T(8,128)(2,1)} %bitcast.41), calls=%async_computation.1 | async-start | bytes 1048576 | tf_op jit(solution)/shard_map/all_to_all | solution.py:803
  48.0 15.4 %collective-permute-start.7 = (bf16[1,144,2048]{2,1,0:T(8,128)(2,1)}, bf16[1,144,2048]{2,1,0:T(8,128)(2,1)}, u32[]{:S(2)}, u32[]{:S(2)}) collective-permute-start(bf16[1,144,2048]{2,1,0:T(8,128)(2,1)} %fence.8), channel_id=1, source_target_pairs={{0,2},{1,3},{2,0},{3,1},{4,6},{5,7},{6,4},{7,5},{8,10},{9,11},{10,... | collective-permute-start | bytes 1769480 | tf_op jit(solution)/shard_map/ppermute | solution.py:797
  55.9 18.0 %collective-permute-start.9 = (bf16[8,128,384]{2,1,0:T(8,128)(2,1)S(1)}, bf16[8,128,384]{2,1,0:T(8,128)(2,1)}, u32[]{:S(2)}, u32[]{:S(2)}) collective-permute-start(bf16[8,128,384]{2,1,0:T(8,128)(2,1)S(1)} %collective-permute-done.refs_1_.refs_9_), channel_id=1, source_target_pairs={{0,16},{16,0},{1,17},{17,1},{2,18},{18,2},{3,19},{19,3},{4,20},{20... | collective-permute-start | bytes 2359304 | tf_op jit(solution)/shard_map/ppermute | solution.py:800
  56.8 7.6 %collective-permute-start.6 = (bf16[1,144,2048]{2,1,0:T(8,128)(2,1)}, bf16[1,144,2048]{2,1,0:T(8,128)(2,1)}, u32[]{:S(2)}, u32[]{:S(2)}) collective-permute-start(bf16[1,144,2048]{2,1,0:T(8,128)(2,1)} %fence.7.refs_7_.refs_9_), channel_id=1, source_target_pairs={{0,1},{1,0},{2,3},{3,2},{4,5},{5,4},{6,7},{7,6},{8,9},{9,8},{10,11... | collective-permute-start | bytes 1769480 | tf_op jit(solution)/shard_map/ppermute | solution.py:797
  56.8 7.6 %collective-permute-start.4 = (bf16[1,144,2048]{2,1,0:T(8,128)(2,1)}, bf16[1,144,2048]{2,1,0:T(8,128)(2,1)S(1)}, u32[]{:S(2)}, u32[]{:S(2)}) collective-permute-start(bf16[1,144,2048]{2,1,0:T(8,128)(2,1)} %fence.6.refs_5_.refs_7_), channel_id=1, source_target_pairs={{0,1},{1,0},{2,3},{3,2},{4,5},{5,4},{6,7},{7,6},{8,9},{9,8},{10,11... | collective-permute-start | bytes 1769480 | tf_op jit(solution)/shard_map/ppermute | solution.py:797
  57.3 7.1 %collective-permute-start.2 = (bf16[1,144,2048]{2,1,0:T(8,128)(2,1)}, bf16[1,144,2048]{2,1,0:T(8,128)(2,1)}, u32[]{:S(2)}, u32[]{:S(2)}) collective-permute-start(bf16[1,144,2048]{2,1,0:T(8,128)(2,1)} %fence.5.refs_3_.refs_5_), channel_id=1, source_target_pairs={{0,1},{1,0},{2,3},{3,2},{4,5},{5,4},{6,7},{7,6},{8,9},{9,8},{10,11... | collective-permute-start | bytes 1769480 | tf_op jit(solution)/shard_map/ppermute | solution.py:797
  63.4 2.3 %collective-permute-start.8 = (bf16[1,144,2048]{2,1,0:T(8,128)(2,1)}, bf16[1,144,2048]{2,1,0:T(8,128)(2,1)}, u32[]{:S(2)}, u32[]{:S(2)}) collective-permute-start(bf16[1,144,2048]{2,1,0:T(8,128)(2,1)} %fence.9.refs_9_.refs_11_), channel_id=1, source_target_pairs={{0,1},{1,0},{2,3},{3,2},{4,5},{5,4},{6,7},{7,6},{8,9},{9,8},{10,11... | collective-permute-start | bytes 1769480 | tf_op jit(solution)/shard_map/ppermute | solution.py:797
  81.7 4.8 %collective-permute-start.10 = (f32[1,1,256]{2,1,0:T(1,128)S(1)}, f32[1,1,256]{2,1,0:T(1,128)S(1)}, u32[]{:S(2)}, u32[]{:S(2)}) collective-permute-start(f32[1,1,256]{2,1,0:T(1,128)S(1)} %get-tuple-element.67), channel_id=1, source_target_pairs={{0,8},{1,9},{2,10},{3,11},{4,12},{5,13},{6,14},{7,15},{8,0},{9,1},... | collective-permute-start | bytes 3080 | tf_op jit(solution)/shard_map/ppermute | solution.py:794
  88.8 7.1 %collective-permute-start.11 = (f32[1,1,256]{2,1,0:T(1,128)S(1)}, f32[1,1,256]{2,1,0:T(1,128)S(1)}, u32[]{:S(2)}, u32[]{:S(2)}) collective-permute-start(f32[1,1,256]{2,1,0:T(1,128)S(1)} %get-tuple-element.69), channel_id=1, source_target_pairs={{0,8},{1,9},{2,10},{3,11},{4,12},{5,13},{6,14},{7,15},{8,0},{9,1},... | collective-permute-start | bytes 3080 | tf_op jit(solution)/shard_map/ppermute | solution.py:794
  103.2 17.6 %collective-permute-start.21 = (bf16[8,144,384]{2,1,0:T(8,128)(2,1)S(1)}, bf16[8,144,384]{2,1,0:T(8,128)(2,1)S(1)}, u32[]{:S(2)}, u32[]{:S(2)}) collective-permute-start(bf16[8,144,384]{2,1,0:T(8,128)(2,1)S(1)} %get-tuple-element.99), channel_id=1, source_target_pairs={{0,16},{16,0},{1,17},{17,1},{2,18},{18,2},{3,19},{19,3},{4,20},{20... | collective-permute-start | bytes 2654216 | tf_op jit(solution)/shard_map/ppermute | solution.py:800
  109.9 2.1 %collective-permute-start.12 = (bf16[2,1,128,1152]{3,2,1,0:T(8,128)(2,1)S(1)}, bf16[2,1,128,1152]{3,2,1,0:T(8,128)(2,1)S(1)}, u32[]{:S(2)}, u32[]{:S(2)}) collective-permute-start(bf16[2,1,128,1152]{3,2,1,0:T(8,128)(2,1)S(1)} %get-tuple-element.83), channel_id=1, source_target_pairs={{0,1},{1,0},{2,3},{3,2},{4,5},{5,4},{6,7},{7,6},{8,9},{9,8},{10,11... | collective-permute-start | bytes 1769480 | tf_op jit(solution)/shard_map/ppermute | solution.py:797
  110.0 2.8 %collective-permute-start.13 = (bf16[2,1,128,1152]{3,2,1,0:T(8,128)(2,1)S(1)}, bf16[2,1,128,1152]{3,2,1,0:T(8,128)(2,1)S(1)}, u32[]{:S(2)}, u32[]{:S(2)}) collective-permute-start(bf16[2,1,128,1152]{3,2,1,0:T(8,128)(2,1)S(1)} %get-tuple-element.84), channel_id=1, source_target_pairs={{0,1},{1,0},{2,3},{3,2},{4,5},{5,4},{6,7},{7,6},{8,9},{9,8},{10,11... | collective-permute-start | bytes 1769480 | tf_op jit(solution)/shard_map/ppermute | solution.py:797
  110.5 3.2 %collective-permute-start.14 = (bf16[2,1,128,1152]{3,2,1,0:T(8,128)(2,1)S(1)}, bf16[2,1,128,1152]{3,2,1,0:T(8,128)(2,1)S(1)}, u32[]{:S(2)}, u32[]{:S(2)}) collective-permute-start(bf16[2,1,128,1152]{3,2,1,0:T(8,128)(2,1)S(1)} %get-tuple-element.85), channel_id=1, source_target_pairs={{0,1},{1,0},{2,3},{3,2},{4,5},{5,4},{6,7},{7,6},{8,9},{9,8},{10,11... | collective-permute-start | bytes 1769480 | tf_op jit(solution)/shard_map/ppermute | solution.py:797
  110.6 3.9 %collective-permute-start.15 = (bf16[2,1,128,1152]{3,2,1,0:T(8,128)(2,1)S(1)}, bf16[2,1,128,1152]{3,2,1,0:T(8,128)(2,1)S(1)}, u32[]{:S(2)}, u32[]{:S(2)}) collective-permute-start(bf16[2,1,128,1152]{3,2,1,0:T(8,128)(2,1)S(1)} %get-tuple-element.86), channel_id=1, source_target_pairs={{0,1},{1,0},{2,3},{3,2},{4,5},{5,4},{6,7},{7,6},{8,9},{9,8},{10,11... | collective-permute-start | bytes 1769480 | tf_op jit(solution)/shard_map/ppermute | solution.py:797
  115.0 19.9 %collective-permute-start.16 = (bf16[2,1,128,1280]{3,2,1,0:T(8,128)(2,1)S(1)}, bf16[2,1,128,1280]{3,2,1,0:T(8,128)(2,1)S(1)}, u32[]{:S(2)}, u32[]{:S(2)}) collective-permute-start(bf16[2,1,128,1280]{3,2,1,0:T(8,128)(2,1)S(1)} %get-tuple-element.89), channel_id=1, source_target_pairs={{0,2},{1,3},{2,0},{3,1},{4,6},{5,7},{6,4},{7,5},{8,10},{9,11},{10,... | collective-permute-start | bytes 1966088 | tf_op jit(solution)/shard_map/ppermute | solution.py:797
  116.0 24.3 %collective-permute-start.17 = (bf16[2,1,128,1280]{3,2,1,0:T(8,128)(2,1)S(1)}, bf16[2,1,128,1280]{3,2,1,0:T(8,128)(2,1)S(1)}, u32[]{:S(2)}, u32[]{:S(2)}) collective-permute-start(bf16[2,1,128,1280]{3,2,1,0:T(8,128)(2,1)S(1)} %get-tuple-element.90), channel_id=1, source_target_pairs={{0,4},{1,5},{2,6},{3,7},{4,0},{5,1},{6,2},{7,3},{8,12},{9,13},{10,... | collective-permute-start | bytes 1966088 | tf_op jit(solution)/shard_map/ppermute | solution.py:797
  121.0 39.8 %collective-permute-start.22 = (bf16[8,128,384]{2,1,0:T(8,128)(2,1)S(1)}, bf16[8,128,384]{2,1,0:T(8,128)(2,1)S(1)}, u32[]{:S(2)}, u32[]{:S(2)}) collective-permute-start(bf16[8,128,384]{2,1,0:T(8,128)(2,1)S(1)} %added.6.refs_5_), channel_id=1, source_target_pairs={{0,8},{1,9},{2,10},{3,11},{4,12},{5,13},{6,14},{7,15},{8,0},{9,1},... | collective-permute-start | bytes 2359304 | tf_op jit(solution)/shard_map/ppermute | solution.py:794
  126.2 1.3 collective-permute-start.25
  127.6 5.7 %collective-permute-start.26 = (f32[8,2048]{1,0:T(8,128)S(1)}, f32[8,2048]{1,0:T(8,128)S(1)}, u32[]{:S(2)}, u32[]{:S(2)}) collective-permute-start(f32[8,2048]{1,0:T(8,128)S(1)} %added.7.refs_0_), channel_id=1, source_target_pairs={{0,2},{1,3},{2,0},{3,1},{4,6},{5,7},{6,4},{7,5},{8,10},{9,11},{10,... | collective-permute-start | bytes 196616 | tf_op jit(solution)/shard_map/ppermute | solution.py:797
  133.3 18.6 %collective-permute-start.27 = (f32[8,2048]{1,0:T(8,128)S(1)}, f32[8,2048]{1,0:T(8,128)S(1)}, u32[]{:S(2)}, u32[]{:S(2)}) collective-permute-start(f32[8,2048]{1,0:T(8,128)S(1)} %added.8.refs_0_), channel_id=1, source_target_pairs={{0,4},{1,5},{2,6},{3,7},{4,0},{5,1},{6,2},{7,3},{8,12},{9,13},{10,... | collective-permute-start | bytes 196616 | tf_op jit(solution)/shard_map/ppermute | solution.py:797
  133.4 19.7 %collective-permute-start.23 = (bf16[8,64,384]{2,1,0:T(8,128)(2,1)S(1)}, bf16[8,64,384]{2,1,0:T(8,128)(2,1)S(1)}, u32[]{:S(2)}, u32[]{:S(2)}) collective-permute-start(bf16[8,64,384]{2,1,0:T(8,128)(2,1)S(1)} %get-tuple-element.101), channel_id=1, source_target_pairs={{0,16},{16,0},{1,17},{17,1},{2,18},{18,2},{3,19},{19,3},{4,20},{20... | collective-permute-start | bytes 1179656 | tf_op jit(solution)/shard_map/ppermute | solution.py:800
  135.0 18.1 %collective-permute-start.24 = (bf16[8,64,384]{2,1,0:T(8,128)(2,1)S(1)}, bf16[8,64,384]{2,1,0:T(8,128)(2,1)S(1)}, u32[]{:S(2)}, u32[]{:S(2)}) collective-permute-start(bf16[8,64,384]{2,1,0:T(8,128)(2,1)S(1)} %get-tuple-element.102), channel_id=1, source_target_pairs={{0,16},{16,0},{1,17},{17,1},{2,18},{18,2},{3,19},{19,3},{4,20},{20... | collective-permute-start | bytes 1179656 | tf_op jit(solution)/shard_map/ppermute | solution.py:800
  140.5 18.7 %collective-permute-start.18 = (bf16[1,1,128,1536]{3,2,1,0:T(8,128)(2,1)S(1)}, bf16[1,1,128,1536]{3,2,1,0:T(8,128)(2,1)S(1)}, u32[]{:S(2)}, u32[]{:S(2)}) collective-permute-start(bf16[1,1,128,1536]{3,2,1,0:T(8,128)(2,1)S(1)} %get-tuple-element.93), channel_id=1, source_target_pairs={{0,4},{1,5},{2,6},{3,7},{4,0},{5,1},{6,2},{7,3},{8,12},{9,13},{10,... | collective-permute-start | bytes 1179656 | tf_op jit(solution)/shard_map/ppermute | solution.py:797
  151.9 8.9 %collective-permute-start.19 = (bf16[1,1,128,1536]{3,2,1,0:T(8,128)(2,1)S(1)}, bf16[1,1,128,1536]{3,2,1,0:T(8,128)(2,1)S(1)}, u32[]{:S(2)}, u32[]{:S(2)}) collective-permute-start(bf16[1,1,128,1536]{3,2,1,0:T(8,128)(2,1)S(1)} %get-tuple-element.94), channel_id=1, source_target_pairs={{0,2},{1,3},{2,0},{3,1},{4,6},{5,7},{6,4},{7,5},{8,10},{9,11},{10,... | collective-permute-start | bytes 1179656 | tf_op jit(solution)/shard_map/ppermute | solution.py:797
  162.0 19.0 %all-to-all-start.2 = ((bf16[8,128,384]{2,1,0:T(8,128)(2,1)}), bf16[8,128,384]{2,1,0:T(8,128)(2,1)S(1)}, u32[]{:S(2)}, u32[]{:S(2)}) async-start(bf16[8,128,384]{2,1,0:T(8,128)(2,1)} %merge.1), calls=%async_computation.2 | async-start | bytes 1572864 | tf_op jit(solution)/shard_map/all_to_all | solution.py:803
  165.9 4.3 %collective-permute-start.28 = (f32[8,2048]{1,0:T(8,128)S(1)}, f32[8,2048]{1,0:T(8,128)S(1)}, u32[]{:S(2)}, u32[]{:S(2)}) collective-permute-start(f32[8,2048]{1,0:T(8,128)S(1)} %added.9.refs_6_.refs_0_), channel_id=1, source_target_pairs={{0,16},{16,0},{1,17},{17,1},{2,18},{18,2},{3,19},{19,3},{4,20},{20... | collective-permute-start | bytes 196616 | tf_op jit(solution)/shard_map/ppermute | solution.py:800
  167.4 9.6 %collective-permute-start.20 = (f32[1,128]{1,0:T(1,128)S(1)}, f32[1,128]{1,0:T(1,128)S(1)}, u32[]{:S(2)}, u32[]{:S(2)}) collective-permute-start(f32[1,128]{1,0:T(1,128)S(1)} %slice.48), channel_id=1, source_target_pairs={{8,0},{9,1},{10,2},{11,3},{12,4},{13,5},{14,6},{15,7},{24,16},{25,... | collective-permute-start | bytes 1544 | tf_op jit(solution)/shard_map/ppermute | solution.py:938
  170.2 9.1 %collective-permute-start.29 = (f32[8,2048]{1,0:T(8,128)S(1)}, f32[8,2048]{1,0:T(8,128)S(1)}, u32[]{:S(2)}, u32[]{:S(2)}) collective-permute-start(f32[8,2048]{1,0:T(8,128)S(1)} %added.10.refs_0_), channel_id=1, source_target_pairs={{0,8},{1,9},{2,10},{3,11},{4,12},{5,13},{6,14},{7,15},{8,0},{9,1},... | collective-permute-start | bytes 196616 | tf_op jit(solution)/shard_map/ppermute | solution.py:794
  (17 other events, 221.2 us)

commit v6 on v5

--- a/solution.py
+++ b/solution.py
@@ -19,7 +19,7 @@
 COVERED = EARLY + 2 * BLOCK
 STATS = 16
 SPARE = 16
-UNROLL = 8
+UNROLL = 16
 TOGETHER = 8
 f32 = jnp.float32
 bf16 = jnp.bfloat16

time: 183 us -> 182 us (level)
  no operation moved by 1% of the time
where the time goes in v6:
time: 182 us
  waiting for transfers between devices  72.1 us (40%)
  Pallas kernels  43.6 us (24%)
  starting transfers between devices  40.8 us (22%)
  blocking collectives  15.4 us (8%)
  local copies, waits for them, and re-layouts  6.62 us (4%)
  other arithmetic  2.06 us (1%)
    ppermute x18, waiting for transfers between devices, flipped(): return lax.ppermute(value, 'fsdp', [(j, j ^ bit) for j in range(sections)])  55.1 us
    pallas_call x24, Pallas kernels, call(): pl.pallas_call(body, in_specs=[in_smem] * len(scalars) + [in_vmem] * len(...  43.6 us
    all_to_all x1, blocking collectives, shared(): lax.all_to_all(value, 'fsdp', 0, 0, tiled=True, axis_index_groups=groups)  15.4 us
    ppermute x5, starting transfers between devices, across(): lax.ppermute(value, 'fsdp', [(j, (j + group) % sections) for j in range(s...  13.5 us
    ppermute x18, starting transfers between devices, flipped(): return lax.ppermute(value, 'fsdp', [(j, j ^ bit) for j in range(sections)])  12 us
    all_to_all x2, starting transfers between devices, shared(): lax.all_to_all(value, 'fsdp', 0, 0, tiled=True, axis_index_groups=groups)  7.88 us
    ppermute x6, waiting for transfers between devices, swapped(): return lax.ppermute(value, 'dp', [(0, 1), (1, 0)])  6.22 us
    ppermute x6, starting transfers between devices, swapped(): return lax.ppermute(value, 'dp', [(0, 1), (1, 0)])  6.21 us
  transfers between devices with their start and end apart: 32, of which 18 were waited for; matrix products, arithmetic and copies ran while one was open for 2% of the time, Pallas kernels for 13%

profile of v6, /device:TPU:8, one launch (start us, length us, event | category | flops | bytes accessed | tf_op | source)
XLA Modules:
  0.0 181.6 jit_solution(10412822368132657120)
XLA Ops:
  2.0 15.4 %all_to_all.15.refs_3_ = bf16[8,128,384]{2,1,0:T(8,128)(2,1)} all-to-all(bf16[8,128,384]{2,1,0:T(8,128)(2,1)S(1)} %deal.2), channel_id=1, replica_groups={{0,1,2,3,4,5,6,7},{8,9,10,11,12,13,14,15},{16,17,18,19,20,21,22,23},{24..., dimensions={0} | all-to-all | bytes 1572864 | tf_op jit(solution)/shard_map/all_to_all | solution.py:803
  19.9 2.6 %collective-permute-start = (bf16[8,128,384]{2,1,0:T(8,128)(2,1)}, bf16[8,128,384]{2,1,0:T(8,128)(2,1)S(1)}, u32[]{:S(2)}, u32[]{:S(2)}) collective-permute-start(bf16[8,128,384]{2,1,0:T(8,128)(2,1)} %all_to_all.15.refs_3_), channel_id=1, source_target_pairs={{0,8},{1,9},{2,10},{3,11},{4,12},{5,13},{6,14},{7,15},{8,0},{9,1},... | collective-permute-start | bytes 2359304 | tf_op jit(solution)/shard_map/ppermute | solution.py:794
  24.9 4.0 %all-to-all-start.1 = ((bf16[8,1,128,256]{3,2,1,0:T(8,128)(2,1)}), bf16[8,1,128,256]{3,2,1,0:T(8,128)(2,1)S(1)}, u32[]{:S(2)}, u32[]{:S(2)}) async-start(bf16[8,1,128,256]{3,2,1,0:T(8,128)(2,1)} %bitcast.41), calls=%async_computation.1 | async-start | bytes 1048576 | tf_op jit(solution)/shard_map/all_to_all | solution.py:803
  28.9 17.4 %collective-permute-done.5.refs_0_ = bf16[1,144,2048]{2,1,0:T(8,128)(2,1)S(1)} collective-permute-done((bf16[1,144,2048]{2,1,0:T(8,128)(2,1)S(1)}, bf16[1,144,2048]{2,1,0:T(8,128)(2,1)S(1)}, u32[]{:S(2)}, u32[]{:S(2)}) %collective-permute-start.5) | collective-permute-done | bytes 589856 | tf_op jit(solution)/shard_map/ppermute | solution.py:797
  48.0 1.9 %collective-permute-start.7 = (bf16[1,144,2048]{2,1,0:T(8,128)(2,1)}, bf16[1,144,2048]{2,1,0:T(8,128)(2,1)}, u32[]{:S(2)}, u32[]{:S(2)}) collective-permute-start(bf16[1,144,2048]{2,1,0:T(8,128)(2,1)} %fence.8), channel_id=1, source_target_pairs={{0,2},{1,3},{2,0},{3,1},{4,6},{5,7},{6,4},{7,5},{8,10},{9,11},{10,... | collective-permute-start | bytes 1769480 | tf_op jit(solution)/shard_map/ppermute | solution.py:797
  50.7 5.2 %collective-permute-done.refs_1_.refs_9_ = bf16[8,128,384]{2,1,0:T(8,128)(2,1)S(1)} collective-permute-done((bf16[8,128,384]{2,1,0:T(8,128)(2,1)}, bf16[8,128,384]{2,1,0:T(8,128)(2,1)S(1)}, u32[]{:S(2)}, u32[]{:S(2)}) %collective-permute-start) | collective-permute-done | bytes 786464 | tf_op jit(solution)/shard_map/ppermute | solution.py:794
  57.4 6.0 %collective-permute-done.7.refs_0_ = bf16[1,144,2048]{2,1,0:T(8,128)(2,1)} collective-permute-done((bf16[1,144,2048]{2,1,0:T(8,128)(2,1)}, bf16[1,144,2048]{2,1,0:T(8,128)(2,1)}, u32[]{:S(2)}, u32[]{:S(2)}) %collective-permute-start.7) | collective-permute-done | bytes 589856 | tf_op jit(solution)/shard_map/ppermute | solution.py:797
  65.7 4.2 %norm.1 = (bf16[1,1024,2048]{2,1,0:T(8,128)(2,1)S(1)}, f32[1,2,1024,128]{3,2,1,0:T(8,128)S(1)}, f32[1,1088,128]{2,1,0:T(8,128)S(1)}, bf16[1,2,1024,128]{3,2,1,0:T(8,128)(2,1)S(1)}) custom-call(s32[5]{0:T(128)S(1)} %stack.23.refs_0_, f32[1,2048]{1,0:T(1,128)S(1)} %bitcast.43, f32[1,2048]{1,0:T(1,128)S(1)} %bitcast.46, bf16[1,144,2048]{2,1,0:T(8,128)(2,1)S(1)} %copy-done.8, ...), custom_call_target="tpu_custom_call" | custom-call | tf_op jit(solution)/shard_map/norm/pallas_call | solution.py:43
  70.0 3.9 %project.1 = (f32[1,6,1024,128]{3,2,1,0:T(8,128)S(1)}, f32[16,768]{1,0:T(8,128)S(1)}, bf16[1024,768]{1,0:T(8,128)(2,1)S(1)}) custom-call(s32[5]{0:T(128)S(1)} %stack.23.refs_0_, bf16[1,1024,2048]{2,1,0:T(8,128)(2,1)S(1)} %get-tuple-element.58.refs_1_.refs_0_, bf16[16,2048]{1,0:T(8,128)(2,1)S(1)} %pad.4.refs_2_, bf16[8,128,384]{2,1,0:T(8,128)(2,1)} %all_to_all.15.refs_3_, ...), custom_call_target="tpu_custom_call" | custom-call | tf_op jit(solution)/shard_map/project/pallas_call | solution.py:43
  73.9 7.6 %blocks_forward.1 = (f32[1,6,1088,128]{3,2,1,0:T(8,128)S(1)}, f32[1,2,1088,128]{3,2,1,0:T(8,128)S(1)}, f32[1,2,336,128]{3,2,1,0:T(8,128)S(1)}, f32[1,1,256]{2,1,...) custom-call(s32[5]{0:T(128)S(1)} %stack.23.refs_0_, ...), custom_call_target="tpu_custom_call" | custom-call | tf_op jit(solution)/shard_map/blocks_forward/pallas_call | solution.py:43
  81.5 3.2 %collective-permute-start.10 = (f32[1,1,256]{2,1,0:T(1,128)S(1)}, f32[1,1,256]{2,1,0:T(1,128)S(1)}, u32[]{:S(2)}, u32[]{:S(2)}) collective-permute-start(f32[1,1,256]{2,1,0:T(1,128)S(1)} %get-tuple-element.67), channel_id=1, source_target_pairs={{0,8},{1,9},{2,10},{3,11},{4,12},{5,13},{6,14},{7,15},{8,0},{9,1},... | collective-permute-start | bytes 3080 | tf_op jit(solution)/shard_map/ppermute | solution.py:794
  86.2 2.2 %entry.1 = (f32[1,2,200,128]{3,2,1,0:T(8,128)S(1)}, f32[1,1,256]{2,1,0:T(1,128)S(1)}) custom-call(f32[1,6,1088,128]{3,2,1,0:T(8,128)S(1)} %get-tuple-element.62.refs_0_.refs_1_, f32[1,1088,128]{2,1,0:T(8,128)S(1)} %get-tuple-element.61.refs_6_.refs_1_.refs_2_, f32[1,2,1088,128]{3,2,1,0:T(8,128)S(1)} %get-tuple-element.63.refs_2_.refs_3_, ...), custom_call_target="tpu_custom_call" | custom-call | tf_op jit(solution)/shard_map/entry/pallas_call | solution.py:43
  88.4 3.0 %collective-permute-start.11 = (f32[1,1,256]{2,1,0:T(1,128)S(1)}, f32[1,1,256]{2,1,0:T(1,128)S(1)}, u32[]{:S(2)}, u32[]{:S(2)}) collective-permute-start(f32[1,1,256]{2,1,0:T(1,128)S(1)} %get-tuple-element.69), channel_id=1, source_target_pairs={{0,8},{1,9},{2,10},{3,11},{4,12},{5,13},{6,14},{7,15},{8,0},{9,1},... | collective-permute-start | bytes 3080 | tf_op jit(solution)/shard_map/ppermute | solution.py:794
  91.4 3.7 %lead_forward.1.refs_4_ = f32[1,2,816,128]{3,2,1,0:T(8,128)S(1)} custom-call(f32[1,6,1088,128]{3,2,1,0:T(8,128)S(1)} %get-tuple-element.62.refs_0_.refs_1_, f32[1,1088,128]{2,1,0:T(8,128)S(1)} %get-tuple-element.61.refs_6_.refs_1_.refs_2_, f32[1,256]{1,0:T(1,128)S(1)} %fusion.7.refs_7_.refs_2_.refs_5_.refs_8_, f32[1,1,256]{2,1,0:T(1,128)S(1)} %get-tuple-element.64.refs_3_, ...), custom_call_target="tpu_custom_call" | custom-call | tf_op jit(solution)/shard_map/lead_forward/pallas_call | solution.py:43
  95.2 5.1 %backward.1 = (bf16[1,1024,768]{2,1,0:T(8,128)(2,1)S(1)}, bf16[8,1,128,256]{3,2,1,0:T(8,128)(2,1)S(1)}, bf16[1,2,1024,128]{3,2,1,0:T(8,128)(2,1)S(1)}, f32[8,768...) custom-call(s32[5]{0:T(128)S(1)} %stack.23.refs_0_, ...), custom_call_target="tpu_custom_call" | custom-call | tf_op jit(solution)/shard_map/backward/pallas_call | solution.py:43
  100.3 2.2 %weight_back.2 = (f32[2,1024]{1,0:T(2,128)S(1)}, bf16[8,128,384]{2,1,0:T(8,128)(2,1)S(1)}, bf16[8,144,384]{2,1,0:T(8,128)(2,1)S(1)}) custom-call(bf16[1,1024,2048]{2,1,0:T(8,128)(2,1)S(1)} %get-tuple-element.58.refs_1_.refs_0_, bf16[1,1024,768]{2,1,0:T(8,128)(2,1)S(1)} %get-tuple-element.72.refs_1_.refs_3_, f32[8,768]{1,0:T(8,128)S(1)} %get-tuple-element.77.refs_2_.refs_1_, ...), custom_call_target="tpu_custom_call" | custom-call | tf_op jit(solution)/shard_map/weight_back/pallas_call | solution.py:43
  103.0 6.2 %norm_back.1 = (bf16[2,1,128,1152]{3,2,1,0:T(8,128)(2,1)S(1)}, bf16[2,1,128,1152]{3,2,1,0:T(8,128)(2,1)S(1)}, bf16[2,1,128,1152]{3,2,1,0:T(8,128)(2,1)S(1)}, bf1...) custom-call(s32[5]{0:T(128)S(1)} %stack.23.refs_0_, ...), custom_call_target="tpu_custom_call" | custom-call | tf_op jit(solution)/shard_map/norm_back/pallas_call | solution.py:43
  115.3 4.8 %collective-permute-done.21.refs_1_ = bf16[8,144,384]{2,1,0:T(8,128)(2,1)S(1)} collective-permute-done((bf16[8,144,384]{2,1,0:T(8,128)(2,1)S(1)}, bf16[8,144,384]{2,1,0:T(8,128)(2,1)S(1)}, u32[]{:S(2)}, u32[]{:S(2)}) %collective-permute-start.21) | collective-permute-done | bytes 884768 | tf_op jit(solution)/shard_map/ppermute | solution.py:800
  120.3 2.5 %collective-permute-start.22 = (bf16[8,128,384]{2,1,0:T(8,128)(2,1)S(1)}, bf16[8,128,384]{2,1,0:T(8,128)(2,1)S(1)}, u32[]{:S(2)}, u32[]{:S(2)}) collective-permute-start(bf16[8,128,384]{2,1,0:T(8,128)(2,1)S(1)} %added.6.refs_5_), channel_id=1, source_target_pairs={{0,8},{1,9},{2,10},{3,11},{4,12},{5,13},{6,14},{7,15},{8,0},{9,1},... | collective-permute-start | bytes 2359304 | tf_op jit(solution)/shard_map/ppermute | solution.py:794
  122.8 2.2 %weight_back.3 = (f32[2,1024]{1,0:T(2,128)S(1)}, bf16[8,128,384]{2,1,0:T(8,128)(2,1)S(1)}, bf16[8,64,384]{2,1,0:T(8,128)(2,1)S(1)}, bf16[8,64,384]{2,1,0:T(8,128)(2,1)S(1)}) custom-call(bf16[1,1024,2048]{2,1,0:T(8,128)(2,1)S(1)} %get-tuple-element.58.refs_1_.refs_0_, bf16[1,1024,768]{2,1,0:T(8,128)(2,1)S(1)} %get-tuple-element.72.refs_1_.refs_3_, ...), custom_call_target="tpu_custom_call" | custom-call | tf_op jit(solution)/shard_map/weight_back/pallas_call | solution.py:43
  128.3 4.3 %collective-permute-done.26.refs_1_ = f32[8,2048]{1,0:T(8,128)S(1)} collective-permute-done((f32[8,2048]{1,0:T(8,128)S(1)}, f32[8,2048]{1,0:T(8,128)S(1)}, u32[]{:S(2)}, u32[]{:S(2)}) %collective-permute-start.26) | collective-permute-done | bytes 65568 | tf_op jit(solution)/shard_map/ppermute | solution.py:797
  132.7 1.6 collective-permute-start.23
  134.8 5.0 %collective-permute-done.17.refs_3_ = bf16[2,1,128,1280]{3,2,1,0:T(8,128)(2,1)S(1)} collective-permute-done((bf16[2,1,128,1280]{3,2,1,0:T(8,128)(2,1)S(1)}, bf16[2,1,128,1280]{3,2,1,0:T(8,128)(2,1)S(1)}, u32[]{:S(2)}, u32[]{:S(2)}) %collective-permute-start.17) | collective-permute-done | bytes 655392 | tf_op jit(solution)/shard_map/ppermute | solution.py:797
  140.1 2.5 %collective-permute-start.18 = (bf16[1,1,128,1536]{3,2,1,0:T(8,128)(2,1)S(1)}, bf16[1,1,128,1536]{3,2,1,0:T(8,128)(2,1)S(1)}, u32[]{:S(2)}, u32[]{:S(2)}) collective-permute-start(bf16[1,1,128,1536]{3,2,1,0:T(8,128)(2,1)S(1)} %get-tuple-element.93), channel_id=1, source_target_pairs={{0,4},{1,5},{2,6},{3,7},{4,0},{5,1},{6,2},{7,3},{8,12},{9,13},{10,... | collective-permute-start | bytes 1179656 | tf_op jit(solution)/shard_map/ppermute | solution.py:797
  142.6 8.6 %collective-permute-done.27.refs_1_ = f32[8,2048]{1,0:T(8,128)S(1)} collective-permute-done((f32[8,2048]{1,0:T(8,128)S(1)}, f32[8,2048]{1,0:T(8,128)S(1)}, u32[]{:S(2)}, u32[]{:S(2)}) %collective-permute-start.27) | collective-permute-done | bytes 65568 | tf_op jit(solution)/shard_map/ppermute | solution.py:797
  152.4 6.1 %collective-permute-done.18.refs_3_.refs_4_ = bf16[1,1,128,1536]{3,2,1,0:T(8,128)(2,1)S(1)} collective-permute-done((bf16[1,1,128,1536]{3,2,1,0:T(8,128)(2,1)S(1)}, bf16[1,1,128,1536]{3,2,1,0:T(8,128)(2,1)S(1)}, u32[]{:S(2)}, u32[]{:S(2)}) %collective-permute-start.18) | collective-permute-done | bytes 393248 | tf_op jit(solution)/shard_map/ppermute | solution.py:797
  158.5 1.6 collective-permute-done.19.refs_4_.refs_5_
  161.3 3.9 %all-to-all-start.2 = ((bf16[8,128,384]{2,1,0:T(8,128)(2,1)}), bf16[8,128,384]{2,1,0:T(8,128)(2,1)S(1)}, u32[]{:S(2)}, u32[]{:S(2)}) async-start(bf16[8,128,384]{2,1,0:T(8,128)(2,1)} %merge.1), calls=%async_computation.2 | async-start | bytes 1572864 | tf_op jit(solution)/shard_map/all_to_all | solution.py:803
  165.2 1.5 collective-permute-start.28
  169.5 2.2 %collective-permute-start.29 = (f32[8,2048]{1,0:T(8,128)S(1)}, f32[8,2048]{1,0:T(8,128)S(1)}, u32[]{:S(2)}, u32[]{:S(2)}) collective-permute-start(f32[8,2048]{1,0:T(8,128)S(1)} %added.10.refs_0_), channel_id=1, source_target_pairs={{0,8},{1,9},{2,10},{3,11},{4,12},{5,13},{6,14},{7,15},{8,0},{9,1},... | collective-permute-start | bytes 196616 | tf_op jit(solution)/shard_map/ppermute | solution.py:794
  171.6 4.7 %collective-permute-done.20 = f32[1,128]{1,0:T(1,128)S(1)} collective-permute-done((f32[1,128]{1,0:T(1,128)S(1)}, f32[1,128]{1,0:T(1,128)S(1)}, u32[]{:S(2)}, u32[]{:S(2)}) %collective-permute-start.20) | collective-permute-done | bytes 544 | tf_op jit(solution)/shard_map/ppermute | solution.py:938
  176.9 1.7 finish.1
  (117 shorter events, 33.6 us)
Async XLA Ops:
  17.3 29.8 %collective-permute-start.1 = (bf16[8,128,384]{2,1,0:T(8,128)(2,1)}, bf16[8,128,384]{2,1,0:T(8,128)(2,1)S(1)}, u32[]{:S(2)}, u32[]{:S(2)}) collective-permute-start(bf16[8,128,384]{2,1,0:T(8,128)(2,1)} %all_to_all.15.refs_3_), channel_id=1, source_target_pairs={{0,16},{16,0},{1,17},{17,1},{2,18},{18,2},{3,19},{19,3},{4,20},{20... | collective-permute-start | bytes 2359304 | tf_op jit(solution)/shard_map/ppermute | solution.py:800
  19.2 27.0 %collective-permute-start.5 = (bf16[1,144,2048]{2,1,0:T(8,128)(2,1)S(1)}, bf16[1,144,2048]{2,1,0:T(8,128)(2,1)S(1)}, u32[]{:S(2)}, u32[]{:S(2)}) collective-permute-start(bf16[1,144,2048]{2,1,0:T(8,128)(2,1)S(1)} %stats.1.refs_0_), channel_id=1, source_target_pairs={{0,4},{1,5},{2,6},{3,7},{4,0},{5,1},{6,2},{7,3},{8,12},{9,13},{10,... | collective-permute-start | bytes 1769480 | tf_op jit(solution)/shard_map/ppermute | solution.py:797
  19.9 36.0 %collective-permute-start = (bf16[8,128,384]{2,1,0:T(8,128)(2,1)}, bf16[8,128,384]{2,1,0:T(8,128)(2,1)S(1)}, u32[]{:S(2)}, u32[]{:S(2)}) collective-permute-start(bf16[8,128,384]{2,1,0:T(8,128)(2,1)} %all_to_all.15.refs_3_), channel_id=1, source_target_pairs={{0,8},{1,9},{2,10},{3,11},{4,12},{5,13},{6,14},{7,15},{8,0},{9,1},... | collective-permute-start | bytes 2359304 | tf_op jit(solution)/shard_map/ppermute | solution.py:794
  22.5 34.3 %collective-permute-start.3 = (bf16[1,144,2048]{2,1,0:T(8,128)(2,1)S(1)}, bf16[1,144,2048]{2,1,0:T(8,128)(2,1)}, u32[]{:S(2)}, u32[]{:S(2)}) collective-permute-start(bf16[1,144,2048]{2,1,0:T(8,128)(2,1)S(1)} %stats.1.refs_0_), channel_id=1, source_target_pairs={{0,2},{1,3},{2,0},{3,1},{4,6},{5,7},{6,4},{7,5},{8,10},{9,11},{10,... | collective-permute-start | bytes 1769480 | tf_op jit(solution)/shard_map/ppermute | solution.py:797
  24.9 39.5 %all-to-all-start.1 = ((bf16[8,1,128,256]{3,2,1,0:T(8,128)(2,1)}), bf16[8,1,128,256]{3,2,1,0:T(8,128)(2,1)S(1)}, u32[]{:S(2)}, u32[]{:S(2)}) async-start(bf16[8,1,128,256]{3,2,1,0:T(8,128)(2,1)} %bitcast.41), calls=%async_computation.1 | async-start | bytes 1048576 | tf_op jit(solution)/shard_map/all_to_all | solution.py:803
  48.0 15.4 %collective-permute-start.7 = (bf16[1,144,2048]{2,1,0:T(8,128)(2,1)}, bf16[1,144,2048]{2,1,0:T(8,128)(2,1)}, u32[]{:S(2)}, u32[]{:S(2)}) collective-permute-start(bf16[1,144,2048]{2,1,0:T(8,128)(2,1)} %fence.8), channel_id=1, source_target_pairs={{0,2},{1,3},{2,0},{3,1},{4,6},{5,7},{6,4},{7,5},{8,10},{9,11},{10,... | collective-permute-start | bytes 1769480 | tf_op jit(solution)/shard_map/ppermute | solution.py:797
  55.9 18.0 %collective-permute-start.9 = (bf16[8,128,384]{2,1,0:T(8,128)(2,1)S(1)}, bf16[8,128,384]{2,1,0:T(8,128)(2,1)}, u32[]{:S(2)}, u32[]{:S(2)}) collective-permute-start(bf16[8,128,384]{2,1,0:T(8,128)(2,1)S(1)} %collective-permute-done.refs_1_.refs_9_), channel_id=1, source_target_pairs={{0,16},{16,0},{1,17},{17,1},{2,18},{18,2},{3,19},{19,3},{4,20},{20... | collective-permute-start | bytes 2359304 | tf_op jit(solution)/shard_map/ppermute | solution.py:800
  56.8 7.6 %collective-permute-start.6 = (bf16[1,144,2048]{2,1,0:T(8,128)(2,1)}, bf16[1,144,2048]{2,1,0:T(8,128)(2,1)}, u32[]{:S(2)}, u32[]{:S(2)}) collective-permute-start(bf16[1,144,2048]{2,1,0:T(8,128)(2,1)} %fence.7.refs_7_.refs_9_), channel_id=1, source_target_pairs={{0,1},{1,0},{2,3},{3,2},{4,5},{5,4},{6,7},{7,6},{8,9},{9,8},{10,11... | collective-permute-start | bytes 1769480 | tf_op jit(solution)/shard_map/ppermute | solution.py:797
  56.8 7.6 %collective-permute-start.4 = (bf16[1,144,2048]{2,1,0:T(8,128)(2,1)}, bf16[1,144,2048]{2,1,0:T(8,128)(2,1)S(1)}, u32[]{:S(2)}, u32[]{:S(2)}) collective-permute-start(bf16[1,144,2048]{2,1,0:T(8,128)(2,1)} %fence.6.refs_5_.refs_7_), channel_id=1, source_target_pairs={{0,1},{1,0},{2,3},{3,2},{4,5},{5,4},{6,7},{7,6},{8,9},{9,8},{10,11... | collective-permute-start | bytes 1769480 | tf_op jit(solution)/shard_map/ppermute | solution.py:797
  57.3 7.1 %collective-permute-start.2 = (bf16[1,144,2048]{2,1,0:T(8,128)(2,1)}, bf16[1,144,2048]{2,1,0:T(8,128)(2,1)}, u32[]{:S(2)}, u32[]{:S(2)}) collective-permute-start(bf16[1,144,2048]{2,1,0:T(8,128)(2,1)} %fence.5.refs_3_.refs_5_), channel_id=1, source_target_pairs={{0,1},{1,0},{2,3},{3,2},{4,5},{5,4},{6,7},{7,6},{8,9},{9,8},{10,11... | collective-permute-start | bytes 1769480 | tf_op jit(solution)/shard_map/ppermute | solution.py:797
  63.4 2.3 %collective-permute-start.8 = (bf16[1,144,2048]{2,1,0:T(8,128)(2,1)}, bf16[1,144,2048]{2,1,0:T(8,128)(2,1)}, u32[]{:S(2)}, u32[]{:S(2)}) collective-permute-start(bf16[1,144,2048]{2,1,0:T(8,128)(2,1)} %fence.9.refs_9_.refs_11_), channel_id=1, source_target_pairs={{0,1},{1,0},{2,3},{3,2},{4,5},{5,4},{6,7},{7,6},{8,9},{9,8},{10,11... | collective-permute-start | bytes 1769480 | tf_op jit(solution)/shard_map/ppermute | solution.py:797
  81.5 4.8 %collective-permute-start.10 = (f32[1,1,256]{2,1,0:T(1,128)S(1)}, f32[1,1,256]{2,1,0:T(1,128)S(1)}, u32[]{:S(2)}, u32[]{:S(2)}) collective-permute-start(f32[1,1,256]{2,1,0:T(1,128)S(1)} %get-tuple-element.67), channel_id=1, source_target_pairs={{0,8},{1,9},{2,10},{3,11},{4,12},{5,13},{6,14},{7,15},{8,0},{9,1},... | collective-permute-start | bytes 3080 | tf_op jit(solution)/shard_map/ppermute | solution.py:794
  88.4 6.7 %collective-permute-start.11 = (f32[1,1,256]{2,1,0:T(1,128)S(1)}, f32[1,1,256]{2,1,0:T(1,128)S(1)}, u32[]{:S(2)}, u32[]{:S(2)}) collective-permute-start(f32[1,1,256]{2,1,0:T(1,128)S(1)} %get-tuple-element.69), channel_id=1, source_target_pairs={{0,8},{1,9},{2,10},{3,11},{4,12},{5,13},{6,14},{7,15},{8,0},{9,1},... | collective-permute-start | bytes 3080 | tf_op jit(solution)/shard_map/ppermute | solution.py:794
  102.5 17.6 %collective-permute-start.21 = (bf16[8,144,384]{2,1,0:T(8,128)(2,1)S(1)}, bf16[8,144,384]{2,1,0:T(8,128)(2,1)S(1)}, u32[]{:S(2)}, u32[]{:S(2)}) collective-permute-start(bf16[8,144,384]{2,1,0:T(8,128)(2,1)S(1)} %get-tuple-element.99), channel_id=1, source_target_pairs={{0,16},{16,0},{1,17},{17,1},{2,18},{18,2},{3,19},{19,3},{4,20},{20... | collective-permute-start | bytes 2654216 | tf_op jit(solution)/shard_map/ppermute | solution.py:800
  109.2 2.1 %collective-permute-start.12 = (bf16[2,1,128,1152]{3,2,1,0:T(8,128)(2,1)S(1)}, bf16[2,1,128,1152]{3,2,1,0:T(8,128)(2,1)S(1)}, u32[]{:S(2)}, u32[]{:S(2)}) collective-permute-start(bf16[2,1,128,1152]{3,2,1,0:T(8,128)(2,1)S(1)} %get-tuple-element.83), channel_id=1, source_target_pairs={{0,1},{1,0},{2,3},{3,2},{4,5},{5,4},{6,7},{7,6},{8,9},{9,8},{10,11... | collective-permute-start | bytes 1769480 | tf_op jit(solution)/shard_map/ppermute | solution.py:797
  109.3 2.8 %collective-permute-start.13 = (bf16[2,1,128,1152]{3,2,1,0:T(8,128)(2,1)S(1)}, bf16[2,1,128,1152]{3,2,1,0:T(8,128)(2,1)S(1)}, u32[]{:S(2)}, u32[]{:S(2)}) collective-permute-start(bf16[2,1,128,1152]{3,2,1,0:T(8,128)(2,1)S(1)} %get-tuple-element.84), channel_id=1, source_target_pairs={{0,1},{1,0},{2,3},{3,2},{4,5},{5,4},{6,7},{7,6},{8,9},{9,8},{10,11... | collective-permute-start | bytes 1769480 | tf_op jit(solution)/shard_map/ppermute | solution.py:797
  109.8 3.2 %collective-permute-start.14 = (bf16[2,1,128,1152]{3,2,1,0:T(8,128)(2,1)S(1)}, bf16[2,1,128,1152]{3,2,1,0:T(8,128)(2,1)S(1)}, u32[]{:S(2)}, u32[]{:S(2)}) collective-permute-start(bf16[2,1,128,1152]{3,2,1,0:T(8,128)(2,1)S(1)} %get-tuple-element.85), channel_id=1, source_target_pairs={{0,1},{1,0},{2,3},{3,2},{4,5},{5,4},{6,7},{7,6},{8,9},{9,8},{10,11... | collective-permute-start | bytes 1769480 | tf_op jit(solution)/shard_map/ppermute | solution.py:797
  109.9 3.9 %collective-permute-start.15 = (bf16[2,1,128,1152]{3,2,1,0:T(8,128)(2,1)S(1)}, bf16[2,1,128,1152]{3,2,1,0:T(8,128)(2,1)S(1)}, u32[]{:S(2)}, u32[]{:S(2)}) collective-permute-start(bf16[2,1,128,1152]{3,2,1,0:T(8,128)(2,1)S(1)} %get-tuple-element.86), channel_id=1, source_target_pairs={{0,1},{1,0},{2,3},{3,2},{4,5},{5,4},{6,7},{7,6},{8,9},{9,8},{10,11... | collective-permute-start | bytes 1769480 | tf_op jit(solution)/shard_map/ppermute | solution.py:797
  114.3 19.9 %collective-permute-start.16 = (bf16[2,1,128,1280]{3,2,1,0:T(8,128)(2,1)S(1)}, bf16[2,1,128,1280]{3,2,1,0:T(8,128)(2,1)S(1)}, u32[]{:S(2)}, u32[]{:S(2)}) collective-permute-start(bf16[2,1,128,1280]{3,2,1,0:T(8,128)(2,1)S(1)} %get-tuple-element.89), channel_id=1, source_target_pairs={{0,2},{1,3},{2,0},{3,1},{4,6},{5,7},{6,4},{7,5},{8,10},{9,11},{10,... | collective-permute-start | bytes 1966088 | tf_op jit(solution)/shard_map/ppermute | solution.py:797
  115.3 24.5 %collective-permute-start.17 = (bf16[2,1,128,1280]{3,2,1,0:T(8,128)(2,1)S(1)}, bf16[2,1,128,1280]{3,2,1,0:T(8,128)(2,1)S(1)}, u32[]{:S(2)}, u32[]{:S(2)}) collective-permute-start(bf16[2,1,128,1280]{3,2,1,0:T(8,128)(2,1)S(1)} %get-tuple-element.90), channel_id=1, source_target_pairs={{0,4},{1,5},{2,6},{3,7},{4,0},{5,1},{6,2},{7,3},{8,12},{9,13},{10,... | collective-permute-start | bytes 1966088 | tf_op jit(solution)/shard_map/ppermute | solution.py:797
  120.3 39.8 %collective-permute-start.22 = (bf16[8,128,384]{2,1,0:T(8,128)(2,1)S(1)}, bf16[8,128,384]{2,1,0:T(8,128)(2,1)S(1)}, u32[]{:S(2)}, u32[]{:S(2)}) collective-permute-start(bf16[8,128,384]{2,1,0:T(8,128)(2,1)S(1)} %added.6.refs_5_), channel_id=1, source_target_pairs={{0,8},{1,9},{2,10},{3,11},{4,12},{5,13},{6,14},{7,15},{8,0},{9,1},... | collective-permute-start | bytes 2359304 | tf_op jit(solution)/shard_map/ppermute | solution.py:794
  125.5 1.3 collective-permute-start.25
  126.9 5.7 %collective-permute-start.26 = (f32[8,2048]{1,0:T(8,128)S(1)}, f32[8,2048]{1,0:T(8,128)S(1)}, u32[]{:S(2)}, u32[]{:S(2)}) collective-permute-start(f32[8,2048]{1,0:T(8,128)S(1)} %added.7.refs_0_), channel_id=1, source_target_pairs={{0,2},{1,3},{2,0},{3,1},{4,6},{5,7},{6,4},{7,5},{8,10},{9,11},{10,... | collective-permute-start | bytes 196616 | tf_op jit(solution)/shard_map/ppermute | solution.py:797
  132.6 18.6 %collective-permute-start.27 = (f32[8,2048]{1,0:T(8,128)S(1)}, f32[8,2048]{1,0:T(8,128)S(1)}, u32[]{:S(2)}, u32[]{:S(2)}) collective-permute-start(f32[8,2048]{1,0:T(8,128)S(1)} %added.8.refs_0_), channel_id=1, source_target_pairs={{0,4},{1,5},{2,6},{3,7},{4,0},{5,1},{6,2},{7,3},{8,12},{9,13},{10,... | collective-permute-start | bytes 196616 | tf_op jit(solution)/shard_map/ppermute | solution.py:797
  132.7 19.7 %collective-permute-start.23 = (bf16[8,64,384]{2,1,0:T(8,128)(2,1)S(1)}, bf16[8,64,384]{2,1,0:T(8,128)(2,1)S(1)}, u32[]{:S(2)}, u32[]{:S(2)}) collective-permute-start(bf16[8,64,384]{2,1,0:T(8,128)(2,1)S(1)} %get-tuple-element.101), channel_id=1, source_target_pairs={{0,16},{16,0},{1,17},{17,1},{2,18},{18,2},{3,19},{19,3},{4,20},{20... | collective-permute-start | bytes 1179656 | tf_op jit(solution)/shard_map/ppermute | solution.py:800
  134.3 18.1 %collective-permute-start.24 = (bf16[8,64,384]{2,1,0:T(8,128)(2,1)S(1)}, bf16[8,64,384]{2,1,0:T(8,128)(2,1)S(1)}, u32[]{:S(2)}, u32[]{:S(2)}) collective-permute-start(bf16[8,64,384]{2,1,0:T(8,128)(2,1)S(1)} %get-tuple-element.102), channel_id=1, source_target_pairs={{0,16},{16,0},{1,17},{17,1},{2,18},{18,2},{3,19},{19,3},{4,20},{20... | collective-permute-start | bytes 1179656 | tf_op jit(solution)/shard_map/ppermute | solution.py:800
  140.1 18.5 %collective-permute-start.18 = (bf16[1,1,128,1536]{3,2,1,0:T(8,128)(2,1)S(1)}, bf16[1,1,128,1536]{3,2,1,0:T(8,128)(2,1)S(1)}, u32[]{:S(2)}, u32[]{:S(2)}) collective-permute-start(bf16[1,1,128,1536]{3,2,1,0:T(8,128)(2,1)S(1)} %get-tuple-element.93), channel_id=1, source_target_pairs={{0,4},{1,5},{2,6},{3,7},{4,0},{5,1},{6,2},{7,3},{8,12},{9,13},{10,... | collective-permute-start | bytes 1179656 | tf_op jit(solution)/shard_map/ppermute | solution.py:797
  151.2 8.9 %collective-permute-start.19 = (bf16[1,1,128,1536]{3,2,1,0:T(8,128)(2,1)S(1)}, bf16[1,1,128,1536]{3,2,1,0:T(8,128)(2,1)S(1)}, u32[]{:S(2)}, u32[]{:S(2)}) collective-permute-start(bf16[1,1,128,1536]{3,2,1,0:T(8,128)(2,1)S(1)} %get-tuple-element.94), channel_id=1, source_target_pairs={{0,2},{1,3},{2,0},{3,1},{4,6},{5,7},{6,4},{7,5},{8,10},{9,11},{10,... | collective-permute-start | bytes 1179656 | tf_op jit(solution)/shard_map/ppermute | solution.py:797
  161.3 18.9 %all-to-all-start.2 = ((bf16[8,128,384]{2,1,0:T(8,128)(2,1)}), bf16[8,128,384]{2,1,0:T(8,128)(2,1)S(1)}, u32[]{:S(2)}, u32[]{:S(2)}) async-start(bf16[8,128,384]{2,1,0:T(8,128)(2,1)} %merge.1), calls=%async_computation.2 | async-start | bytes 1572864 | tf_op jit(solution)/shard_map/all_to_all | solution.py:803
  165.2 4.3 %collective-permute-start.28 = (f32[8,2048]{1,0:T(8,128)S(1)}, f32[8,2048]{1,0:T(8,128)S(1)}, u32[]{:S(2)}, u32[]{:S(2)}) collective-permute-start(f32[8,2048]{1,0:T(8,128)S(1)} %added.9.refs_6_.refs_0_), channel_id=1, source_target_pairs={{0,16},{16,0},{1,17},{17,1},{2,18},{18,2},{3,19},{19,3},{4,20},{20... | collective-permute-start | bytes 196616 | tf_op jit(solution)/shard_map/ppermute | solution.py:800
  166.7 9.6 %collective-permute-start.20 = (f32[1,128]{1,0:T(1,128)S(1)}, f32[1,128]{1,0:T(1,128)S(1)}, u32[]{:S(2)}, u32[]{:S(2)}) collective-permute-start(f32[1,128]{1,0:T(1,128)S(1)} %slice.48), channel_id=1, source_target_pairs={{8,0},{9,1},{10,2},{11,3},{12,4},{13,5},{14,6},{15,7},{24,16},{25,... | collective-permute-start | bytes 1544 | tf_op jit(solution)/shard_map/ppermute | solution.py:938
  169.5 9.1 %collective-permute-start.29 = (f32[8,2048]{1,0:T(8,128)S(1)}, f32[8,2048]{1,0:T(8,128)S(1)}, u32[]{:S(2)}, u32[]{:S(2)}) collective-permute-start(f32[8,2048]{1,0:T(8,128)S(1)} %added.10.refs_0_), channel_id=1, source_target_pairs={{0,8},{1,9},{2,10},{3,11},{4,12},{5,13},{6,14},{7,15},{8,0},{9,1},... | collective-permute-start | bytes 196616 | tf_op jit(solution)/shard_map/ppermute | solution.py:794
  (17 other events, 221.2 us)
